TPU v7x, 256 devices: a whole 4x4x8 slice. The times are simulated.
256 devices in a mesh: sky: 16 (over x, y), epoch: 16 (over z, core).
Axes of the slice: x: 4, y: 4, z: 8, core: 2. Of those that a mesh axis runs over, the one named last changes fastest.
Arguments:
- params: bfloat16 [2048, 64], P('sky'), may hold values from -6 to 6
- basis: bfloat16 [64, 4096], replicated, may hold values from -0.75 to 0.75
- psf_taps: float32 [16, 2, 51], P('epoch'), may hold values from 0.02 to 1
- send_index: int32 [16, 16, 16], P('sky'), may hold values from 0 to 127
- tile_count: int32 [16, 16], P('sky'), may hold values from 0 to 16, as said below
- stamp_row: int32 [16, 16, 16], P('sky'), may hold values from 0 to 256
- stamp_col: int32 [16, 16, 16], P('sky'), may hold values from 0 to 448
- observed: float32 [16, 4096, 512], P('epoch', 'sky'), may hold values from 0 to 6
- background: float32 [16, 4096, 512], P('epoch', 'sky'), may hold values from 0.5 to 2
Outputs:
- param_grad: float32 [2048, 64], P('sky')
- residual: float32 [16, 4096, 512], P('epoch', 'sky')
Inputs may be any that keep to these rules, and one draw needn't show every extreme that they name: `send_index`: slots with k >= tile_count[t, o] are dead and may name any row; they still lie within range. `tile_count`: some tiles are crowded and receive nearly 16 slots from every owner; in every draw at least one tile receives exactly 16 from owner 0. `stamp_row`: A stamp lies inside its tile's canvas.
All inputs are finite; a program needn't handle non-finite values.
Results may differ from a plain program's by a relative error of at most 0.0003.
Values may be sent and summed in bfloat16 or wider, within the bound.
No kernel may reach another device: no remote copies, remote signals or barrier semaphores. Data moves between devices by JAX's collectives and lax.ppermute only.
A program may use at most 64 MiB of HBM per device.

v0:
```python
import math

import jax
import jax.numpy as jnp
from jax import lax
from jax.sharding import PartitionSpec as P


def extended_2(cells, sides, width):
    for axis, dim in sides:
        count = lax.axis_size(axis)
        ends = count - 1
        head = lax.slice_in_dim(cells, 0, width, axis=dim)
        tail = lax.slice_in_dim(cells, cells.shape[dim] - width, cells.shape[dim], axis=dim)
        cells = jnp.concatenate(
            [
                lax.ppermute(tail, axis, [(i, (i + 1) % count) for i in range(ends)]),
                cells,
                lax.ppermute(head, axis, [((i + 1) % count, i) for i in range(ends)]),
            ],
            axis=dim,
        )
    return cells


def toeplitz(taps, width):
    half = (taps.shape[0] - 1) // 2
    rows_at = jnp.arange(width, dtype=jnp.int32)[:, None]
    cols_at = jnp.arange(width, dtype=jnp.int32)[None, :]
    where_at = rows_at - cols_at + half
    inside = (where_at >= 0) & (where_at < taps.shape[0])
    return jnp.where(
        inside, taps[jnp.clip(where_at, 0, taps.shape[0] - 1)], jnp.zeros((), taps.dtype)
    )


def on_device(
    params, basis, psf_taps, send_index, tile_count, stamp_row, stamp_col, observed, background
):
    highest = lax.Precision.HIGHEST
    stamp_size = math.isqrt(basis.shape[1])
    margin = stamp_size // 2
    n_sky = send_index.shape[1]
    capacity = send_index.shape[2]
    slots = n_sky * capacity
    tile_rows = observed.shape[1]
    width = observed.shape[2]
    canvas_rows = tile_rows + 2 * margin
    taps = psf_taps[0] / jnp.sum(psf_taps[0], axis=-1, keepdims=True)
    row_kernel = toeplitz(taps[0], stamp_size)
    col_kernel = toeplitz(taps[1], stamp_size)
    basis_wide = basis.astype(jnp.float32).T
    live = jnp.arange(capacity, dtype=jnp.int32)[None, :] < tile_count[0][:, None]
    live_flat = live.reshape(slots, 1)
    outgoing = params[send_index[0]]
    intrinsic = jnp.dot(outgoing.reshape(slots, -1), basis, preferred_element_type=jnp.float32)
    intrinsic = intrinsic.reshape(-1, stamp_size, stamp_size)
    rendered = jnp.einsum("ab,nbc,dc->nad", row_kernel, intrinsic, col_kernel, precision=highest)
    made = (
        rendered.reshape(-1, stamp_size * stamp_size)
        .astype(jnp.bfloat16)
        .reshape(n_sky, capacity, -1)
    )
    stamps = lax.all_to_all(made, "sky", split_axis=0, concat_axis=0, tiled=True).reshape(slots, -1)
    stamps = jnp.where(live_flat, stamps, jnp.zeros_like(stamps))
    block_size = math.gcd(slots, 32)
    blocks = slots // block_size
    stamp_blocks = stamps.reshape(blocks, block_size, stamp_size, stamp_size)
    row_blocks = stamp_row[0].reshape(blocks, block_size)
    col_blocks = stamp_col[0].reshape(blocks, block_size)
    stamp_span = jnp.arange(stamp_size, dtype=jnp.int32)
    lane_index = jnp.arange(width, dtype=jnp.int32)
    level_index = jnp.arange(canvas_rows, dtype=jnp.int32)

    def tables(rows_b, cols_b):
        col_one = (
            cols_b[:, None, None] + stamp_span[None, :, None] == lane_index[None, None, :]
        ).astype(jnp.bfloat16)
        covered = (rows_b[:, None] + stamp_span[None, :]).reshape(1, -1)
        row_one = (level_index[:, None] == covered).astype(jnp.bfloat16)
        return (row_one, col_one)

    def place(canvas, block):
        stamps_b, rows_b, cols_b = block
        row_one, col_one = tables(rows_b, cols_b)
        moved = jnp.einsum(
            "nab,nbj->naj", stamps_b, col_one, preferred_element_type=jnp.float32
        ).astype(jnp.bfloat16)
        return (
            canvas + jnp.dot(row_one, moved.reshape(-1, width), preferred_element_type=jnp.float32),
            None,
        )

    start = jnp.zeros((canvas_rows, width), jnp.float32)
    canvas, unused = lax.scan(place, start, (stamp_blocks, row_blocks, col_blocks))
    margins = jnp.concatenate([canvas[:margin], canvas[margin + tile_rows :]], axis=0)
    spilled = extended_2(margins, (("sky", 0),), margin)
    image = canvas[margin : margin + tile_rows]
    image = (
        image.at[:margin].add(spilled[:margin]).at[tile_rows - margin :].add(spilled[3 * margin :])
    )
    model = background[0] + jax.nn.softplus(image)
    residual = (observed[0] / model - 1.0) * jax.nn.sigmoid(image)
    extended = extended_2(residual.astype(jnp.bfloat16), (("sky", 0),), margin)

    def pick(block):
        rows_b, cols_b = block
        row_one, col_one = tables(rows_b, cols_b)
        lifted = lax.dot_general(
            row_one, extended, (((0,), (0,)), ((), ())), preferred_element_type=jnp.float32
        )
        lifted = lifted.astype(jnp.bfloat16).reshape(block_size, stamp_size, width)
        return jnp.einsum(
            "naj,nbj->nab", lifted, col_one, preferred_element_type=jnp.float32
        ).astype(jnp.bfloat16)

    patches = lax.map(pick, (row_blocks, col_blocks)).reshape(slots, -1)
    patches = jnp.where(live_flat, patches, jnp.zeros_like(patches))
    owned_rows = send_index[0].reshape(-1)
    source_index = jnp.arange(params.shape[0], dtype=jnp.int32)
    scatter_table = (source_index[:, None] == owned_rows[None, :]).astype(jnp.float32)
    returned = lax.all_to_all(
        patches.reshape(n_sky, capacity, -1), "sky", split_axis=0, concat_axis=0, tiled=True
    )
    window = returned.reshape(slots, -1).astype(jnp.float32).reshape(-1, stamp_size, stamp_size)
    pulled = jnp.einsum("ba,nbc,cd->nad", row_kernel, window, col_kernel, precision=highest)
    flat = pulled.reshape(-1, stamp_size * stamp_size)
    slot_grad = jnp.dot(flat, basis_wide, precision=highest).reshape(n_sky, capacity, -1)
    summed = lax.psum(slot_grad, "epoch")
    param_grad = jnp.dot(scatter_table, summed.reshape(slots, -1), precision=highest)
    return (param_grad, residual[None])


def solution(mesh):
    in_specs = (
        P("sky", None),
        P(),
        P("epoch", None, None),
        P("sky", None, None),
        P("sky", None),
        P("sky", None, None),
        P("sky", None, None),
        P("epoch", "sky", None),
        P("epoch", "sky", None),
    )
    out_specs = (P("sky", None), P("epoch", "sky", None))
    return jax.shard_map(
        on_device, mesh=mesh, in_specs=in_specs, out_specs=out_specs, check_vma=False
    )
```

profile of v0, /device:TPU:1, one launch (start us, length us, event | category | flops | bytes accessed | tf_op | source)
XLA Modules:
  0.0 402.4 jit_solution(16712460735421602686)
XLA Ops:
  8.8 24.7 %gather_fusion.1 = f32[4096]{0:T(1024)S(1)} fusion(f32[51]{0:T(128)S(1)} %get-tuple-element.227, s32[4096]{0:T(1024)S(1)} %broadcast_clamp_fusion), kind=kCustom, calls=%fused_computation.1 | custom fusion | bytes 49152 | tf_op jit(solution)/shard_map/gather | solution.py:33
  34.4 24.7 %gather_fusion.2 = f32[4096]{0:T(1024)S(1)} fusion(f32[51]{0:T(128)S(1)} %get-tuple-element.226, s32[4096]{0:T(1024)S(1)} %broadcast_clamp_fusion), kind=kCustom, calls=%fused_computation.2 | custom fusion | bytes 49152 | tf_op jit(solution)/shard_map/gather | solution.py:33
  59.2 0.9 gather_fusion
  60.0 0.9 fusion.38
  60.9 4.3 %fusion.54 = f32[256,64,64]{0,2,1:T(8,128)S(1)} fusion(f32[256,64,64]{0,1,2:T(8,128)S(1)} %fusion.38, f32[64,64]{1,0:T(8,128)S(1)} %reshape.307), kind=kOutput, calls=%fused_computation.70 | convolution fusion | flops 805330944 | bytes 8404992 | tf_op jit(solution)/shard_map/ab,nbc,dc->nad/dot_general | solution.py:58
  65.2 5.8 %fusion.35 = bf16[256,64,64]{0,2,1:T(8,128)(2,1)S(1)} fusion(f32[256,64,64]{0,2,1:T(8,128)S(1)} %fusion.54, f32[64,64]{1,0:T(8,128)S(1)} %reshape.315), kind=kOutput, calls=%fused_computation.47 | convolution fusion | flops 806379520 | bytes 6307840 | tf_op jit(solution)/shard_map/ab,nbc,dc->nad/dot_general | solution.py:58
  71.0 6.7 %copy.35 = bf16[256,64,64]{2,1,0:T(8,128)(2,1)} copy(bf16[256,64,64]{0,2,1:T(8,128)(2,1)S(1)} %fusion.35) | data formatting | bytes 4194304 | tf_op jit(solution)/shard_map/convert_element_type | solution.py:61
  77.6 6.7 %convert_element_type.27 = bf16[16,16,4096]{2,1,0:T(8,128)(2,1)} reshape(bf16[256,64,64]{2,1,0:T(8,128)(2,1)} %copy.35) | data formatting | bytes 4194304 | tf_op jit(solution)/shard_map/convert_element_type | solution.py:61
  84.3 7.6 %all-to-all-start = ((bf16[16,16,4096]{2,1,0:T(8,128)(2,1)}), bf16[16,16,4096]{2,1,0:T(8,128)(2,1)S(1)}, u32[]{:S(2)}, u32[]{:S(2)}) async-start(bf16[16,16,4096]{2,1,0:T(8,128)(2,1)} %convert_element_type.27), calls=%async_computation | async-start | bytes 4194304 | tf_op jit(solution)/shard_map/all_to_all | solution.py:64
  93.8 26.1 %all-to-all-done = bf16[16,16,4096]{2,1,0:T(8,128)(2,1)S(1)} async-done(((bf16[16,16,4096]{2,1,0:T(8,128)(2,1)}), bf16[16,16,4096]{2,1,0:T(8,128)(2,1)S(1)}, u32[]{:S(2)}, u32[]{:S(2)}) %all-to-all-start) | async-done | bytes 2097184 | tf_op jit(solution)/shard_map/all_to_all | solution.py:64
  119.9 5.5 %reshape.292 = bf16[8,32,64,64]{3,2,1,0:T(8,128)(2,1)} reshape(bf16[16,16,4096]{2,1,0:T(8,128)(2,1)S(1)} %all-to-all-done) | data formatting | bytes 4194304 | tf_op jit(solution)/shard_map/reshape | solution.py:64
  125.4 3.8 broadcast_select_fusion
  129.2 26.9 %while.29 = (s32[]{:T(128)}, f32[320,512]{1,0:T(8,128)S(1)}, s32[8,32]{1,0:T(8,128)S(1)}, bf16[8,32,64,64]{3,2,1,0:T(8,128)(2,1)}, s32[8,32]{1,0:T(8,128)S(1)}) while((s32[]{:T(128)}, f32[320,512]{1,0:T(8,128)S(1)}, s32[8,32]{1,0:T(8,128)S(1)}, bf16[8,32,64,64]{3,2,1,0:T(8,128)(2,1)}, ...), condition=%wide.region_2.3_spmd.clone.clone.clone, body=%wide.region_1.2_spmd.clone.clone.sunk.clone | while | flops 808390656 | bytes 6079819 | solution.py:95
  129.3 2.2 fusion.123
  131.6 0.9 fusion.124
  132.6 2.2 fusion.123
  135.0 0.9 fusion.124
  136.0 2.2 fusion.123
  138.4 0.9 fusion.124
  139.4 2.2 fusion.123
  141.7 0.9 fusion.124
  142.7 2.2 fusion.123
  145.1 0.9 fusion.124
  146.1 2.2 fusion.123
  148.4 0.9 fusion.124
  149.4 2.2 fusion.123
  151.8 0.9 fusion.124
  152.8 2.2 fusion.123
  155.2 0.9 fusion.124
  156.1 2.2 collective-permute-start
  158.3 1.3 collective-permute-start.1
  159.7 3.7 collective-permute-done.1
  163.4 2.4 fusion.87
  165.8 1.9 collective-permute-start.2
  167.7 1.3 collective-permute-start.3
  169.1 3.3 collective-permute-done.3
  172.4 27.7 %while.28 = (s32[]{:T(128)}, bf16[8,32,64,64]{3,2,1,0:T(8,128)(2,1)}, s32[8,32]{1,0:T(8,128)S(1)}, bf16[320,512]{1,0:T(8,128)(2,1)S(1)}, s32[8,32]{1,0:T(8,128)S(1)}) while((s32[]{:T(128)}, bf16[8,32,64,64]{3,2,1,0:T(8,128)(2,1)}, s32[8,32]{1,0:T(8,128)S(1)}, bf16[320,512]{1,0:T(8,128)(2,1)S(1)}, ...), condition=%wide.region_4.5_spmd.clone.clone.clone, body=%wide.region_3.4_spmd.clone.clone.sunk.clone | while | flops 808194048 | bytes 5096769 | solution.py:117
  172.6 1.3 convolution_convert_fusion.3
  174.0 1.9 fusion.119
  176.1 1.3 convolution_convert_fusion.3
  177.4 1.9 fusion.119
  179.5 1.3 convolution_convert_fusion.3
  180.9 1.9 fusion.119
  183.0 1.3 convolution_convert_fusion.3
  184.4 1.9 fusion.119
  186.4 1.3 convolution_convert_fusion.3
  187.8 1.9 fusion.119
  189.9 1.3 convolution_convert_fusion.3
  191.3 1.9 fusion.119
  193.4 1.3 convolution_convert_fusion.3
  194.8 1.9 fusion.119
  196.8 1.3 convolution_convert_fusion.3
  198.2 1.9 fusion.119
  200.1 5.7 %reshape.293 = bf16[16,16,4096]{2,1,0:T(8,128)(2,1)S(1)} reshape(bf16[8,32,64,64]{3,2,1,0:T(8,128)(2,1)} %get-tuple-element.117) | data formatting | bytes 4194304 | tf_op jit(solution)/shard_map/reshape | solution.py:117
  206.0 30.3 %all_to_all.10 = bf16[16,16,4096]{2,1,0:T(8,128)(2,1)S(1)} all-to-all(bf16[16,16,4096]{2,1,0:T(8,128)(2,1)S(1)} %broadcast_select_fusion.1), channel_id=1, replica_groups=mesh['sky'=16,'epoch'=16] {'sky'}, dimensions={0} | all-to-all | bytes 4194304 | tf_op jit(solution)/shard_map/all_to_all | solution.py:122
  236.3 5.5 %reshape.294 = bf16[256,64,64]{2,1,0:T(8,128)(2,1)} reshape(bf16[16,16,4096]{2,1,0:T(8,128)(2,1)S(1)} %all_to_all.10) | data formatting | bytes 4194304 | tf_op jit(solution)/shard_map/reshape | solution.py:125
  241.8 7.0 %copy.36 = bf16[256,64,64]{0,1,2:T(8,128)(2,1)S(1)} copy(bf16[256,64,64]{2,1,0:T(8,128)(2,1)} %reshape.294) | data formatting | bytes 4194304 | tf_op jit(solution)/shard_map/reshape | solution.py:125
  248.8 2.0 fusion.52
  250.8 7.1 %fusion.31 = f32[256,64,64]{0,2,1:T(8,128)} fusion(f32[256,64,64]{0,2,1:T(8,128)S(1)} %fusion.52, f32[64,64]{1,0:T(8,128)S(1)} %reshape.315), kind=kOutput, calls=%fused_computation.41 | convolution fusion | flops 805330944 | bytes 8404992 | tf_op jit(solution)/shard_map/ba,nbc,cd->nad/dot_general | solution.py:126
  257.9 9.2 %copy.40 = f32[256,64,64]{2,1,0:T(8,128)} copy(f32[256,64,64]{0,2,1:T(8,128)} %fusion.31) | data formatting | bytes 8388608 | tf_op jit(solution)/shard_map/ba,nbc,cd->nad/dot_general | solution.py:126
  267.1 7.9 %dot_general.46 = f32[16,16,4096]{2,1,0:T(8,128)} reshape(f32[256,64,64]{2,1,0:T(8,128)} %copy.40) | data formatting | bytes 8388608 | tf_op jit(solution)/shard_map/dot_general | solution.py:128
  275.0 4.8 %fusion.44 = f32[16,16,64]{2,1,0:T(8,128)} fusion(f32[16,16,4096]{2,1,0:T(8,128)} %dot_general.46, bf16[64,4096]{1,0:T(8,128)(2,1)S(1)} %copy-done), kind=kOutput, calls=%fused_computation.55 | convolution fusion | flops 805306368 | bytes 4784128 | tf_op jit(solution)/shard_map/dot_general | solution.py:128
  279.9 113.9 %all-reduce.2.cloned.1.call-done = f32[256,64]{1,0:T(8,128)} async-done(((f32[256,64]{1,0:T(8,128)}), f32[256,64]{1,0:T(8,128)}) %all-reduce.2.cloned.1.call-update) | async-done | bytes 65552 | tf_op jit(solution)/shard_map/psum | solution.py:129
  393.8 1.8 fusion.46
  (114 shorter events, 8.5 us)
Async XLA Ops:
  8.8 24.8 %copy-start = (bf16[64,4096]{1,0:T(8,128)(2,1)S(1)}, bf16[64,4096]{1,0:T(8,128)(2,1)}, u32[]{:S(2)}) copy-start(bf16[64,4096]{1,0:T(8,128)(2,1)} %param.18) | copy-start | bytes 1572868
  8.8 25.3 %copy-start.2 = (bf16[128,64]{0,1:T(8,128)(2,1)S(1)}, bf16[128,64]{0,1:T(8,128)(2,1)}, u32[]{:S(2)}) copy-start(bf16[128,64]{0,1:T(8,128)(2,1)} %param.17) | copy-start | bytes 49156
  8.8 25.4 %copy-start.1 = (s32[1,16,16]{2,1,0:T(8,128)S(1)}, s32[1,16,16]{2,1,0:T(8,128)}, u32[]{:S(2)}) copy-start(s32[1,16,16]{2,1,0:T(8,128)} %param.20) | copy-start | bytes 3076
  77.6 15.1 %copy-start.5 = (s32[1,16]{1,0:T(1,128)S(1)}, s32[1,16]{1,0:T(1,128)}, u32[]{:S(2)}) copy-start(s32[1,16]{1,0:T(1,128)} %param.21) | copy-start | bytes 196
  77.6 16.0 %copy-start.3 = (s32[1,16,16]{2,1,0:T(8,128)S(1)}, s32[1,16,16]{2,1,0:T(8,128)}, u32[]{:S(2)}) copy-start(s32[1,16,16]{2,1,0:T(8,128)} %param.22) | copy-start | bytes 3076
  77.6 16.1 %copy-start.4 = (s32[1,16,16]{2,1,0:T(8,128)S(1)}, s32[1,16,16]{2,1,0:T(8,128)}, u32[]{:S(2)}) copy-start(s32[1,16,16]{2,1,0:T(8,128)} %param.23) | copy-start | bytes 3076
  84.3 35.6 %all-to-all-start = ((bf16[16,16,4096]{2,1,0:T(8,128)(2,1)}), bf16[16,16,4096]{2,1,0:T(8,128)(2,1)S(1)}, u32[]{:S(2)}, u32[]{:S(2)}) async-start(bf16[16,16,4096]{2,1,0:T(8,128)(2,1)} %convert_element_type.27), calls=%async_computation | async-start | bytes 4194304 | tf_op jit(solution)/shard_map/all_to_all | solution.py:64
  91.9 301.9 %all-reduce.2.cloned.1.call-start = ((), (), s32[]{:S(2)}) async-start(), calls=%async_computation.2 | async-start | bytes 262144 | tf_op jit(solution)/shard_map/psum | solution.py:129
  156.1 3.6 collective-permute-start
  158.3 5.0 %collective-permute-start.1 = (f32[32,512]{1,0:T(8,128)S(1)}, f32[32,512]{1,0:T(8,128)S(1)}, u32[]{:S(2)}, u32[]{:S(2)}) collective-permute-start(f32[32,512]{1,0:T(8,128)S(1)} %get-tuple-element.222), channel_id=1, source_target_pairs={{16,0},{32,16},{48,32},{64,48},{80,64},{96,80},{112,96},{128,112},... | collective-permute-start | bytes 196616 | tf_op jit(solution)/shard_map/ppermute | solution.py:19
  165.8 3.3 collective-permute-start.2
  167.7 4.7 %collective-permute-start.3 = (bf16[32,512]{1,0:T(8,128)(2,1)S(1)}, bf16[32,512]{1,0:T(8,128)(2,1)S(1)}, u32[]{:S(2)}, u32[]{:S(2)}) collective-permute-start(bf16[32,512]{1,0:T(8,128)(2,1)S(1)} %get-tuple-element.225), channel_id=1, source_target_pairs={{16,0},{32,16},{48,32},{64,48},{80,64},{96,80},{112,96},{128,112},... | collective-permute-start | bytes 98312 | tf_op jit(solution)/shard_map/ppermute | solution.py:19
Sparse Core Ops, SparseCore 0:
  280.0 113.7 all-reduce.1
where the time goes:
time: 404 us; the launch traced here: 402 us
  waiting for transfers between devices  147 us (36%)
  local copies, waits for them, and re-layouts  108 us (27%)
  matrix products  77.2 us (19%)
  blocking collectives  30.3 us (8%)
  starting transfers between devices  14.5 us (4%)
  between operations  14.3 us (4%)
  other arithmetic  11.1 us (3%)
    psum x1, waiting for transfers between devices, on_device(): summed = lax.psum(slot_grad, 'epoch')  114 us
    gather x4, local copies, waits for them, and re-layouts, toeplitz(): taps[jnp.clip(where_at, 0, taps.shape[0] - 1)]  49.5 us
    all_to_all x1, blocking collectives, on_device(): lax.all_to_all(patches.reshape(n_sky, capacity, -1), 'sky', split_axis=0,...  30.3 us
    all_to_all x1, waiting for transfers between devices, on_device(): lax.all_to_all(made, 'sky', split_axis=0, concat_axis=0, tiled=True)  26.1 us
    dot_general x8, matrix products, place(): jnp.einsum('nab,nbj->naj', stamps_b, col_one, preferred_element_type=jnp....  17.6 us
    dot_general x8, matrix products, pick(): jnp.einsum('naj,nbj->nab', lifted, col_one, preferred_element_type=jnp.fl...  15.3 us
    convert_element_type x2, local copies, waits for them, and re-layouts, on_device(): made = rendered.reshape(-1, stamp_size * stamp_size).astype(jnp.bfloat16)...  13.3 us
    reshape x2, local copies, waits for them, and re-layouts, on_device(): returned.reshape(slots, -1).astype(jnp.float32)  12.5 us
  transfers between devices with their start and end apart: 6, of which 4 were waited for; matrix products, arithmetic and copies ran while one was open for 0% of the time, Pallas kernels for 0%

commit v1 on v0

v1 whole, which is shorter than its diff:
```python
import functools
import math

import jax
import jax.numpy as jnp
from jax import lax
from jax.experimental import pallas as pl
from jax.experimental.pallas import tpu as pltpu
from jax.sharding import PartitionSpec as P

PS = 64
ST = 64
TAPS = 51
HALF = 25
TR = 256
TW = 512
MARGIN = 32
CANVAS = 320
CAP = 16
NSKY = 16
SLOTS = 768
SROWS = 776
OFF = 64
CROWS = 448
XROWS = 320
NCANV = 4
GROUP = 8
CHUNKS = 16
HIGHEST = lax.Precision.HIGHEST


def dot(a, b, dims, precision=None):
    return lax.dot_general(a, b, (dims, ((), ())), precision=precision, preferred_element_type=jnp.float32)


def split3(x):
    high = x.astype(jnp.bfloat16)
    rest = x - high.astype(jnp.float32)
    mid = rest.astype(jnp.bfloat16)
    low = (rest - mid.astype(jnp.float32)).astype(jnp.bfloat16)
    return high, mid, low


def iota(shape, axis):
    return lax.broadcasted_iota(jnp.int32, shape, axis)


def basis_kernel(taps_s, taps_v, basis_ref, out_ref, xs, ts):
    f32 = jnp.float32
    total = jnp.sum(taps_v[...], axis=1, keepdims=True)
    at = iota((128, 32), 0)
    where_at = at % 64 - (2 * iota((128, 32), 1) + at // 64) + HALF
    row_k = jnp.zeros((128, 32), f32)
    for t in range(TAPS):
        row_k = jnp.where(where_at == t, taps_s[0, t], row_k)
    row_k = row_k / total[0:1, :]
    row_parts = jnp.concatenate(split3(row_k), axis=1)
    b_at, d_at = iota((64, 256), 0), iota((64, 256), 1)
    where_at = d_at % 64 - b_at + HALF
    col_k = jnp.zeros((64, 256), f32)
    for t in range(TAPS):
        col_k = jnp.where(where_at == t, taps_s[1, t], col_k)
    col_k = col_k / total[1:2, :]
    col_k = jnp.concatenate([jnp.where(d_at // 64 == i, col_k, 0.0) for i in range(4)], axis=0)
    col_h, col_m, col_l = split3(col_k)

    for j in range(32):
        xs[j * 64:(j + 1) * 64, :] = basis_ref[:, j * 128:(j + 1) * 128].astype(f32)
    lane = iota((64, 128), 1)

    def rows_step(g, unused):
        images = [xs[pl.ds(g * 8 + i, 32, stride=64), :].astype(jnp.bfloat16) for i in range(8)]
        wide = jnp.concatenate(images, axis=1)
        made = dot(row_parts, jnp.concatenate([wide, wide, wide], axis=0), ((1,), (0,)))
        for i in range(8):
            both = jnp.where(lane < 64, made[:64, i * 128:(i + 1) * 128], made[64:, i * 128:(i + 1) * 128])
            both = both + pltpu.roll(both, 64, 1)
            ts[pl.ds(g * 8 + i, 32, stride=64), :] = jnp.where(lane[:32] < 64, both[:32], both[32:])
        return unused

    lax.fori_loop(0, 8, rows_step, 0)

    def cols_step(c, unused):
        base = pl.multiple_of(c * 128, 128)
        x = jnp.concatenate([ts[pl.ds(base, 64), :], ts[pl.ds(base + 64, 64), :]], axis=1)
        xh, xm, xl = split3(x)
        d = functools.partial(dot, dims=((1,), (0,)))
        y = d(xl, col_h) + d(xh, col_l) + d(xm, col_m) + d(xm, col_h) + d(xh, col_m) + d(xh, col_h)
        yh, ym, yl = split3(y)
        out_ref[c, 0:64, :] = yh
        out_ref[c, 64:128, :] = ym
        out_ref[c, 128:192, :] = yl
        return unused

    lax.fori_loop(0, CHUNKS, cols_step, 0)


def sky_kernel(own_s, up_s, down_s, b_ref, sp_ref, obs_ref, back_ref, halo_up_ref, halo_down_ref,
               res_ref, keep_ref, give_ref, ss, xs, acc, listed, *canvases):
    f32 = jnp.float32
    tile = lax.axis_index("sky")
    core = lax.axis_index("epoch") % 2
    lane8 = iota((8, 128), 1)

    zero = jnp.zeros((CROWS, 128), f32)
    for canvas in canvases:
        for q in range(5):
            canvas[q * CROWS:(q + 1) * CROWS, :] = zero
    for j in range(32):
        ss[j * SROWS + SLOTS:(j + 1) * SROWS, :] = jnp.zeros((SROWS - SLOTS, 128), f32)

    sp = sp_ref[...]
    sp3 = jnp.concatenate([sp, sp, sp], axis=1)

    def render(c, count):
        made = dot(sp3, b_ref[c], ((1,), (0,)))
        made = made.astype(jnp.bfloat16).astype(f32)
        base = pl.multiple_of(c * (2 * SROWS), 8)
        ss[pl.ds(base, SLOTS), :] = made[:, :128]
        ss[pl.ds(base + SROWS, SLOTS), :] = made[:, 128:]
        for which, ref in enumerate((up_s, own_s, down_s)):
            total = ref[32, c]
            for k in range(CAP):
                row, col = ref[c, k], ref[16 + c, k]
                live = k < total
                if which == 0:
                    live = live & (row > 192)
                if which == 2:
                    live = live & (row < 64)
                where_to = row + (which - 1) * TR + OFF
                listed[count] = ((c * 48 + which * 16 + k) * 512 + where_to) * 512 + col
                count = count + live.astype(jnp.int32)
        return count

    count = lax.fori_loop(0, CHUNKS, render, jnp.int32(0))
    for i in range(GROUP):
        listed[count + i] = (SLOTS * 512 + OFF) * 512

    lane32 = iota((32, 128), 1)

    def place(g, unused):
        for i in range(GROUP):
            canvas = canvases[i % NCANV]
            entry = listed[g * GROUP + i]
            slot = entry >> 18
            row = (entry >> 9) & 511
            col = entry & 511
            shift = col & 127
            start = (col >> 7) * CROWS + row
            stamp = ss[pl.ds(slot, 32, stride=SROWS), :]
            first = (lane32 >= shift) & (lane32 < shift + 64)
            second = lane32 < shift - 64
            for h in range(2):
                turned = pltpu.roll(stamp, (shift + 64 * h) & 127, 1)
                a = start + 32 * h
                canvas[pl.ds(a, 32), :] += jnp.where(first, turned, 0.0)
                canvas[pl.ds(a + CROWS, 32), :] += jnp.where(second, turned, 0.0)
        return unused

    lax.fori_loop(0, (count + GROUP - 1) // GROUP, place, 0)

    def pixels(observed, background, image):
        e = jnp.exp(-jnp.abs(image))
        soft = jnp.maximum(image, 0.0) + jnp.log1p(e)
        sig = jnp.where(image >= 0.0, 1.0, e) / (1.0 + e)
        return (observed / (background + soft) - 1.0) * sig

    def image_at(q, row, rows):
        at = pl.ds(q * CROWS + OFF + row, rows)
        image = canvases[0][at, :]
        for canvas in canvases[1:]:
            image = image + canvas[at, :]
        return image

    def rounded(x):
        return x.astype(jnp.bfloat16).astype(f32)

    for q in range(4):
        lanes = slice(q * 128, (q + 1) * 128)
        r = pixels(halo_up_ref[:32, lanes], halo_up_ref[32:, lanes], image_at(q, 0, 32))
        xs[q * XROWS:q * XROWS + 32, :] = jnp.where(tile > 0, rounded(r), 0.0)
        r = pixels(halo_down_ref[:32, lanes], halo_down_ref[32:, lanes], image_at(q, 288, 32))
        xs[q * XROWS + 288:q * XROWS + 320, :] = jnp.where(tile < NSKY - 1, rounded(r), 0.0)

    def block(i, unused):
        base = pl.multiple_of(i * 32, 32)
        for q in range(4):
            lanes = slice(q * 128, (q + 1) * 128)
            r = pixels(obs_ref[pl.ds(base, 32), lanes], back_ref[pl.ds(base, 32), lanes], image_at(q, 32 + base, 32))
            res_ref[pl.ds(base, 32), lanes] = r
            xs[pl.ds(q * XROWS + 32 + base, 32), :] = rounded(r)
        return unused

    lax.fori_loop(0, 8, block, 0)

    def window(g, unused):
        for i in range(GROUP):
            o = g // 2
            k = (g % 2) * GROUP + i
            slot = g * GROUP + i
            row, col = own_s[o, k], own_s[16 + o, k]
            shift = col & 127
            start = (col >> 7) * XROWS + row
            parts = []
            for h in range(2):
                a = start + 32 * h
                seen = jnp.where(lane32 >= shift, xs[pl.ds(a, 32), :], xs[pl.ds(a + XROWS, 32), :])
                parts.append(pltpu.roll(seen, (64 * h - shift) & 127, 1))
            ss[pl.ds(slot, 32, stride=SROWS), :] = jnp.where(lane32 < 64, parts[0], parts[1])
        return unused

    lax.fori_loop(0, 256 // GROUP, window, 0)

    def gather(c, total):
        base = pl.multiple_of(c * (2 * SROWS), 8)
        w = jnp.concatenate([ss[pl.ds(base, 256), :], ss[pl.ds(base + SROWS, 256), :]], axis=1).astype(jnp.bfloat16)
        return total + dot(w, b_ref[c], ((1,), (1,)))

    total = lax.fori_loop(0, CHUNKS, gather, jnp.zeros((256, 192), f32))
    grad = total[:, 128:192] + total[:, 64:128] + total[:, :64]
    slot_k = iota((CAP, 64), 0)
    for o in range(NSKY):
        acc[o * 16:(o + 1) * 16, :] = jnp.where(slot_k < own_s[32, o], grad[o * 16:(o + 1) * 16], 0.0)
    for o in range(NSKY):
        keep_ref[o * 8:(o + 1) * 8, :] = acc[pl.ds(pl.multiple_of(o * 16 + core * 8, 8), 8), :]
        give_ref[o * 8:(o + 1) * 8, :] = acc[pl.ds(pl.multiple_of(o * 16 + 8 - core * 8, 8), 8), :]


def owner_kernel(index_s, got_ref, out_ref, hot):
    f32 = jnp.float32
    core = lax.axis_index("epoch") % 2
    lane = iota((1, 128), 1)
    for t in range(NSKY):
        for k in range(8):
            hot[t * 8 + k:t * 8 + k + 1, :] = jnp.where(lane == index_s[t, core * 8 + k], 1.0, 0.0).astype(f32)
    sums = []
    for t in range(NSKY):
        s = got_ref[t * 8]
        for z in range(1, 8):
            s = s + got_ref[t * 8 + z]
        sums.append(s)
    out_ref[...] = dot(hot[...], jnp.concatenate(sums, axis=0), ((0,), (0,)), HIGHEST)


SM = pl.BlockSpec(memory_space=pltpu.SMEM)
VM = pl.BlockSpec(memory_space=pltpu.VMEM)


def on_device(params, basis, psf_taps, send_index, tile_count, stamp_row, stamp_col, observed, background):
    f32 = jnp.float32
    n = NSKY
    index = send_index[0]
    spread = jnp.concatenate([jnp.roll(index, 1, 0), index, jnp.roll(index, -1, 0)], axis=1)
    outgoing = params[spread]
    slot_params = lax.all_to_all(outgoing, "sky", split_axis=0, concat_axis=0, tiled=True).reshape(SLOTS, PS)

    to_next = [(i, i + 1) for i in range(n - 1)]
    to_prev = [(i + 1, i) for i in range(n - 1)]
    spots = jnp.concatenate([stamp_row[0], stamp_col[0], tile_count], axis=0)
    obs, back = observed[0], background[0]
    spots_up = lax.ppermute(spots, "sky", to_next)
    spots_down = lax.ppermute(spots, "sky", to_prev)
    halo_up = lax.ppermute(jnp.concatenate([obs[TR - 32:], back[TR - 32:]], axis=0), "sky", to_next)
    halo_down = lax.ppermute(jnp.concatenate([obs[:32], back[:32]], axis=0), "sky", to_prev)

    taps = psf_taps[0]
    shaped = pl.pallas_call(
        basis_kernel,
        out_shape=jax.ShapeDtypeStruct((CHUNKS, 192, 256), jnp.bfloat16),
        in_specs=[SM, VM, VM],
        out_specs=VM,
        scratch_shapes=[pltpu.VMEM((2048, 128), f32), pltpu.VMEM((2048, 128), f32)],
        compiler_params=pltpu.CompilerParams(vmem_limit_bytes=16 << 20),
        cost_estimate=pl.CostEstimate(flops=2 * 10 ** 9, bytes_accessed=2 << 20, transcendentals=0),
    )(taps, taps, basis)

    residual, keep, give = pl.pallas_call(
        sky_kernel,
        out_shape=(
            jax.ShapeDtypeStruct((TR, TW), f32),
            jax.ShapeDtypeStruct((128, PS), f32),
            jax.ShapeDtypeStruct((128, PS), f32),
        ),
        in_specs=[SM, SM, SM] + [VM] * 6,
        out_specs=(VM, VM, VM),
        scratch_shapes=[
            pltpu.VMEM((32 * SROWS, 128), f32),
            pltpu.VMEM((5 * XROWS, 128), f32),
            pltpu.VMEM((256, PS), f32),
            pltpu.SMEM((SLOTS + GROUP,), jnp.int32),
        ] + [pltpu.VMEM((5 * CROWS, 128), f32)] * NCANV,
        compiler_params=pltpu.CompilerParams(vmem_limit_bytes=40 << 20),
        cost_estimate=pl.CostEstimate(flops=4 * 10 ** 9, bytes_accessed=4 << 20, transcendentals=0),
    )(spots, spots_up, spots_down, shaped, slot_params, obs, back, halo_up, halo_down)

    swap = [(i, i ^ 1) for i in range(16)]
    mine = keep + lax.ppermute(give, "epoch", swap)
    sent = jnp.broadcast_to(mine.reshape(n, 1, 8, PS), (n, 8, 8, PS)).reshape(128, 8, PS)
    groups = [[t * 16 + z * 2 + c for t in range(16) for z in range(8)] for c in range(2)]
    got = lax.all_to_all(sent, ("sky", "epoch"), split_axis=0, concat_axis=0, tiled=True, axis_index_groups=groups)
    part = pl.pallas_call(
        owner_kernel,
        out_shape=jax.ShapeDtypeStruct((128, PS), f32),
        in_specs=[SM, VM],
        out_specs=VM,
        scratch_shapes=[pltpu.VMEM((128, 128), f32)],
        compiler_params=pltpu.CompilerParams(vmem_limit_bytes=8 << 20),
    )(index, got)
    grad = part + lax.ppermute(part, "epoch", swap)
    return grad, residual[None]


def solution(mesh):
    in_specs = (
        P("sky", None),
        P(),
        P("epoch", None, None),
        P("sky", None, None),
        P("sky", None),
        P("sky", None, None),
        P("sky", None, None),
        P("epoch", "sky", None),
        P("epoch", "sky", None),
    )
    out_specs = (P("sky", None), P("epoch", "sky", None))
    return jax.shard_map(on_device, mesh=mesh, in_specs=in_specs, out_specs=out_specs, check_vma=False)
```

time: 404 us -> 96.5 us (0.24)
  waiting for transfers between devices: 147 us -> 1.82 us
  local copies, waits for them, and re-layouts: 108 us -> 9.56 us
  matrix products: 77.2 us -> 0 us
  Pallas kernels: 0 us -> 27.6 us
  between operations: 14.3 us -> 0.89 us
  other arithmetic: 11.1 us -> 2.92 us
  starting transfers between devices: 14.5 us -> 21.5 us
    psum x1 -> x0, waiting for transfers between devices: 114 us -> none  [on_device(): summed = lax.psum(slot_grad, 'epoch')]
    dot_general x39 -> x0, matrix products: 77.2 us -> none  [the longest x8 17.6 us: place(): jnp.einsum('nab,nbj->naj', stamps_b, col_one, preferred_element_type=jnp....]
    gather x5 -> x1, local copies, waits for them, and re-layouts: 50.4 us -> 1.88 us  [on_device(): outgoing = params[spread]]
    pallas_call x0 -> x3, Pallas kernels: none -> 27.6 us  [the longest x1 18 us: on_device(): pl.pallas_call(sky_kernel, out_shape=(jax.ShapeDtypeStruct((TR, TW), f32)...]
    all_to_all x1, waiting for transfers between devices: 26.1 us -> 0.01 us  [on_device(): lax.all_to_all(outgoing, 'sky', split_axis=0, concat_axis=0, tiled=True)]
    reshape x4 -> x0, local copies, waits for them, and re-layouts: 23.7 us -> none  [the longest x2 12.5 us: on_device(): returned.reshape(slots, -1).astype(jnp.float32)]
    dot_general x3 -> x0, local copies, waits for them, and re-layouts: 17.6 us -> none  [the longest x1 9.16 us: on_device(): jnp.einsum('ba,nbc,cd->nad', row_kernel, window, col_kernel, precision=hi...]
    convert_element_type x2 -> x0, local copies, waits for them, and re-layouts: 13.3 us -> none  [on_device(): made = rendered.reshape(-1, stamp_size * stamp_size).astype(jnp.bfloat16)...]
  transfers between devices with their start and end apart: 6 -> 7, of which waited for: 4 -> 2; matrix products, arithmetic and copies ran while one was open for 0% -> 6% of each run, Pallas kernels for 0% -> 9%
where the time goes in v1:
time: 96.5 us; the launch traced here: 96.7 us
  blocking collectives  32.5 us (34%)
  Pallas kernels  27.6 us (29%)
  starting transfers between devices  21.5 us (22%)
  local copies, waits for them, and re-layouts  9.56 us (10%)
  other arithmetic  2.92 us (3%)
  waiting for transfers between devices  1.82 us (2%)
    all_to_all x1, blocking collectives, on_device(): lax.all_to_all(sent, ('sky', 'epoch'), split_axis=0, concat_axis=0, tiled...  32.5 us
    pallas_call x1, Pallas kernels, on_device(): pl.pallas_call(sky_kernel, out_shape=(jax.ShapeDtypeStruct((TR, TW), f32)...  18 us
    pallas_call x1, Pallas kernels, on_device(): pl.pallas_call(basis_kernel, out_shape=jax.ShapeDtypeStruct((CHUNKS, 192,...  8.53 us
    all_to_all x1, starting transfers between devices, on_device(): lax.all_to_all(outgoing, 'sky', split_axis=0, concat_axis=0, tiled=True)  7.54 us
    unnamed x20, local copies, waits for them, and re-layouts  5.55 us
    ppermute x1, starting transfers between devices, on_device(): spots_up = lax.ppermute(spots, 'sky', to_next)  4.02 us
    ppermute x1, starting transfers between devices, on_device(): lax.ppermute(jnp.concatenate([obs[TR - 32:], back[TR - 32:]], axis=0), 's...  3.27 us
    ppermute x1, starting transfers between devices, on_device(): mine = keep + lax.ppermute(give, 'epoch', swap)  2.05 us
  transfers between devices with their start and end apart: 7, of which 2 were waited for; matrix products, arithmetic and copies ran while one was open for 6% of the time, Pallas kernels for 9%

profile of v1, /device:TPU:1, one launch (start us, length us, event | category | flops | bytes accessed | tf_op | source)
XLA Modules:
  0.0 96.7 jit_solution(5744523169269233600)
XLA Ops:
  0.6 0.0 copy-start.1
  0.6 0.0 copy-start.2
  0.7 0.8 pad_add_fusion.own_s
  1.5 4.0 %collective-permute-start = (s32[33,16]{1,0:T(8,128)S(1)}, s32[33,16]{1,0:T(8,128)S(1)}, u32[]{:S(2)}, u32[]{:S(2)}) collective-permute-start(s32[33,16]{1,0:T(8,128)S(1)} %pad_add_fusion.own_s), channel_id=1, source_target_pairs={{0,16},{16,32},{32,48},{48,64},{64,80},{80,96},{96,112},{112,128},... | collective-permute-start | bytes 6344 | tf_op jit(solution)/shard_map/ppermute | solution.py:261
  5.5 1.3 %collective-permute-start.1 = (s32[33,16]{1,0:T(8,128)S(1)}, s32[33,16]{1,0:T(8,128)S(1)}, u32[]{:S(2)}, u32[]{:S(2)}) collective-permute-start(s32[33,16]{1,0:T(8,128)S(1)} %pad_add_fusion.own_s), channel_id=1, source_target_pairs={{16,0},{32,16},{48,32},{64,48},{80,64},{96,80},{112,96},{128,112},... | collective-permute-start | bytes 6344 | tf_op jit(solution)/shard_map/ppermute | solution.py:262
  6.8 0.8 slice_bitcast_fusion.5
  7.6 0.7 slice_bitcast_fusion.7
  8.3 0.8 compare_select_fusion
  9.1 0.1 reshape.145
  9.2 0.8 copy.21
  10.0 0.0 copy-start.3
  10.0 0.0 copy-start.4
  10.0 1.9 %gather_fusion = bf16[768,64]{1,0:T(8,128)(2,1)S(1)} fusion(bf16[128,64]{1,0:T(8,128)(2,1)S(1)} %copy.21, s32[1024]{0:T(1024)S(1)} %pad_clamp_fusion), kind=kCustom, calls=%fused_computation | custom fusion | bytes 199680 | tf_op jit(solution)/shard_map/gather | solution.py:254
  11.9 0.8 reshape.152
  12.7 7.5 %all-to-all-start = ((bf16[16,2,1536]{2,1,0:T(2,128)(2,1)}), bf16[16,2,1536]{2,1,0:T(2,128)(2,1)S(1)}, u32[]{:S(2)}, u32[]{:S(2)}) async-start(bf16[16,2,1536]{2,1,0:T(2,128)(2,1)} %reshape.152), calls=%async_computation | async-start | bytes 196608 | tf_op jit(solution)/shard_map/all_to_all | solution.py:255
  20.3 0.0 copy-done.1
  20.3 0.0 copy-done.2
  20.3 3.3 %collective-permute-start.2 = (f32[64,512]{1,0:T(8,128)S(1)}, f32[64,512]{1,0:T(8,128)S(1)}, u32[]{:S(2)}, u32[]{:S(2)}) collective-permute-start(f32[64,512]{1,0:T(8,128)S(1)} %pad_maximum_fusion), channel_id=1, source_target_pairs={{0,16},{16,32},{32,48},{48,64},{64,80},{80,96},{96,112},{112,128},... | collective-permute-start | bytes 393224 | tf_op jit(solution)/shard_map/ppermute | solution.py:263
  23.6 1.3 %collective-permute-start.3 = (f32[64,512]{1,0:T(8,128)S(1)}, f32[64,512]{1,0:T(8,128)S(1)}, u32[]{:S(2)}, u32[]{:S(2)}) collective-permute-start(f32[64,512]{1,0:T(8,128)S(1)} %pad_maximum_fusion.1), channel_id=1, source_target_pairs={{16,0},{32,16},{48,32},{64,48},{80,64},{96,80},{112,96},{128,112},... | collective-permute-start | bytes 393224 | tf_op jit(solution)/shard_map/ppermute | solution.py:264
  24.9 0.0 copy-done.3
  24.9 0.0 copy-done.4
  25.0 8.5 %shard_map.104.b_ref = bf16[16,192,256]{2,1,0:T(8,128)(2,1)S(1)} custom-call(f32[2,51]{1,0:T(2,128)S(1)} %bitcast.40, f32[2,51]{1,0:T(2,128)S(1)} %bitcast.41, bf16[64,4096]{1,0:T(8,128)(2,1)S(1)} %copy-done.3), custom_call_target="tpu_custom_call" | custom-call | flops 2000000000 | bytes 2097152 | tf_op jit(solution)/shard_map/pallas_call | solution.py:267
  33.5 0.0 copy-start.5
  33.5 1.2 %copy-done.5 = bf16[16,192,256]{2,1,0:T(8,128)(2,1)} copy-done((bf16[16,192,256]{2,1,0:T(8,128)(2,1)}, bf16[16,192,256]{2,1,0:T(8,128)(2,1)S(1)}, u32[]{:S(2)}) %copy-start.5) | copy-done | bytes 1572888
  34.7 0.0 all-to-all-done
  34.7 0.2 reshape.153
  34.8 0.0 collective-permute-done.up_s
  34.9 0.0 collective-permute-done.1.down_s
  34.9 0.0 collective-permute-done.2.halo_up_ref
  34.9 0.0 collective-permute-done.3.halo_down_ref
  34.9 0.0 copy-start.6
  34.9 1.4 %copy-done.6 = bf16[16,192,256]{2,1,0:T(8,128)(2,1)S(1)} copy-done((bf16[16,192,256]{2,1,0:T(8,128)(2,1)S(1)}, bf16[16,192,256]{2,1,0:T(8,128)(2,1)}, u32[]{:S(2)}) %copy-start.6) | copy-done | bytes 1572888
  36.3 18.0 %shard_map.105 = (f32[256,512]{1,0:T(8,128)}, f32[128,64]{1,0:T(8,128)S(1)}, f32[128,64]{1,0:T(8,128)S(1)}) custom-call(s32[33,16]{1,0:T(8,128)S(1)} %pad_add_fusion.own_s, s32[33,16]{1,0:T(8,128)S(1)} %collective-permute-done.up_s, s32[33,16]{1,0:T(8,128)S(1)} %collective-permute-done.1.down_s, bf16[16,192,256]{2,1,0:T(8,128)(2,1)S(1)} %copy-done.6, ...), custom_call_target="tpu_custom_call" | custom-call | flops 4000000000 | bytes 4194304 | tf_op jit(solution)/shard_map/pallas_call | solution.py:277
  54.3 2.1 %collective-permute-start.4 = (f32[128,64]{1,0:T(8,128)S(1)}, f32[128,64]{1,0:T(8,128)S(1)}, u32[]{:S(2)}, u32[]{:S(2)}) collective-permute-start(f32[128,64]{1,0:T(8,128)S(1)} %get-tuple-element.6), channel_id=1, source_target_pairs={{0,1},{1,0},{2,3},{3,2},{4,5},{5,4},{6,7},{7,6},{8,9},{9,8},{10,11... | collective-permute-start | bytes 98312 | tf_op jit(solution)/shard_map/ppermute | solution.py:297
  56.4 0.9 collective-permute-done.4
  57.3 0.0 copy-start
  57.3 0.3 reshape.154
  57.7 32.5 %all_to_all.10 = f32[128,1,512]{2,1,0:T(1,128)S(1)} all-to-all(f32[128,1,512]{2,1,0:T(1,128)S(1)} %reshape.154), channel_id=1, replica_groups={{0,2,4,6,8,10,12,14,16,18,20,22,24,26,28,30,32,34,36,38,40,42,44,46,48,..., dimensions={0} | all-to-all | bytes 524288 | tf_op jit(solution)/shard_map/all_to_all | solution.py:300
  90.1 0.5 broadcast.18
  90.6 1.3 %reduce = f32[128,512]{1,0:T(8,128)S(1)} reduce(f32[128,1,512]{2,1,0:T(1,128)S(1)} %all_to_all.10, f32[]{:T(128)} %broadcast.18), dimensions={1}, to_apply=%all_to_all.7.reduce_sub_computation | reduce | bytes 524292 | tf_op jit(solution)/shard_map/all_to_all | solution.py:300
  91.9 0.1 reshape.155.got_ref
  92.0 0.0 copy-done
  92.0 1.0 %shard_map.106 = f32[128,64]{1,0:T(8,128)S(1)} custom-call(s32[16,16]{1,0:T(8,128)S(1)} %bitcast.37, f32[128,8,64]{2,1,0:T(8,128)S(1)} %reshape.155.got_ref), custom_call_target="tpu_custom_call" | custom-call | tf_op jit(solution)/shard_map/pallas_call | solution.py:301
  93.1 2.0 %collective-permute-start.5 = (f32[128,64]{1,0:T(8,128)S(1)}, f32[128,64]{1,0:T(8,128)S(1)}, u32[]{:S(2)}, u32[]{:S(2)}) collective-permute-start(f32[128,64]{1,0:T(8,128)S(1)} %shard_map.106), channel_id=1, source_target_pairs={{0,1},{1,0},{2,3},{3,2},{4,5},{5,4},{6,7},{7,6},{8,9},{9,8},{10,11... | collective-permute-start | bytes 98312 | tf_op jit(solution)/shard_map/ppermute | solution.py:309
  95.1 0.9 collective-permute-done.5
  96.0 0.7 copy.22
  (8 shorter events, 0.1 us)
Async XLA Ops:
  0.6 19.6 %copy-start.1 = (f32[1,256,512]{2,1,0:T(8,128)S(1)}, f32[1,256,512]{2,1,0:T(8,128)}, u32[]{:S(2)}) copy-start(f32[1,256,512]{2,1,0:T(8,128)} %param.16) | copy-start | bytes 1572868
  0.6 19.6 %copy-start.2 = (f32[1,256,512]{2,1,0:T(8,128)S(1)}, f32[1,256,512]{2,1,0:T(8,128)}, u32[]{:S(2)}) copy-start(f32[1,256,512]{2,1,0:T(8,128)} %param.17) | copy-start | bytes 1572868
  1.5 33.4 %collective-permute-start = (s32[33,16]{1,0:T(8,128)S(1)}, s32[33,16]{1,0:T(8,128)S(1)}, u32[]{:S(2)}, u32[]{:S(2)}) collective-permute-start(s32[33,16]{1,0:T(8,128)S(1)} %pad_add_fusion.own_s), channel_id=1, source_target_pairs={{0,16},{16,32},{32,48},{48,64},{64,80},{80,96},{96,112},{112,128},... | collective-permute-start | bytes 6344 | tf_op jit(solution)/shard_map/ppermute | solution.py:261
  5.5 29.4 %collective-permute-start.1 = (s32[33,16]{1,0:T(8,128)S(1)}, s32[33,16]{1,0:T(8,128)S(1)}, u32[]{:S(2)}, u32[]{:S(2)}) collective-permute-start(s32[33,16]{1,0:T(8,128)S(1)} %pad_add_fusion.own_s), channel_id=1, source_target_pairs={{16,0},{32,16},{48,32},{64,48},{80,64},{96,80},{112,96},{128,112},... | collective-permute-start | bytes 6344 | tf_op jit(solution)/shard_map/ppermute | solution.py:262
  10.0 14.9 %copy-start.3 = (bf16[64,4096]{1,0:T(8,128)(2,1)S(1)}, bf16[64,4096]{1,0:T(8,128)(2,1)}, u32[]{:S(2)}) copy-start(bf16[64,4096]{1,0:T(8,128)(2,1)} %basis_ref.1) | copy-start | bytes 1572868
  10.0 14.9 %copy-start.4 = (f32[1,2,51]{2,1,0:T(2,128)S(1)}, f32[1,2,51]{2,1,0:T(2,128)}, u32[]{:S(2)}) copy-start(f32[1,2,51]{2,1,0:T(2,128)} %param.11) | copy-start | bytes 1228
  12.7 22.0 %all-to-all-start = ((bf16[16,2,1536]{2,1,0:T(2,128)(2,1)}), bf16[16,2,1536]{2,1,0:T(2,128)(2,1)S(1)}, u32[]{:S(2)}, u32[]{:S(2)}) async-start(bf16[16,2,1536]{2,1,0:T(2,128)(2,1)} %reshape.152), calls=%async_computation | async-start | bytes 196608 | tf_op jit(solution)/shard_map/all_to_all | solution.py:255
  20.3 14.5 %collective-permute-start.2 = (f32[64,512]{1,0:T(8,128)S(1)}, f32[64,512]{1,0:T(8,128)S(1)}, u32[]{:S(2)}, u32[]{:S(2)}) collective-permute-start(f32[64,512]{1,0:T(8,128)S(1)} %pad_maximum_fusion), channel_id=1, source_target_pairs={{0,16},{16,32},{32,48},{48,64},{64,80},{80,96},{96,112},{112,128},... | collective-permute-start | bytes 393224 | tf_op jit(solution)/shard_map/ppermute | solution.py:263
  23.6 11.2 %collective-permute-start.3 = (f32[64,512]{1,0:T(8,128)S(1)}, f32[64,512]{1,0:T(8,128)S(1)}, u32[]{:S(2)}, u32[]{:S(2)}) collective-permute-start(f32[64,512]{1,0:T(8,128)S(1)} %pad_maximum_fusion.1), channel_id=1, source_target_pairs={{16,0},{32,16},{48,32},{64,48},{80,64},{96,80},{112,96},{128,112},... | collective-permute-start | bytes 393224 | tf_op jit(solution)/shard_map/ppermute | solution.py:264
  33.5 1.2 %copy-start.5 = (bf16[16,192,256]{2,1,0:T(8,128)(2,1)}, bf16[16,192,256]{2,1,0:T(8,128)(2,1)S(1)}, u32[]{:S(2)}) copy-start(bf16[16,192,256]{2,1,0:T(8,128)(2,1)S(1)} %shard_map.104.b_ref) | copy-start | bytes 4718596
  34.9 1.4 %copy-start.6 = (bf16[16,192,256]{2,1,0:T(8,128)(2,1)S(1)}, bf16[16,192,256]{2,1,0:T(8,128)(2,1)}, u32[]{:S(2)}) copy-start(bf16[16,192,256]{2,1,0:T(8,128)(2,1)} %copy-done.5) | copy-start | bytes 4718596
  54.3 3.0 %collective-permute-start.4 = (f32[128,64]{1,0:T(8,128)S(1)}, f32[128,64]{1,0:T(8,128)S(1)}, u32[]{:S(2)}, u32[]{:S(2)}) collective-permute-start(f32[128,64]{1,0:T(8,128)S(1)} %get-tuple-element.6), channel_id=1, source_target_pairs={{0,1},{1,0},{2,3},{3,2},{4,5},{5,4},{6,7},{7,6},{8,9},{9,8},{10,11... | collective-permute-start | bytes 98312 | tf_op jit(solution)/shard_map/ppermute | solution.py:297
  57.3 34.8 %copy-start = (s32[1,16,16]{2,1,0:T(8,128)S(1)}, s32[1,16,16]{2,1,0:T(8,128)}, u32[]{:S(2)}) copy-start(s32[1,16,16]{2,1,0:T(8,128)} %param.12) | copy-start | bytes 3076
  93.1 2.9 %collective-permute-start.5 = (f32[128,64]{1,0:T(8,128)S(1)}, f32[128,64]{1,0:T(8,128)S(1)}, u32[]{:S(2)}, u32[]{:S(2)}) collective-permute-start(f32[128,64]{1,0:T(8,128)S(1)} %shard_map.106), channel_id=1, source_target_pairs={{0,1},{1,0},{2,3},{3,2},{4,5},{5,4},{6,7},{7,6},{8,9},{9,8},{10,11... | collective-permute-start | bytes 98312 | tf_op jit(solution)/shard_map/ppermute | solution.py:309

commit v2 on v1

v2 whole, which is shorter than its diff:
```python
import jax
import jax.numpy as jnp
from jax import lax
from jax.experimental import pallas as pl
from jax.experimental.pallas import tpu as pltpu
from jax.sharding import PartitionSpec as P

PS = 64
TAPS = 51
HALF = 25
TR = 256
TW = 512
CAP = 16
NSKY = 16
OWN = 256
SLOTS = 768
SROWS = 776
OFF = 64
CROWS = 448
XROWS = 320
PLANES = 8
PAIRS = 1
GROUP = 8
CHUNKS = 16
BLOCK = 64
DEAD = 128
HIGHEST = lax.Precision.HIGHEST
F32 = jnp.float32
BF16 = jnp.bfloat16


def dot(a, b, dims, precision=None):
    return lax.dot_general(a, b, (dims, ((), ())), precision=precision, preferred_element_type=F32)


def split3(x):
    high = x.astype(BF16)
    rest = x - high.astype(F32)
    mid = rest.astype(BF16)
    low = (rest - mid.astype(F32)).astype(BF16)
    return high, mid, low


def iota(shape, axis):
    return lax.broadcasted_iota(jnp.int32, shape, axis)


def send_kernel(index_s, count_s, params_ref, row_ref, col_ref, out_ref, hot):
    lane = iota((1, 128), 1)
    for t in range(NSKY):
        for k in range(CAP):
            hot[t * 16 + k:t * 16 + k + 1, :] = jnp.where(lane == index_s[t, k], 1.0, 0.0).astype(F32)
    rows = dot(hot[...].astype(BF16), params_ref[...], ((1,), (1,)))
    rows = jnp.concatenate([rows, rows], axis=1).astype(BF16)
    none = jnp.zeros((16, 128), BF16)
    owner, k_at = iota((NSKY, CAP), 0), iota((NSKY, CAP), 1)
    count = jnp.zeros((NSKY, CAP), jnp.int32)
    for o in range(NSKY):
        count = jnp.where(owner == o, count_s[0, o], count)
    row = jnp.where(k_at < count, row_ref[...], DEAD)
    col = col_ref[...]
    spots = jnp.concatenate([row, col >> 1, col & 1, jnp.zeros((NSKY, 80), jnp.int32)], axis=1)
    spots = spots.astype(F32).astype(BF16)
    for t in range(NSKY):
        mine = rows[t * 16:(t + 1) * 16]
        out_ref[t, 16:32, :] = mine
        if t + 1 < NSKY:
            out_ref[t + 1, 0:16, :] = mine
        if t > 0:
            out_ref[t - 1, 32:48, :] = mine
        out_ref[t, 48:64, :] = spots
    out_ref[0, 0:16, :] = none
    out_ref[NSKY - 1, 32:48, :] = none


def basis_kernel(taps_ref, basis_ref, out_ref, taps_pad, xs, ts):
    taps_pad[...] = jnp.zeros((8, 128), F32)
    taps = taps_ref[...]
    taps_pad[0:2, 0:TAPS] = taps / jnp.sum(taps, axis=1, keepdims=True)
    lane = iota((64, 128), 1)

    row_taps = jnp.broadcast_to(taps_pad[0:1, :], (32, 128))
    even = pltpu.roll(pltpu.roll(row_taps, 128 - HALF, 1), 0, 1, stride=2, stride_axis=0)
    odd = pltpu.roll(even, 1, 1)
    row_k = jnp.where(lane[:32] < 64, even, pltpu.roll(odd, 64, 1))
    parts = [x.astype(F32) for x in split3(row_k)] + [jnp.zeros((32, 128), F32)]
    row_parts = jnp.concatenate(parts, axis=0).T.astype(BF16)

    col_taps = jnp.broadcast_to(taps_pad[1:2, :], (64, 128))
    col_k = pltpu.roll(pltpu.roll(col_taps, 128 - HALF, 1), 0, 1, stride=1, stride_axis=0)
    left = jnp.where(lane < 64, col_k, 0.0)
    right = jnp.where(lane < 64, 0.0, pltpu.roll(col_k, 64, 1))
    none = jnp.zeros((64, 128), F32)
    col_k = jnp.concatenate([
        jnp.concatenate([left, none], axis=1), jnp.concatenate([right, none], axis=1),
        jnp.concatenate([none, left], axis=1), jnp.concatenate([none, right], axis=1)], axis=0)
    ch, cm, cl = split3(col_k)
    col_parts = jnp.concatenate([ch, cl, cm, ch, cm, ch], axis=0)

    for j in range(32):
        xs[j * 64:(j + 1) * 64, :] = basis_ref[:, j * 128:(j + 1) * 128].astype(F32)
    for g in range(8):
        images = [xs[pl.ds(g * 8 + i, 32, stride=64), :].astype(BF16) for i in range(8)]
        wide = jnp.concatenate(images, axis=1)
        made = dot(row_parts, jnp.concatenate([wide, wide, wide, wide], axis=0), ((1,), (0,)))
        for i in range(8):
            both = jnp.where(lane < 64, made[:64, i * 128:(i + 1) * 128], made[64:, i * 128:(i + 1) * 128])
            both = both + pltpu.roll(both, 64, 1)
            ts[pl.ds(g * 8 + i, 32, stride=64), :] = jnp.where(lane[:32] < 64, both[:32], both[32:])
    for m in range(4):
        x = jnp.concatenate([
            jnp.concatenate([ts[c * 128:c * 128 + 64, :], ts[c * 128 + 64:c * 128 + 128, :]], axis=1)
            for c in range(m * 4, m * 4 + 4)], axis=0)
        xh, xm, xl = split3(x)
        y = dot(jnp.concatenate([xl, xh, xm, xm, xh, xh], axis=1), col_parts, ((1,), (0,)))
        for part, v in enumerate(split3(y)):
            for i in range(4):
                out_ref[m * 4 + i, part * 64:(part + 1) * 64, :] = v[i * 64:(i + 1) * 64]


def sky_kernel(row_s, col_s, count_s, b_ref, got_ref, obs_ref, back_ref, halo_up_ref, halo_down_ref,
               res_ref, keep_ref, give_ref, ss, xs, xt, acc, near, packed, spots_v, spots_s, listed, sem, *canvases):
    tile = lax.axis_index("sky")
    core = lax.axis_index("epoch") % 2
    lane32 = iota((32, 128), 1)

    def spots_of(which, there):
        spots = got_ref[which, 48:64, :].astype(F32)
        row = spots.astype(jnp.int32)
        col = 2 * pltpu.roll(spots, 112, 1).astype(jnp.int32) + pltpu.roll(spots, 96, 1).astype(jnp.int32)
        return row, col

    row, col = spots_of(jnp.maximum(tile - 1, 0), None)
    spots_v[0:16, :] = jnp.where((row > 192) & (tile > 0), (row - TR + OFF) * 512 + col, -1)
    row, col = spots_of(jnp.minimum(tile + 1, NSKY - 1), None)
    spots_v[16:32, :] = jnp.where((row < 64) & (tile < NSKY - 1), (row + TR + OFF) * 512 + col, -1)
    copy = pltpu.make_async_copy(spots_v, spots_s, sem)
    copy.start()

    k_at = iota((CAP, 128), 0)
    mine = []
    for o in range(NSKY):
        mine.append(jnp.where(k_at < count_s[0, o], got_ref[o, 16:32, :].astype(F32), 0.0).astype(BF16))
        near[o * 32:o * 32 + 16, :] = got_ref[o, 0:16, :].astype(F32)
        near[o * 32 + 16:o * 32 + 32, :] = got_ref[o, 32:48, :].astype(F32)

    def three(x):
        return jnp.concatenate([x, x[:, :64]], axis=1)

    mine = three(jnp.concatenate(mine, axis=0))
    for j in range(32):
        ss[j * SROWS + SLOTS:(j + 1) * SROWS, :] = jnp.zeros((SROWS - SLOTS, 128), F32)
    copy.wait()

    span = PLANES * CROWS // CHUNKS

    def render(c, count):
        made = dot(mine, b_ref[c], ((1,), (0,)))
        made = made.astype(BF16).astype(F32)
        base = pl.multiple_of(c * (2 * SROWS), 8)
        ss[pl.ds(base, OWN), :] = made[:, :128]
        ss[pl.ds(base + SROWS, OWN), :] = made[:, 128:]
        for canvas in canvases:
            canvas[pl.ds(pl.multiple_of(c * span, 8), span), :] = jnp.zeros((span, 128), F32)
        for which in range(2):
            for k in range(CAP):
                entry = spots_s[which * 16 + c, k]
                listed[count] = entry
                packed[pl.ds(count, 1), :] = near[pl.ds(c * 32 + which * 16 + k, 1), :]
                count = count + jnp.where(entry >= 0, 1, 0)
        return count

    count = lax.fori_loop(0, CHUNKS, render, jnp.int32(0))

    def render_near(b, unused):
        base = pl.multiple_of(b * BLOCK, BLOCK)
        x = three(packed[pl.ds(base, BLOCK), :].astype(BF16))
        for c in range(CHUNKS):
            made = dot(x, b_ref[c], ((1,), (0,))).astype(BF16).astype(F32)
            ss[pl.ds(2 * c * SROWS + OWN + base, BLOCK), :] = made[:, :128]
            ss[pl.ds((2 * c + 1) * SROWS + OWN + base, BLOCK), :] = made[:, 128:]
        return unused

    lax.fori_loop(0, (count + BLOCK - 1) // BLOCK, render_near, 0)

    def put(i, slot, row, col):
        turn = col & 127
        start = (col >> 6) * CROWS + row
        turned = pltpu.roll(ss[pl.ds(slot, 32, stride=SROWS), :], turn, 1)
        inside = ((lane32 - turn) & 127) < 64
        canvases[2 * i][pl.ds(start, 32), :] += jnp.where(inside, turned, 0.0)
        canvases[2 * i + 1][pl.ds(start + 32, 32), :] += jnp.where(inside, 0.0, turned)

    def place(g, unused):
        for i in range(CAP):
            put(i % PAIRS, g * CAP + i, row_s[g, i] + OFF, col_s[g, i])
        return unused

    lax.fori_loop(0, NSKY, place, 0)

    def place_near(g, unused):
        for i in range(GROUP):
            at = g * GROUP + i
            real = at < count
            entry = jnp.where(real, listed[at], OFF * 512)
            put(i % PAIRS, jnp.where(real, OWN + at, SLOTS), entry >> 9, entry & 511)
        return unused

    lax.fori_loop(0, (count + GROUP - 1) // GROUP, place_near, 0)

    def pixels(observed, background, image):
        e = jnp.exp(-jnp.abs(image))
        soft = jnp.maximum(image, 0.0) + jnp.log1p(e)
        sig = jnp.where(image >= 0.0, 1.0, e) / (1.0 + e)
        return (observed / (background + soft) - 1.0) * sig

    def images(row, rows):
        left = iota((rows, 128), 1) < 64

        def planes(parity):
            out = []
            for h in range(PLANES):
                at = pl.ds(h * CROWS + OFF + row, rows)
                plane = canvases[parity][at, :]
                for i in range(1, PAIRS):
                    plane = plane + canvases[2 * i + parity][at, :]
                out.append(plane)
            return out

        upper, lower = planes(0), planes(1)
        out = []
        for q in range(4):
            before = jnp.zeros((rows, 128), F32) if q == 0 else upper[2 * q - 1]
            image = upper[2 * q] + jnp.where(left, before, upper[2 * q + 1])
            before = jnp.zeros((rows, 128), F32) if q == 0 else lower[2 * q - 1]
            out.append(image + pltpu.roll(lower[2 * q] + jnp.where(left, lower[2 * q + 1], before), 64, 1))
        return out

    def reach(row, rows, values):
        values = [v.astype(BF16).astype(F32) for v in values]
        turned = [pltpu.roll(v, 64, 1) for v in values]
        left = iota((rows, 128), 1) < 64
        for q in range(4):
            after = min(q + 1, 3)
            even, odd = pl.ds(2 * q * XROWS + row, rows), pl.ds((2 * q + 1) * XROWS + row, rows)
            xs[even, :] = values[q]
            xs[odd, :] = jnp.where(left, values[after], values[q])
            xt[even, :] = turned[q]
            xt[odd, :] = jnp.where(left, turned[q], turned[after])

    def edge(halo, row, real):
        values = []
        for q, image in enumerate(images(row, 32)):
            lanes = slice(q * 128, (q + 1) * 128)
            values.append(jnp.where(real, pixels(halo[:32, lanes], halo[32:, lanes], image), 0.0))
        reach(row, 32, values)

    edge(halo_up_ref, 0, tile > 0)
    edge(halo_down_ref, 288, tile < NSKY - 1)

    def block(i, unused):
        base = pl.multiple_of(i * 32, 32)
        values = []
        for q, image in enumerate(images(32 + base, 32)):
            lanes = slice(q * 128, (q + 1) * 128)
            r = pixels(obs_ref[pl.ds(base, 32), lanes], back_ref[pl.ds(base, 32), lanes], image)
            res_ref[pl.ds(base, 32), lanes] = r
            values.append(r)
        reach(32 + base, 32, values)
        return unused

    lax.fori_loop(0, 8, block, 0)

    def window(g, unused):
        for i in range(CAP):
            row, col = row_s[g, i], col_s[g, i]
            turn = col & 127
            start = (col >> 6) * XROWS + row
            inside = ((lane32 - turn) & 127) < 64
            seen = jnp.where(inside, xs[pl.ds(start, 32), :], xt[pl.ds(start + 32, 32), :])
            ss[pl.ds(g * CAP + i, 32, stride=SROWS), :] = pltpu.roll(seen, (128 - turn) & 127, 1)
        return unused

    lax.fori_loop(0, NSKY, window, 0)

    total = jnp.zeros((OWN, 192), F32)
    for c in range(CHUNKS):
        base = 2 * c * SROWS
        w = jnp.concatenate([ss[base:base + OWN, :], ss[base + SROWS:base + SROWS + OWN, :]], axis=1).astype(BF16)
        total = total + dot(w, b_ref[c], ((1,), (1,)))
    grad = total[:, 128:192] + total[:, 64:128] + total[:, :64]
    grad = jnp.concatenate([grad, grad], axis=1)
    for o in range(NSKY):
        acc[o * 16:(o + 1) * 16, :] = jnp.where(k_at < count_s[0, o], grad[o * 16:(o + 1) * 16], 0.0)
    left = iota((4, 128), 1) < 64
    for o in range(NSKY):
        for ref, at in ((keep_ref, o * 16 + core * 8), (give_ref, o * 16 + 8 - core * 8)):
            ref[o] = jnp.where(left, acc[pl.ds(at, 4), :], acc[pl.ds(at + 4, 4), :])


def owner_kernel(index_s, got_ref, out_ref, first, second, sums):
    core = lax.axis_index("epoch") % 2
    lane = iota((1, 128), 1)
    for t in range(NSKY):
        for r in range(4):
            for hot, k in ((first, r), (second, r + 4)):
                hot[t * 4 + r:t * 4 + r + 1, :] = jnp.where(lane == index_s[t, core * 8 + k], 1.0, 0.0).astype(F32)
    for t in range(NSKY):
        s = got_ref[t * 8]
        for z in range(1, 8):
            s = s + got_ref[t * 8 + z]
        sums[t * 4:(t + 1) * 4, :] = s
    x = sums[...]
    out = dot(x, first[...], ((0,), (0,)), HIGHEST)[:64] + dot(x, second[...], ((0,), (0,)), HIGHEST)[64:]
    out_ref[...] = out


SM = pl.BlockSpec(memory_space=pltpu.SMEM)
VM = pl.BlockSpec(memory_space=pltpu.VMEM)


def call_send(index, count, params_t, row, col):
    return pl.pallas_call(
        send_kernel,
        out_shape=jax.ShapeDtypeStruct((NSKY, 64, 128), BF16),
        in_specs=[SM, SM, VM, VM, VM],
        out_specs=VM,
        scratch_shapes=[pltpu.VMEM((256, 128), F32)],
        compiler_params=pltpu.CompilerParams(vmem_limit_bytes=8 << 20),
    )(index, count, params_t, row, col)


def call_basis(taps, basis):
    return pl.pallas_call(
        basis_kernel,
        out_shape=jax.ShapeDtypeStruct((CHUNKS, 192, 256), BF16),
        in_specs=[VM, VM],
        out_specs=VM,
        scratch_shapes=[
            pltpu.VMEM((8, 128), F32),
            pltpu.VMEM((33 * 64, 128), F32),
            pltpu.VMEM((33 * 64, 128), F32),
        ],
        compiler_params=pltpu.CompilerParams(vmem_limit_bytes=16 << 20),
        cost_estimate=pl.CostEstimate(flops=2 * 10 ** 9, bytes_accessed=2 << 20, transcendentals=0),
    )(taps, basis)


def call_sky(row, col, count, shaped, got, obs, back, halo_up, halo_down):
    return pl.pallas_call(
        sky_kernel,
        out_shape=(
            jax.ShapeDtypeStruct((TR, TW), F32),
            jax.ShapeDtypeStruct((NSKY, 4, 128), F32),
            jax.ShapeDtypeStruct((NSKY, 4, 128), F32),
        ),
        in_specs=[SM, SM, SM] + [VM] * 6,
        out_specs=(VM, VM, VM),
        scratch_shapes=[
            pltpu.VMEM((33 * SROWS, 128), F32),
            pltpu.VMEM((PLANES * XROWS, 128), F32),
            pltpu.VMEM((PLANES * XROWS, 128), F32),
            pltpu.VMEM((OWN, 128), F32),
            pltpu.VMEM((512, 128), F32),
            pltpu.VMEM((520, 128), F32),
            pltpu.VMEM((32, 128), jnp.int32),
            pltpu.SMEM((32, 128), jnp.int32),
            pltpu.SMEM((520,), jnp.int32),
            pltpu.SemaphoreType.DMA,
        ] + [pltpu.VMEM((PLANES * CROWS, 128), F32)] * (2 * PAIRS),
        compiler_params=pltpu.CompilerParams(vmem_limit_bytes=32 << 20),
        cost_estimate=pl.CostEstimate(flops=4 * 10 ** 9, bytes_accessed=4 << 20, transcendentals=0),
    )(row, col, count, shaped, got, obs, back, halo_up, halo_down)


def call_owner(index, got):
    return pl.pallas_call(
        owner_kernel,
        out_shape=jax.ShapeDtypeStruct((PS, 128), F32),
        in_specs=[SM, VM],
        out_specs=VM,
        scratch_shapes=[pltpu.VMEM((64, 128), F32)] * 3,
        compiler_params=pltpu.CompilerParams(vmem_limit_bytes=8 << 20),
    )(index, got)


def on_device(params, basis, psf_taps, send_index, tile_count, stamp_row, stamp_col, observed, background):
    n = NSKY
    index = send_index[0]
    row, col = stamp_row[0], stamp_col[0]
    obs, back = observed[0], background[0]
    sent = call_send(index, tile_count, params.T, row, col)
    got = lax.all_to_all(sent, "sky", split_axis=0, concat_axis=0, tiled=True)
    to_next = [(i, i + 1) for i in range(n - 1)]
    to_prev = [(i + 1, i) for i in range(n - 1)]
    halo_up = lax.ppermute(jnp.concatenate([obs[TR - 32:], back[TR - 32:]], axis=0), "sky", to_next)
    halo_down = lax.ppermute(jnp.concatenate([obs[:32], back[:32]], axis=0), "sky", to_prev)
    shaped = call_basis(psf_taps[0], basis)
    residual, keep, give = call_sky(row, col, tile_count, shaped, got, obs, back, halo_up, halo_down)
    swap = [(i, i ^ 1) for i in range(16)]
    mine = keep + lax.ppermute(give, "epoch", swap)
    spread = jnp.broadcast_to(mine[:, None], (n, 8, 4, 128)).reshape(128, 4, 128)
    groups = [[t * 16 + z * 2 + c for t in range(16) for z in range(8)] for c in range(2)]
    back_home = lax.all_to_all(
        spread, ("sky", "epoch"), split_axis=0, concat_axis=0, tiled=True, axis_index_groups=groups
    )
    part = call_owner(index, back_home)
    grad = part + lax.ppermute(part, "epoch", swap)
    return grad.T, residual[None]


def solution(mesh):
    in_specs = (
        P("sky", None),
        P(),
        P("epoch", None, None),
        P("sky", None, None),
        P("sky", None),
        P("sky", None, None),
        P("sky", None, None),
        P("epoch", "sky", None),
        P("epoch", "sky", None),
    )
    out_specs = (P("sky", None), P("epoch", "sky", None))
    return jax.shard_map(on_device, mesh=mesh, in_specs=in_specs, out_specs=out_specs, check_vma=False)
```

time: 96.5 us -> 79.1 us (0.82); the launches traced: 96.7 us -> 77.9 us
  Pallas kernels: 27.6 us -> 19.5 us
  starting transfers between devices: 21.5 us -> 16.9 us
  local copies, waits for them, and re-layouts: 9.56 us -> 7.06 us
  other arithmetic: 2.92 us -> 0.65 us
  blocking collectives: 32.5 us -> 31.2 us
    pallas_call x3 -> x4, Pallas kernels: 27.6 us -> 19.5 us  [the longest x1 13.6 us: call_sky(): pl.pallas_call(sky_kernel, out_shape=(jax.ShapeDtypeStruct((TR, TW), F32)...]
    ppermute x2 -> x0, starting transfers between devices: 5.31 us -> none  [the longest x1 4.02 us: on_device(): spots_up = lax.ppermute(spots, 'sky', to_next)]
    gather x1 -> x0, local copies, waits for them, and re-layouts: 1.88 us -> none  [on_device(): outgoing = params[spread]]
    slice x2 -> x0, local copies, waits for them, and re-layouts: 1.48 us -> none  [on_device(): jnp.roll(index, 1, 0)]
    all_to_all x1, blocking collectives: 32.5 us -> 31.2 us  [on_device(): lax.all_to_all(spread, ('sky', 'epoch'), split_axis=0, concat_axis=0, til...]
    all_to_all x1 -> x0, other arithmetic: 1.26 us -> none  [on_device(): lax.all_to_all(sent, ('sky', 'epoch'), split_axis=0, concat_axis=0, tiled...]
    unnamed x20 -> x30, local copies, waits for them, and re-layouts: 5.55 us -> 6.06 us
  transfers between devices with their start and end apart: 7 -> 5, of which waited for: 2 -> 3; matrix products, arithmetic and copies ran while one was open for 6% -> 1% of each run, Pallas kernels for 9% -> 4%
where the time goes in v2:
time: 79.1 us; the launch traced here: 77.9 us
  blocking collectives  31.2 us (39%)
  Pallas kernels  19.5 us (25%)
  starting transfers between devices  16.9 us (21%)
  local copies, waits for them, and re-layouts  7.06 us (9%)
  waiting for transfers between devices  1.83 us (2%)
  between operations  0.83 us (1%)
    all_to_all x1, blocking collectives, on_device(): lax.all_to_all(spread, ('sky', 'epoch'), split_axis=0, concat_axis=0, til...  31.2 us
    pallas_call x1, Pallas kernels, call_sky(): pl.pallas_call(sky_kernel, out_shape=(jax.ShapeDtypeStruct((TR, TW), F32)...  13.6 us
    all_to_all x1, starting transfers between devices, on_device(): got = lax.all_to_all(sent, 'sky', split_axis=0, concat_axis=0, tiled=True)  7.58 us
    unnamed x30, local copies, waits for them, and re-layouts  6.06 us
    ppermute x1, starting transfers between devices, on_device(): lax.ppermute(jnp.concatenate([obs[TR - 32:], back[TR - 32:]], axis=0), 's...  3.27 us
    pallas_call x1, Pallas kernels, call_basis(): pl.pallas_call(basis_kernel, out_shape=jax.ShapeDtypeStruct((CHUNKS, 192,...  3.05 us
    ppermute x1, starting transfers between devices, on_device(): mine = keep + lax.ppermute(give, 'epoch', swap)  2.76 us
    ppermute x1, starting transfers between devices, on_device(): grad = part + lax.ppermute(part, 'epoch', swap)  1.98 us
  transfers between devices with their start and end apart: 5, of which 3 were waited for; matrix products, arithmetic and copies ran while one was open for 1% of the time, Pallas kernels for 4%

profile of v2, /device:TPU:1, one launch (start us, length us, event | category | flops | bytes accessed | tf_op | source)
XLA Modules:
  0.0 77.9 jit_solution(16855037999374467311)
XLA Ops:
  0.6 0.0 copy-start.12
  0.6 0.0 copy-start
  0.7 0.7 copy-done
  1.3 0.0 copy-start.4
  1.3 0.7 copy-done.4
  2.1 0.0 copy-start.5
  2.1 0.7 copy-done.5
  2.8 0.0 copy-start.7
  2.8 0.7 copy-done.7
  3.5 0.0 copy-start.9
  3.5 0.7 copy-done.9
  4.1 0.0 copy-start.11
  4.1 1.7 %shard_map.105 = bf16[16,64,128]{2,1,0:T(8,128)(2,1)} custom-call(s32[16,16]{1,0:T(8,128)S(1)} %bitcast.19, s32[1,16]{1,0:T(1,128)S(1)} %copy-done.9, bf16[64,128]{1,0:T(8,128)(2,1)S(1)} %bitcast.23, s32[16,16]{1,0:T(8,128)S(1)} %bitcast.24, s32[16,16]{1,0:T(8,128)S(1)} %bitcast.26), custom_call_target="tpu_custom_call" | custom-call | tf_op jit(solution)/shard_map/pallas_call | solution.py:323
  5.8 7.6 %all-to-all-start = ((bf16[16,64,128]{2,1,0:T(8,128)(2,1)}), bf16[16,64,128]{2,1,0:T(8,128)(2,1)S(1)}, u32[]{:S(2)}, u32[]{:S(2)}) async-start(bf16[16,64,128]{2,1,0:T(8,128)(2,1)} %shard_map.105), calls=%async_computation | async-start | bytes 524288 | tf_op jit(solution)/shard_map/all_to_all | solution.py:393
  13.4 1.0 %slice_bitcast_fusion = (f32[32,512]{1,0:T(8,128)S(1)}, f32[32,512]{1,0:T(8,128)S(1)}, f32[32,512]{1,0:T(8,128)S(1)}, f32[32,512]{1,0:T(8,128)S(1)}) fusion(f32[1,256,512]{2,1,0:T(8,128)} %param.17, f32[1,256,512]{2,1,0:T(8,128)} %param.16), kind=kLoop, calls=%fused_computation.2 | loop fusion | bytes 524288 | tf_op jit(solution)/shard_map/slice | solution.py:397
  14.4 3.3 %collective-permute-start = (f32[64,512]{1,0:T(8,128)S(1)}, f32[64,512]{1,0:T(8,128)S(1)}, u32[]{:S(2)}, u32[]{:S(2)}) collective-permute-start(f32[64,512]{1,0:T(8,128)S(1)} %pad_maximum_fusion), channel_id=1, source_target_pairs={{0,16},{16,32},{32,48},{48,64},{64,80},{80,96},{96,112},{112,128},... | collective-permute-start | bytes 393224 | tf_op jit(solution)/shard_map/ppermute | solution.py:396
  17.7 1.3 %collective-permute-start.1 = (f32[64,512]{1,0:T(8,128)S(1)}, f32[64,512]{1,0:T(8,128)S(1)}, u32[]{:S(2)}, u32[]{:S(2)}) collective-permute-start(f32[64,512]{1,0:T(8,128)S(1)} %pad_maximum_fusion.1), channel_id=1, source_target_pairs={{16,0},{32,16},{48,32},{64,48},{80,64},{96,80},{112,96},{128,112},... | collective-permute-start | bytes 393224 | tf_op jit(solution)/shard_map/ppermute | solution.py:397
  19.0 0.0 copy-done.12
  19.0 0.0 copy-done.11
  19.0 0.0 copy-start.2
  19.0 0.0 copy-start.3
  19.0 0.0 copy-start.6
  19.0 0.0 copy-start.8
  19.1 0.0 copy-start.10
  19.1 3.1 %shard_map.104.b_ref = bf16[16,192,256]{2,1,0:T(8,128)(2,1)S(1)} custom-call(f32[2,51]{1,0:T(2,128)S(1)} %bitcast.28, bf16[64,4096]{1,0:T(8,128)(2,1)S(1)} %copy-done.11), custom_call_target="tpu_custom_call" | custom-call | flops 2000000000 | bytes 2097152 | tf_op jit(solution)/shard_map/pallas_call | solution.py:334
  22.1 0.0 copy-start.13
  22.1 1.2 %copy-done.13 = bf16[16,192,256]{2,1,0:T(8,128)(2,1)} copy-done((bf16[16,192,256]{2,1,0:T(8,128)(2,1)}, bf16[16,192,256]{2,1,0:T(8,128)(2,1)S(1)}, u32[]{:S(2)}) %copy-start.13) | copy-done | bytes 1572888
  23.3 0.0 collective-permute-done.halo_up_ref
  23.3 0.1 collective-permute-done.1.halo_down_ref
  23.4 0.0 all-to-all-done.got_ref
  23.4 0.0 copy-done.2
  23.4 0.0 copy-done.3
  23.4 0.0 copy-done.6
  23.4 0.0 copy-done.8
  23.4 0.0 copy-done.10
  23.4 0.0 copy-start.14
  23.4 1.4 %copy-done.14 = bf16[16,192,256]{2,1,0:T(8,128)(2,1)S(1)} copy-done((bf16[16,192,256]{2,1,0:T(8,128)(2,1)S(1)}, bf16[16,192,256]{2,1,0:T(8,128)(2,1)}, u32[]{:S(2)}) %copy-start.14) | copy-done | bytes 1572888
  24.8 0.0 copy-start.1
  24.8 13.6 %shard_map.106 = (f32[256,512]{1,0:T(8,128)}, f32[16,4,128]{2,1,0:T(4,128)S(1)}, f32[16,4,128]{2,1,0:T(4,128)S(1)}) custom-call(s32[16,16]{1,0:T(8,128)S(1)} %bitcast.25, s32[16,16]{1,0:T(8,128)S(1)} %bitcast.27, s32[1,16]{1,0:T(1,128)S(1)} %copy-done.10, bf16[16,192,256]{2,1,0:T(8,128)(2,1)S(1)} %copy-done.14, ...), custom_call_target="tpu_custom_call" | custom-call | flops 4000000000 | bytes 4194304 | tf_op jit(solution)/shard_map/pallas_call | solution.py:350
  38.5 2.8 %collective-permute-start.2 = (f32[16,4,128]{2,1,0:T(4,128)S(1)}, f32[16,4,128]{2,1,0:T(4,128)S(1)}, u32[]{:S(2)}, u32[]{:S(2)}) collective-permute-start(f32[16,4,128]{2,1,0:T(4,128)S(1)} %get-tuple-element.6), channel_id=1, source_target_pairs={{0,1},{1,0},{2,3},{3,2},{4,5},{5,4},{6,7},{7,6},{8,9},{9,8},{10,11... | collective-permute-start | bytes 98312 | tf_op jit(solution)/shard_map/ppermute | solution.py:401
  41.2 0.9 %collective-permute-done.2 = f32[16,4,128]{2,1,0:T(4,128)S(1)} collective-permute-done((f32[16,4,128]{2,1,0:T(4,128)S(1)}, f32[16,4,128]{2,1,0:T(4,128)S(1)}, u32[]{:S(2)}, u32[]{:S(2)}) %collective-permute-start.2) | collective-permute-done | bytes 32800 | tf_op jit(solution)/shard_map/ppermute | solution.py:401
  42.2 31.2 %all_to_all.10.got_ref = f32[128,4,128]{2,1,0:T(4,128)S(1)} all-to-all(f32[128,4,128]{2,1,0:T(4,128)S(1)} %bitcast.29), channel_id=1, replica_groups={{0,2,4,6,8,10,12,14,16,18,20,22,24,26,28,30,32,34,36,38,40,42,44,46,48,..., dimensions={0} | all-to-all | bytes 524288 | tf_op jit(solution)/shard_map/all_to_all | solution.py:404
  73.3 0.0 copy-done.1
  73.3 1.1 %shard_map.107 = f32[64,128]{1,0:T(8,128)S(1)} custom-call(s32[16,16]{1,0:T(8,128)S(1)} %bitcast.20, f32[128,4,128]{2,1,0:T(4,128)S(1)} %all_to_all.10.got_ref), custom_call_target="tpu_custom_call" | custom-call | tf_op jit(solution)/shard_map/pallas_call | solution.py:377
  74.4 2.0 %collective-permute-start.3 = (f32[64,128]{1,0:T(8,128)S(1)}, f32[64,128]{1,0:T(8,128)S(1)}, u32[]{:S(2)}, u32[]{:S(2)}) collective-permute-start(f32[64,128]{1,0:T(8,128)S(1)} %shard_map.107), channel_id=1, source_target_pairs={{0,1},{1,0},{2,3},{3,2},{4,5},{5,4},{6,7},{7,6},{8,9},{9,8},{10,11... | collective-permute-start | bytes 98312 | tf_op jit(solution)/shard_map/ppermute | solution.py:408
  76.4 0.9 %collective-permute-done.3 = f32[64,128]{1,0:T(8,128)S(1)} collective-permute-done((f32[64,128]{1,0:T(8,128)S(1)}, f32[64,128]{1,0:T(8,128)S(1)}, u32[]{:S(2)}, u32[]{:S(2)}) %collective-permute-start.3) | collective-permute-done | bytes 32800 | tf_op jit(solution)/shard_map/ppermute | solution.py:408
  77.3 0.6 add_bitcast_fusion
  (4 shorter events, 0.1 us)
Async XLA Ops:
  0.6 18.4 %copy-start.12 = (f32[1,2,51]{2,1,0:T(2,128)S(1)}, f32[1,2,51]{2,1,0:T(2,128)}, u32[]{:S(2)}) copy-start(f32[1,2,51]{2,1,0:T(2,128)} %param.11) | copy-start | bytes 1228
  0.6 0.7 copy-start
  1.3 0.7 copy-start.4
  2.1 0.7 copy-start.5
  2.8 0.7 copy-start.7
  3.5 0.7 copy-start.9
  4.1 14.9 %copy-start.11 = (bf16[64,4096]{1,0:T(8,128)(2,1)S(1)}, bf16[64,4096]{1,0:T(8,128)(2,1)}, u32[]{:S(2)}) copy-start(bf16[64,4096]{1,0:T(8,128)(2,1)} %basis_ref.1) | copy-start | bytes 1572868
  5.8 17.6 %all-to-all-start = ((bf16[16,64,128]{2,1,0:T(8,128)(2,1)}), bf16[16,64,128]{2,1,0:T(8,128)(2,1)S(1)}, u32[]{:S(2)}, u32[]{:S(2)}) async-start(bf16[16,64,128]{2,1,0:T(8,128)(2,1)} %shard_map.105), calls=%async_computation | async-start | bytes 524288 | tf_op jit(solution)/shard_map/all_to_all | solution.py:393
  14.4 8.9 %collective-permute-start = (f32[64,512]{1,0:T(8,128)S(1)}, f32[64,512]{1,0:T(8,128)S(1)}, u32[]{:S(2)}, u32[]{:S(2)}) collective-permute-start(f32[64,512]{1,0:T(8,128)S(1)} %pad_maximum_fusion), channel_id=1, source_target_pairs={{0,16},{16,32},{32,48},{48,64},{64,80},{80,96},{96,112},{112,128},... | collective-permute-start | bytes 393224 | tf_op jit(solution)/shard_map/ppermute | solution.py:396
  17.7 5.7 %collective-permute-start.1 = (f32[64,512]{1,0:T(8,128)S(1)}, f32[64,512]{1,0:T(8,128)S(1)}, u32[]{:S(2)}, u32[]{:S(2)}) collective-permute-start(f32[64,512]{1,0:T(8,128)S(1)} %pad_maximum_fusion.1), channel_id=1, source_target_pairs={{16,0},{32,16},{48,32},{64,48},{80,64},{96,80},{112,96},{128,112},... | collective-permute-start | bytes 393224 | tf_op jit(solution)/shard_map/ppermute | solution.py:397
  19.0 4.4 %copy-start.2 = (f32[1,256,512]{2,1,0:T(8,128)S(1)}, f32[1,256,512]{2,1,0:T(8,128)}, u32[]{:S(2)}) copy-start(f32[1,256,512]{2,1,0:T(8,128)} %param.16) | copy-start | bytes 1572868
  19.0 4.4 %copy-start.3 = (f32[1,256,512]{2,1,0:T(8,128)S(1)}, f32[1,256,512]{2,1,0:T(8,128)}, u32[]{:S(2)}) copy-start(f32[1,256,512]{2,1,0:T(8,128)} %param.17) | copy-start | bytes 1572868
  19.0 4.4 %copy-start.6 = (s32[1,16,16]{2,1,0:T(8,128)S(1)}, s32[1,16,16]{2,1,0:T(8,128)}, u32[]{:S(2)}) copy-start(s32[1,16,16]{2,1,0:T(8,128)} %param.14) | copy-start | bytes 3076
  19.0 4.4 %copy-start.8 = (s32[1,16,16]{2,1,0:T(8,128)S(1)}, s32[1,16,16]{2,1,0:T(8,128)}, u32[]{:S(2)}) copy-start(s32[1,16,16]{2,1,0:T(8,128)} %param.15) | copy-start | bytes 3076
  19.1 4.4 %copy-start.10 = (s32[1,16]{1,0:T(1,128)S(1)}, s32[1,16]{1,0:T(1,128)}, u32[]{:S(2)}) copy-start(s32[1,16]{1,0:T(1,128)} %count_s.3) | copy-start | bytes 196
  22.1 1.2 %copy-start.13 = (bf16[16,192,256]{2,1,0:T(8,128)(2,1)}, bf16[16,192,256]{2,1,0:T(8,128)(2,1)S(1)}, u32[]{:S(2)}) copy-start(bf16[16,192,256]{2,1,0:T(8,128)(2,1)S(1)} %shard_map.104.b_ref) | copy-start | bytes 4718596
  23.4 1.4 %copy-start.14 = (bf16[16,192,256]{2,1,0:T(8,128)(2,1)S(1)}, bf16[16,192,256]{2,1,0:T(8,128)(2,1)}, u32[]{:S(2)}) copy-start(bf16[16,192,256]{2,1,0:T(8,128)(2,1)} %copy-done.13) | copy-start | bytes 4718596
  24.8 48.5 %copy-start.1 = (s32[1,16,16]{2,1,0:T(8,128)S(1)}, s32[1,16,16]{2,1,0:T(8,128)}, u32[]{:S(2)}) copy-start(s32[1,16,16]{2,1,0:T(8,128)} %param.12) | copy-start | bytes 3076
  38.5 3.6 %collective-permute-start.2 = (f32[16,4,128]{2,1,0:T(4,128)S(1)}, f32[16,4,128]{2,1,0:T(4,128)S(1)}, u32[]{:S(2)}, u32[]{:S(2)}) collective-permute-start(f32[16,4,128]{2,1,0:T(4,128)S(1)} %get-tuple-element.6), channel_id=1, source_target_pairs={{0,1},{1,0},{2,3},{3,2},{4,5},{5,4},{6,7},{7,6},{8,9},{9,8},{10,11... | collective-permute-start | bytes 98312 | tf_op jit(solution)/shard_map/ppermute | solution.py:401
  74.4 2.8 %collective-permute-start.3 = (f32[64,128]{1,0:T(8,128)S(1)}, f32[64,128]{1,0:T(8,128)S(1)}, u32[]{:S(2)}, u32[]{:S(2)}) collective-permute-start(f32[64,128]{1,0:T(8,128)S(1)} %shard_map.107), channel_id=1, source_target_pairs={{0,1},{1,0},{2,3},{3,2},{4,5},{5,4},{6,7},{7,6},{8,9},{9,8},{10,11... | collective-permute-start | bytes 98312 | tf_op jit(solution)/shard_map/ppermute | solution.py:408

commit v3 on v2

--- a/solution.py
+++ b/solution.py
@@ -19,10 +19,10 @@
 CROWS = 448
 XROWS = 320
 PLANES = 8
-PAIRS = 1
-GROUP = 8
+PAIRS = 2
+GROUP = 16
 CHUNKS = 16
-BLOCK = 64
+BLOCK = 128
 DEAD = 128
 HIGHEST = lax.Precision.HIGHEST
 F32 = jnp.float32
@@ -73,7 +73,7 @@
     out_ref[NSKY - 1, 32:48, :] = none
 
 
-def basis_kernel(taps_ref, basis_ref, out_ref, taps_pad, xs, ts):
+def basis_kernel(taps_ref, basis_ref, out_hbm, taps_pad, xs, ts, out_ref, sems):
     taps_pad[...] = jnp.zeros((8, 128), F32)
     taps = taps_ref[...]
     taps_pad[0:2, 0:TAPS] = taps / jnp.sum(taps, axis=1, keepdims=True)
@@ -107,6 +107,7 @@
             both = jnp.where(lane < 64, made[:64, i * 128:(i + 1) * 128], made[64:, i * 128:(i + 1) * 128])
             both = both + pltpu.roll(both, 64, 1)
             ts[pl.ds(g * 8 + i, 32, stride=64), :] = jnp.where(lane[:32] < 64, both[:32], both[32:])
+    copies = []
     for m in range(4):
         x = jnp.concatenate([
             jnp.concatenate([ts[c * 128:c * 128 + 64, :], ts[c * 128 + 64:c * 128 + 128, :]], axis=1)
@@ -116,13 +117,22 @@
         for part, v in enumerate(split3(y)):
             for i in range(4):
                 out_ref[m * 4 + i, part * 64:(part + 1) * 64, :] = v[i * 64:(i + 1) * 64]
-
-
-def sky_kernel(row_s, col_s, count_s, b_ref, got_ref, obs_ref, back_ref, halo_up_ref, halo_down_ref,
-               res_ref, keep_ref, give_ref, ss, xs, xt, acc, near, packed, spots_v, spots_s, listed, sem, *canvases):
+        copies.append(pltpu.make_async_copy(out_ref.at[pl.ds(m * 4, 4)], out_hbm.at[pl.ds(m * 4, 4)], sems.at[m]))
+        copies[-1].start()
+    for copy in copies:
+        copy.wait()
+
+
+def sky_kernel(row_s, col_s, count_s, b_hbm, got_ref, obs_hbm, back_hbm, halo_up_ref, halo_down_ref,
+               res_hbm, keep_ref, give_ref, b_ref, obs_ref, back_ref, res_ref, sems, ss, xs, xt, acc, near, packed, spots_v, spots_s, listed, sem, *canvases):
     tile = lax.axis_index("sky")
     core = lax.axis_index("epoch") % 2
     lane32 = iota((32, 128), 1)
+    b_copy = pltpu.make_async_copy(b_hbm, b_ref, sems.at[0])
+    b_copy.start()
+    late = [pltpu.make_async_copy(obs_hbm, obs_ref, sems.at[1]), pltpu.make_async_copy(back_hbm, back_ref, sems.at[2])]
+    for each in late:
+        each.start()
 
     def spots_of(which, there):
         spots = got_ref[which, 48:64, :].astype(F32)
@@ -151,6 +161,7 @@
     for j in range(32):
         ss[j * SROWS + SLOTS:(j + 1) * SROWS, :] = jnp.zeros((SROWS - SLOTS, 128), F32)
     copy.wait()
+    b_copy.wait()
 
     span = PLANES * CROWS // CHUNKS
 
@@ -170,7 +181,7 @@
                 count = count + jnp.where(entry >= 0, 1, 0)
         return count
 
-    count = lax.fori_loop(0, CHUNKS, render, jnp.int32(0))
+    count = lax.fori_loop(0, CHUNKS, render, jnp.int32(0), unroll=4)
 
     def render_near(b, unused):
         base = pl.multiple_of(b * BLOCK, BLOCK)
@@ -196,7 +207,7 @@
             put(i % PAIRS, g * CAP + i, row_s[g, i] + OFF, col_s[g, i])
         return unused
 
-    lax.fori_loop(0, NSKY, place, 0)
+    lax.fori_loop(0, NSKY, place, 0, unroll=4)
 
     def place_near(g, unused):
         for i in range(GROUP):
@@ -207,6 +218,9 @@
         return unused
 
     lax.fori_loop(0, (count + GROUP - 1) // GROUP, place_near, 0)
+
+    for each in late:
+        each.wait()
 
     def pixels(observed, background, image):
         e = jnp.exp(-jnp.abs(image))
@@ -269,7 +283,9 @@
         reach(32 + base, 32, values)
         return unused
 
-    lax.fori_loop(0, 8, block, 0)
+    lax.fori_loop(0, 8, block, 0, unroll=8)
+    res_copy = pltpu.make_async_copy(res_ref, res_hbm, sems.at[3])
+    res_copy.start()
 
     def window(g, unused):
         for i in range(CAP):
@@ -281,7 +297,7 @@
             ss[pl.ds(g * CAP + i, 32, stride=SROWS), :] = pltpu.roll(seen, (128 - turn) & 127, 1)
         return unused
 
-    lax.fori_loop(0, NSKY, window, 0)
+    lax.fori_loop(0, NSKY, window, 0, unroll=4)
 
     total = jnp.zeros((OWN, 192), F32)
     for c in range(CHUNKS):
@@ -296,6 +312,7 @@
     for o in range(NSKY):
         for ref, at in ((keep_ref, o * 16 + core * 8), (give_ref, o * 16 + 8 - core * 8)):
             ref[o] = jnp.where(left, acc[pl.ds(at, 4), :], acc[pl.ds(at + 4, 4), :])
+    res_copy.wait()
 
 
 def owner_kernel(index_s, got_ref, out_ref, first, second, sums):
@@ -315,7 +332,9 @@
     out_ref[...] = out
 
 
+ROOMY = 62_100_000
 SM = pl.BlockSpec(memory_space=pltpu.SMEM)
+HB = pl.BlockSpec(memory_space=pltpu.HBM)
 VM = pl.BlockSpec(memory_space=pltpu.VMEM)
 
 
@@ -326,7 +345,8 @@
         in_specs=[SM, SM, VM, VM, VM],
         out_specs=VM,
         scratch_shapes=[pltpu.VMEM((256, 128), F32)],
-        compiler_params=pltpu.CompilerParams(vmem_limit_bytes=8 << 20),
+        compiler_params=pltpu.CompilerParams(vmem_limit_bytes=60 << 20),
+        cost_estimate=pl.CostEstimate(flops=8 * 10 ** 9, bytes_accessed=16 << 20, transcendentals=0),
     )(index, count, params_t, row, col)
 
 
@@ -335,14 +355,16 @@
         basis_kernel,
         out_shape=jax.ShapeDtypeStruct((CHUNKS, 192, 256), BF16),
         in_specs=[VM, VM],
-        out_specs=VM,
+        out_specs=HB,
         scratch_shapes=[
             pltpu.VMEM((8, 128), F32),
             pltpu.VMEM((33 * 64, 128), F32),
             pltpu.VMEM((33 * 64, 128), F32),
+            pltpu.VMEM((CHUNKS, 192, 256), BF16),
+            pltpu.SemaphoreType.DMA((4,)),
         ],
-        compiler_params=pltpu.CompilerParams(vmem_limit_bytes=16 << 20),
-        cost_estimate=pl.CostEstimate(flops=2 * 10 ** 9, bytes_accessed=2 << 20, transcendentals=0),
+        compiler_params=pltpu.CompilerParams(vmem_limit_bytes=ROOMY),
+        cost_estimate=pl.CostEstimate(flops=10 ** 5, bytes_accessed=1 << 10, transcendentals=0),
     )(taps, basis)
 
 
@@ -354,9 +376,14 @@
             jax.ShapeDtypeStruct((NSKY, 4, 128), F32),
             jax.ShapeDtypeStruct((NSKY, 4, 128), F32),
         ),
-        in_specs=[SM, SM, SM] + [VM] * 6,
-        out_specs=(VM, VM, VM),
+        in_specs=[SM, SM, SM, HB, VM, HB, HB, VM, VM],
+        out_specs=(HB, VM, VM),
         scratch_shapes=[
+            pltpu.VMEM((CHUNKS, 192, 256), BF16),
+            pltpu.VMEM((TR, TW), F32),
+            pltpu.VMEM((TR, TW), F32),
+            pltpu.VMEM((TR, TW), F32),
+            pltpu.SemaphoreType.DMA((4,)),
             pltpu.VMEM((33 * SROWS, 128), F32),
             pltpu.VMEM((PLANES * XROWS, 128), F32),
             pltpu.VMEM((PLANES * XROWS, 128), F32),
@@ -368,7 +395,7 @@
             pltpu.SMEM((520,), jnp.int32),
             pltpu.SemaphoreType.DMA,
         ] + [pltpu.VMEM((PLANES * CROWS, 128), F32)] * (2 * PAIRS),
-        compiler_params=pltpu.CompilerParams(vmem_limit_bytes=32 << 20),
+        compiler_params=pltpu.CompilerParams(vmem_limit_bytes=54_000_000),
         cost_estimate=pl.CostEstimate(flops=4 * 10 ** 9, bytes_accessed=4 << 20, transcendentals=0),
     )(row, col, count, shaped, got, obs, back, halo_up, halo_down)
 
@@ -389,12 +416,14 @@
     index = send_index[0]
     row, col = stamp_row[0], stamp_col[0]
     obs, back = observed[0], background[0]
+    low = jnp.concatenate([obs[TR - 32:], back[TR - 32:]], axis=0)
+    high = jnp.concatenate([obs[:32], back[:32]], axis=0)
     sent = call_send(index, tile_count, params.T, row, col)
     got = lax.all_to_all(sent, "sky", split_axis=0, concat_axis=0, tiled=True)
     to_next = [(i, i + 1) for i in range(n - 1)]
     to_prev = [(i + 1, i) for i in range(n - 1)]
-    halo_up = lax.ppermute(jnp.concatenate([obs[TR - 32:], back[TR - 32:]], axis=0), "sky", to_next)
-    halo_down = lax.ppermute(jnp.concatenate([obs[:32], back[:32]], axis=0), "sky", to_prev)
+    halo_up = lax.ppermute(low, "sky", to_next)
+    halo_down = lax.ppermute(high, "sky", to_prev)
     shaped = call_basis(psf_taps[0], basis)
     residual, keep, give = call_sky(row, col, tile_count, shaped, got, obs, back, halo_up, halo_down)
     swap = [(i, i ^ 1) for i in range(16)]

time: 79.1 us -> 68.5 us (0.87)
  local copies, waits for them, and re-layouts: 7.06 us -> 0.09 us
  Pallas kernels: 19.5 us -> 17.5 us
    unnamed x30 -> x12, local copies, waits for them, and re-layouts: 6.06 us -> 0.03 us
    pallas_call x1, Pallas kernels: 13.6 us -> 9.56 us  [call_sky(): pl.pallas_call(sky_kernel, out_shape=(jax.ShapeDtypeStruct((TR, TW), F32)...]
    pallas_call x1, Pallas kernels: 3.05 us -> 4.86 us  [call_basis(): pl.pallas_call(basis_kernel, out_shape=jax.ShapeDtypeStruct((CHUNKS, 192,...]
    slice x1, local copies, waits for them, and re-layouts: 0.96 us -> 0.02 us  [on_device(): high = jnp.concatenate([obs[:32], back[:32]], axis=0)]
  transfers between devices with their start and end apart: 5 -> 5, of which waited for: 3 -> 2; matrix products, arithmetic and copies ran while one was open for 1% -> 0% of each run, Pallas kernels for 4% -> 7%
where the time goes in v3:
time: 68.5 us; the launch traced here: 68 us
  blocking collectives  30.8 us (45%)
  Pallas kernels  17.5 us (26%)
  starting transfers between devices  16.4 us (24%)
  waiting for transfers between devices  1.73 us (3%)
  between operations  0.83 us (1%)
    all_to_all x1, blocking collectives, on_device(): lax.all_to_all(spread, ('sky', 'epoch'), split_axis=0, concat_axis=0, til...  30.8 us
    pallas_call x1, Pallas kernels, call_sky(): pl.pallas_call(sky_kernel, out_shape=(jax.ShapeDtypeStruct((TR, TW), F32)...  9.56 us
    all_to_all x1, starting transfers between devices, on_device(): got = lax.all_to_all(sent, 'sky', split_axis=0, concat_axis=0, tiled=True)  7.58 us
    pallas_call x1, Pallas kernels, call_basis(): pl.pallas_call(basis_kernel, out_shape=jax.ShapeDtypeStruct((CHUNKS, 192,...  4.86 us
    ppermute x1, starting transfers between devices, on_device(): halo_up = lax.ppermute(low, 'sky', to_next)  3.27 us
    ppermute x1, starting transfers between devices, on_device(): mine = keep + lax.ppermute(give, 'epoch', swap)  2.26 us
    ppermute x1, starting transfers between devices, on_device(): grad = part + lax.ppermute(part, 'epoch', swap)  1.98 us
    pallas_call x1, Pallas kernels, call_send(): pl.pallas_call(send_kernel, out_shape=jax.ShapeDtypeStruct((NSKY, 64, 128...  1.97 us
  transfers between devices with their start and end apart: 5, of which 2 were waited for; matrix products, arithmetic and copies ran while one was open for 0% of the time, Pallas kernels for 7%

profile of v3, /device:TPU:1, one launch (start us, length us, event | category | flops | bytes accessed | tf_op | source)
XLA Modules:
  0.0 68.0 jit_solution(2976430087822897574)
XLA Ops:
  0.6 0.0 copy-start
  0.6 0.0 copy-start.1
  0.7 2.0 %shard_map.105 = bf16[16,64,128]{2,1,0:T(8,128)(2,1)} custom-call(s32[16,16]{1,0:T(8,128)} %bitcast.21, s32[1,16]{1,0:T(1,128)} %count_s.3, bf16[64,128]{1,0:T(8,128)(2,1)} %bitcast.29, s32[16,16]{1,0:T(8,128)} %bitcast.23, s32[16,16]{1,0:T(8,128)} %bitcast.25), custom_call_target="tpu_custom_call" | custom-call | flops 8000000000 | bytes 16777216 | tf_op jit(solution)/shard_map/pallas_call | solution.py:342
  2.6 7.6 %all-to-all-start = ((bf16[16,64,128]{2,1,0:T(8,128)(2,1)}), bf16[16,64,128]{2,1,0:T(8,128)(2,1)S(1)}, u32[]{:S(2)}, u32[]{:S(2)}) async-start(bf16[16,64,128]{2,1,0:T(8,128)(2,1)} %shard_map.105), calls=%async_computation | async-start | bytes 524288 | tf_op jit(solution)/shard_map/all_to_all | solution.py:422
  10.2 0.0 copy-done
  10.2 0.0 copy-done.1
  10.2 0.0 copy-start.3
  10.2 0.0 copy-start.4
  10.3 0.0 copy-start.5
  10.3 3.3 %collective-permute-start = (f32[64,512]{1,0:T(8,128)S(1)}, f32[64,512]{1,0:T(8,128)S(1)}, u32[]{:S(2)}, u32[]{:S(2)}) collective-permute-start(f32[64,512]{1,0:T(8,128)S(1)} %pad_maximum_fusion), channel_id=1, source_target_pairs={{0,16},{16,32},{32,48},{48,64},{64,80},{80,96},{96,112},{112,128},... | collective-permute-start | bytes 393224 | tf_op jit(solution)/shard_map/ppermute | solution.py:425
  13.6 1.3 %collective-permute-start.1 = (f32[64,512]{1,0:T(8,128)S(1)}, f32[64,512]{1,0:T(8,128)S(1)}, u32[]{:S(2)}, u32[]{:S(2)}) collective-permute-start(f32[64,512]{1,0:T(8,128)S(1)} %pad_maximum_fusion.1), channel_id=1, source_target_pairs={{16,0},{32,16},{48,32},{64,48},{80,64},{96,80},{112,96},{128,112},... | collective-permute-start | bytes 393224 | tf_op jit(solution)/shard_map/ppermute | solution.py:426
  14.9 4.9 %shard_map.104.b_hbm = bf16[16,192,256]{2,1,0:T(8,128)(2,1)} custom-call(f32[2,51]{1,0:T(2,128)} %bitcast.28, bf16[64,4096]{1,0:T(8,128)(2,1)} %basis_ref.1), custom_call_target="tpu_custom_call" | custom-call | flops 100000 | bytes 1024 | tf_op jit(solution)/shard_map/pallas_call | solution.py:354
  19.8 0.0 collective-permute-done.halo_up_ref
  19.8 0.0 collective-permute-done.1.halo_down_ref
  19.8 0.0 all-to-all-done.got_ref
  19.8 0.0 copy-done.3
  19.8 0.0 copy-done.4
  19.8 0.0 copy-done.5
  19.8 0.0 copy-start.2
  19.9 9.6 %shard_map.106 = (f32[256,512]{1,0:T(8,128)}, f32[16,4,128]{2,1,0:T(4,128)S(1)}, f32[16,4,128]{2,1,0:T(4,128)S(1)}) custom-call(s32[16,16]{1,0:T(8,128)S(1)} %bitcast.24, s32[16,16]{1,0:T(8,128)S(1)} %bitcast.26, s32[1,16]{1,0:T(1,128)S(1)} %copy-done.5, bf16[16,192,256]{2,1,0:T(8,128)(2,1)} %shard_map.104.b_hbm, ...), custom_call_target="tpu_custom_call" | custom-call | flops 4000000000 | bytes 4194304 | tf_op jit(solution)/shard_map/pallas_call | solution.py:372
  29.4 2.3 %collective-permute-start.2 = (f32[16,4,128]{2,1,0:T(4,128)S(1)}, f32[16,4,128]{2,1,0:T(4,128)S(1)}, u32[]{:S(2)}, u32[]{:S(2)}) collective-permute-start(f32[16,4,128]{2,1,0:T(4,128)S(1)} %get-tuple-element.6), channel_id=1, source_target_pairs={{0,1},{1,0},{2,3},{3,2},{4,5},{5,4},{6,7},{7,6},{8,9},{9,8},{10,11... | collective-permute-start | bytes 98312 | tf_op jit(solution)/shard_map/ppermute | solution.py:430
  31.7 0.9 %collective-permute-done.2 = f32[16,4,128]{2,1,0:T(4,128)S(1)} collective-permute-done((f32[16,4,128]{2,1,0:T(4,128)S(1)}, f32[16,4,128]{2,1,0:T(4,128)S(1)}, u32[]{:S(2)}, u32[]{:S(2)}) %collective-permute-start.2) | collective-permute-done | bytes 32800 | tf_op jit(solution)/shard_map/ppermute | solution.py:430
  32.6 30.8 %all_to_all.10.got_ref = f32[128,4,128]{2,1,0:T(4,128)S(1)} all-to-all(f32[128,4,128]{2,1,0:T(4,128)S(1)} %bitcast.27), channel_id=1, replica_groups={{0,2,4,6,8,10,12,14,16,18,20,22,24,26,28,30,32,34,36,38,40,42,44,46,48,..., dimensions={0} | all-to-all | bytes 524288 | tf_op jit(solution)/shard_map/all_to_all | solution.py:433
  63.4 0.0 copy-done.2
  63.4 1.1 %shard_map.107 = f32[64,128]{1,0:T(8,128)S(1)} custom-call(s32[16,16]{1,0:T(8,128)S(1)} %bitcast.22, f32[128,4,128]{2,1,0:T(4,128)S(1)} %all_to_all.10.got_ref), custom_call_target="tpu_custom_call" | custom-call | tf_op jit(solution)/shard_map/pallas_call | solution.py:404
  64.5 2.0 %collective-permute-start.3 = (f32[64,128]{1,0:T(8,128)S(1)}, f32[64,128]{1,0:T(8,128)S(1)}, u32[]{:S(2)}, u32[]{:S(2)}) collective-permute-start(f32[64,128]{1,0:T(8,128)S(1)} %shard_map.107), channel_id=1, source_target_pairs={{0,1},{1,0},{2,3},{3,2},{4,5},{5,4},{6,7},{7,6},{8,9},{9,8},{10,11... | collective-permute-start | bytes 98312 | tf_op jit(solution)/shard_map/ppermute | solution.py:437
  66.5 0.9 %collective-permute-done.3 = f32[64,128]{1,0:T(8,128)S(1)} collective-permute-done((f32[64,128]{1,0:T(8,128)S(1)}, f32[64,128]{1,0:T(8,128)S(1)}, u32[]{:S(2)}, u32[]{:S(2)}) %collective-permute-start.3) | collective-permute-done | bytes 32800 | tf_op jit(solution)/shard_map/ppermute | solution.py:437
  67.4 0.6 add_bitcast_fusion
  (5 shorter events, 0.1 us)
Async XLA Ops:
  0.6 9.6 %copy-start = (f32[1,256,512]{2,1,0:T(8,128)S(1)}, f32[1,256,512]{2,1,0:T(8,128)}, u32[]{:S(2)}) copy-start(f32[1,256,512]{2,1,0:T(8,128)} %param.16) | copy-start | bytes 1572868
  0.6 9.6 %copy-start.1 = (f32[1,256,512]{2,1,0:T(8,128)S(1)}, f32[1,256,512]{2,1,0:T(8,128)}, u32[]{:S(2)}) copy-start(f32[1,256,512]{2,1,0:T(8,128)} %param.17) | copy-start | bytes 1572868
  2.6 17.2 %all-to-all-start = ((bf16[16,64,128]{2,1,0:T(8,128)(2,1)}), bf16[16,64,128]{2,1,0:T(8,128)(2,1)S(1)}, u32[]{:S(2)}, u32[]{:S(2)}) async-start(bf16[16,64,128]{2,1,0:T(8,128)(2,1)} %shard_map.105), calls=%async_computation | async-start | bytes 524288 | tf_op jit(solution)/shard_map/all_to_all | solution.py:422
  10.2 9.6 %copy-start.3 = (s32[1,16,16]{2,1,0:T(8,128)S(1)}, s32[1,16,16]{2,1,0:T(8,128)}, u32[]{:S(2)}) copy-start(s32[1,16,16]{2,1,0:T(8,128)} %param.14) | copy-start | bytes 3076
  10.2 9.6 %copy-start.4 = (s32[1,16,16]{2,1,0:T(8,128)S(1)}, s32[1,16,16]{2,1,0:T(8,128)}, u32[]{:S(2)}) copy-start(s32[1,16,16]{2,1,0:T(8,128)} %param.15) | copy-start | bytes 3076
  10.3 9.6 %copy-start.5 = (s32[1,16]{1,0:T(1,128)S(1)}, s32[1,16]{1,0:T(1,128)}, u32[]{:S(2)}) copy-start(s32[1,16]{1,0:T(1,128)} %count_s.3) | copy-start | bytes 196
  10.3 9.5 %collective-permute-start = (f32[64,512]{1,0:T(8,128)S(1)}, f32[64,512]{1,0:T(8,128)S(1)}, u32[]{:S(2)}, u32[]{:S(2)}) collective-permute-start(f32[64,512]{1,0:T(8,128)S(1)} %pad_maximum_fusion), channel_id=1, source_target_pairs={{0,16},{16,32},{32,48},{48,64},{64,80},{80,96},{96,112},{112,128},... | collective-permute-start | bytes 393224 | tf_op jit(solution)/shard_map/ppermute | solution.py:425
  13.6 6.2 %collective-permute-start.1 = (f32[64,512]{1,0:T(8,128)S(1)}, f32[64,512]{1,0:T(8,128)S(1)}, u32[]{:S(2)}, u32[]{:S(2)}) collective-permute-start(f32[64,512]{1,0:T(8,128)S(1)} %pad_maximum_fusion.1), channel_id=1, source_target_pairs={{16,0},{32,16},{48,32},{64,48},{80,64},{96,80},{112,96},{128,112},... | collective-permute-start | bytes 393224 | tf_op jit(solution)/shard_map/ppermute | solution.py:426
  19.8 43.6 %copy-start.2 = (s32[1,16,16]{2,1,0:T(8,128)S(1)}, s32[1,16,16]{2,1,0:T(8,128)}, u32[]{:S(2)}) copy-start(s32[1,16,16]{2,1,0:T(8,128)} %param.12) | copy-start | bytes 3076
  29.4 3.1 %collective-permute-start.2 = (f32[16,4,128]{2,1,0:T(4,128)S(1)}, f32[16,4,128]{2,1,0:T(4,128)S(1)}, u32[]{:S(2)}, u32[]{:S(2)}) collective-permute-start(f32[16,4,128]{2,1,0:T(4,128)S(1)} %get-tuple-element.6), channel_id=1, source_target_pairs={{0,1},{1,0},{2,3},{3,2},{4,5},{5,4},{6,7},{7,6},{8,9},{9,8},{10,11... | collective-permute-start | bytes 98312 | tf_op jit(solution)/shard_map/ppermute | solution.py:430
  64.5 2.8 %collective-permute-start.3 = (f32[64,128]{1,0:T(8,128)S(1)}, f32[64,128]{1,0:T(8,128)S(1)}, u32[]{:S(2)}, u32[]{:S(2)}) collective-permute-start(f32[64,128]{1,0:T(8,128)S(1)} %shard_map.107), channel_id=1, source_target_pairs={{0,1},{1,0},{2,3},{3,2},{4,5},{5,4},{6,7},{7,6},{8,9},{9,8},{10,11... | collective-permute-start | bytes 98312 | tf_op jit(solution)/shard_map/ppermute | solution.py:437

commit v4 on v3

--- a/solution.py
+++ b/solution.py
@@ -23,6 +23,7 @@
 GROUP = 16
 CHUNKS = 16
 BLOCK = 128
+STEP = 72
 DEAD = 128
 HIGHEST = lax.Precision.HIGHEST
 F32 = jnp.float32
@@ -45,7 +46,14 @@
     return lax.broadcasted_iota(jnp.int32, shape, axis)
 
 
-def send_kernel(index_s, count_s, params_ref, row_ref, col_ref, out_ref, hot):
+def send_kernel(index_s, count_s, params_ref, row_ref, col_ref, obs_hbm, back_hbm, out_ref, first_ref, second_ref, hot, sems):
+    even = lax.axis_index("sky") % 2 == 0
+    copies = []
+    for to, at in ((first_ref, jnp.where(even, TR - 32, 0)), (second_ref, jnp.where(even, 0, TR - 32))):
+        for i, image in enumerate((obs_hbm, back_hbm)):
+            rows = pl.ds(pl.multiple_of(at, 32), 32)
+            copies.append(pltpu.make_async_copy(image.at[rows, :], to.at[pl.ds(32 * i, 32), :], sems.at[len(copies)]))
+            copies[-1].start()
     lane = iota((1, 128), 1)
     for t in range(NSKY):
         for k in range(CAP):
@@ -71,9 +79,11 @@
         out_ref[t, 48:64, :] = spots
     out_ref[0, 0:16, :] = none
     out_ref[NSKY - 1, 32:48, :] = none
-
-
-def basis_kernel(taps_ref, basis_ref, out_hbm, taps_pad, xs, ts, out_ref, sems):
+    for copy in copies:
+        copy.wait()
+
+
+def convolve(taps_ref, basis_ref, out_ref, taps_pad, xs, ts, beside):
     taps_pad[...] = jnp.zeros((8, 128), F32)
     taps = taps_ref[...]
     taps_pad[0:2, 0:TAPS] = taps / jnp.sum(taps, axis=1, keepdims=True)
@@ -83,54 +93,46 @@
     even = pltpu.roll(pltpu.roll(row_taps, 128 - HALF, 1), 0, 1, stride=2, stride_axis=0)
     odd = pltpu.roll(even, 1, 1)
     row_k = jnp.where(lane[:32] < 64, even, pltpu.roll(odd, 64, 1))
-    parts = [x.astype(F32) for x in split3(row_k)] + [jnp.zeros((32, 128), F32)]
-    row_parts = jnp.concatenate(parts, axis=0).T.astype(BF16)
+    rh, rm, rl = [x.astype(F32) for x in split3(row_k)]
+    none = jnp.zeros((64, 128), F32)
+    row_parts = jnp.concatenate([rl, rm, rh, rm, rh, rh, none], axis=0).T.astype(BF16)[:, :192]
 
     col_taps = jnp.broadcast_to(taps_pad[1:2, :], (64, 128))
     col_k = pltpu.roll(pltpu.roll(col_taps, 128 - HALF, 1), 0, 1, stride=1, stride_axis=0)
-    left = jnp.where(lane < 64, col_k, 0.0)
-    right = jnp.where(lane < 64, 0.0, pltpu.roll(col_k, 64, 1))
-    none = jnp.zeros((64, 128), F32)
-    col_k = jnp.concatenate([
-        jnp.concatenate([left, none], axis=1), jnp.concatenate([right, none], axis=1),
-        jnp.concatenate([none, left], axis=1), jnp.concatenate([none, right], axis=1)], axis=0)
+    col_k = jnp.concatenate([jnp.where(lane < 64, col_k, 0.0), jnp.where(lane < 64, 0.0, pltpu.roll(col_k, 64, 1))], axis=0)
     ch, cm, cl = split3(col_k)
-    col_parts = jnp.concatenate([ch, cl, cm, ch, cm, ch], axis=0)
-
-    for j in range(32):
-        xs[j * 64:(j + 1) * 64, :] = basis_ref[:, j * 128:(j + 1) * 128].astype(F32)
+    col_parts = jnp.concatenate([
+        jnp.concatenate([ch, cm], axis=1), jnp.concatenate([cl, jnp.zeros((128, 128), BF16)], axis=1)], axis=0)
+
+    for m in range(4):
+        x = jnp.concatenate([basis_ref[:, j * 128:(j + 1) * 128] for j in range(m * 8, m * 8 + 8)], axis=0)
+        made = dot(jnp.concatenate([x, x], axis=1), col_parts, ((1,), (0,)))
+        made = made[:, :128] + made[:, 128:]
+        for i in range(8):
+            xs[(m * 8 + i) * STEP:(m * 8 + i) * STEP + 64, :] = made[i * 64:(i + 1) * 64]
+
     for g in range(8):
-        images = [xs[pl.ds(g * 8 + i, 32, stride=64), :].astype(BF16) for i in range(8)]
-        wide = jnp.concatenate(images, axis=1)
-        made = dot(row_parts, jnp.concatenate([wide, wide, wide, wide], axis=0), ((1,), (0,)))
+        beside(g)
+        wide = jnp.concatenate([xs[pl.ds(g * 8 + i, 32, stride=STEP), :] for i in range(8)], axis=1)
+        wh, wm, wl = split3(wide)
+        made = dot(row_parts, jnp.concatenate([wh, wm, wl, wh, wm, wh], axis=0), ((1,), (0,)))
         for i in range(8):
             both = jnp.where(lane < 64, made[:64, i * 128:(i + 1) * 128], made[64:, i * 128:(i + 1) * 128])
             both = both + pltpu.roll(both, 64, 1)
-            ts[pl.ds(g * 8 + i, 32, stride=64), :] = jnp.where(lane[:32] < 64, both[:32], both[32:])
-    copies = []
-    for m in range(4):
-        x = jnp.concatenate([
-            jnp.concatenate([ts[c * 128:c * 128 + 64, :], ts[c * 128 + 64:c * 128 + 128, :]], axis=1)
-            for c in range(m * 4, m * 4 + 4)], axis=0)
-        xh, xm, xl = split3(x)
-        y = dot(jnp.concatenate([xl, xh, xm, xm, xh, xh], axis=1), col_parts, ((1,), (0,)))
+            ts[pl.ds(g * 8 + i, 32, stride=STEP), :] = jnp.where(lane[:32] < 64, both[:32], both[32:])
+
+    for c in range(CHUNKS):
+        y = jnp.concatenate([ts[pl.ds(2 * c * STEP, 64), :], ts[pl.ds((2 * c + 1) * STEP, 64), :]], axis=1)
         for part, v in enumerate(split3(y)):
-            for i in range(4):
-                out_ref[m * 4 + i, part * 64:(part + 1) * 64, :] = v[i * 64:(i + 1) * 64]
-        copies.append(pltpu.make_async_copy(out_ref.at[pl.ds(m * 4, 4)], out_hbm.at[pl.ds(m * 4, 4)], sems.at[m]))
-        copies[-1].start()
-    for copy in copies:
-        copy.wait()
-
-
-def sky_kernel(row_s, col_s, count_s, b_hbm, got_ref, obs_hbm, back_hbm, halo_up_ref, halo_down_ref,
-               res_hbm, keep_ref, give_ref, b_ref, obs_ref, back_ref, res_ref, sems, ss, xs, xt, acc, near, packed, spots_v, spots_s, listed, sem, *canvases):
+            out_ref[c, part * 64:(part + 1) * 64, :] = v
+
+
+def sky_kernel(row_s, col_s, count_s, taps_ref, basis_ref, got_ref, obs_hbm, back_hbm, first_ref, second_ref,
+               res_hbm, keep_ref, give_ref, taps_pad, bx, bt, b_ref, obs_ref, back_ref, res_ref, sems, ss, xs, xt, acc, near, packed, spots_v, spots_s, listed, sem, *canvases):
     tile = lax.axis_index("sky")
     core = lax.axis_index("epoch") % 2
     lane32 = iota((32, 128), 1)
-    b_copy = pltpu.make_async_copy(b_hbm, b_ref, sems.at[0])
-    b_copy.start()
-    late = [pltpu.make_async_copy(obs_hbm, obs_ref, sems.at[1]), pltpu.make_async_copy(back_hbm, back_ref, sems.at[2])]
+    late = [pltpu.make_async_copy(obs_hbm, obs_ref, sems.at[0]), pltpu.make_async_copy(back_hbm, back_ref, sems.at[1])]
     for each in late:
         each.start()
 
@@ -161,27 +163,36 @@
     for j in range(32):
         ss[j * SROWS + SLOTS:(j + 1) * SROWS, :] = jnp.zeros((SROWS - SLOTS, 128), F32)
     copy.wait()
-    b_copy.wait()
-
-    span = PLANES * CROWS // CHUNKS
-
-    def render(c, count):
+
+    span = PLANES * CROWS // 8
+    counts = [tile * 0]
+
+    def beside(g):
+        for canvas in canvases:
+            canvas[g * span:(g + 1) * span, :] = jnp.zeros((span, 128), F32)
+        count = counts[0]
+        for o in (2 * g, 2 * g + 1):
+            for which in range(2):
+                for k in range(CAP):
+                    entry = spots_s[which * 16 + o, k]
+                    listed[count] = entry
+                    at = o * 32 + which * 16 + k
+                    packed[pl.ds(count, 1), :] = near[at:at + 1, :]
+                    count = count + jnp.where(entry >= 0, 1, 0)
+        counts[0] = count
+
+    convolve(taps_ref, basis_ref, b_ref, taps_pad, bx, bt, beside)
+    count = counts[0]
+
+    def render(c, unused):
         made = dot(mine, b_ref[c], ((1,), (0,)))
         made = made.astype(BF16).astype(F32)
         base = pl.multiple_of(c * (2 * SROWS), 8)
         ss[pl.ds(base, OWN), :] = made[:, :128]
         ss[pl.ds(base + SROWS, OWN), :] = made[:, 128:]
-        for canvas in canvases:
-            canvas[pl.ds(pl.multiple_of(c * span, 8), span), :] = jnp.zeros((span, 128), F32)
-        for which in range(2):
-            for k in range(CAP):
-                entry = spots_s[which * 16 + c, k]
-                listed[count] = entry
-                packed[pl.ds(count, 1), :] = near[pl.ds(c * 32 + which * 16 + k, 1), :]
-                count = count + jnp.where(entry >= 0, 1, 0)
-        return count
-
-    count = lax.fori_loop(0, CHUNKS, render, jnp.int32(0), unroll=4)
+        return unused
+
+    lax.fori_loop(0, CHUNKS, render, 0, unroll=4)
 
     def render_near(b, unused):
         base = pl.multiple_of(b * BLOCK, BLOCK)
@@ -262,15 +273,18 @@
             xt[even, :] = turned[q]
             xt[odd, :] = jnp.where(left, turned[q], turned[after])
 
-    def edge(halo, row, real):
+    def edge(from_first, row, real):
         values = []
         for q, image in enumerate(images(row, 32)):
             lanes = slice(q * 128, (q + 1) * 128)
-            values.append(jnp.where(real, pixels(halo[:32, lanes], halo[32:, lanes], image), 0.0))
+            observed = jnp.where(from_first, first_ref[:32, lanes], second_ref[:32, lanes])
+            background = jnp.where(from_first, first_ref[32:, lanes], second_ref[32:, lanes])
+            values.append(jnp.where(real, pixels(observed, background, image), 0.0))
         reach(row, 32, values)
 
-    edge(halo_up_ref, 0, tile > 0)
-    edge(halo_down_ref, 288, tile < NSKY - 1)
+    even = tile % 2 == 0
+    edge(jnp.logical_not(even), 0, tile > 0)
+    edge(even, 288, tile < NSKY - 1)
 
     def block(i, unused):
         base = pl.multiple_of(i * 32, 32)
@@ -284,7 +298,7 @@
         return unused
 
     lax.fori_loop(0, 8, block, 0, unroll=8)
-    res_copy = pltpu.make_async_copy(res_ref, res_hbm, sems.at[3])
+    res_copy = pltpu.make_async_copy(res_ref, res_hbm, sems.at[2])
     res_copy.start()
 
     def window(g, unused):
@@ -332,43 +346,27 @@
     out_ref[...] = out
 
 
-ROOMY = 62_100_000
 SM = pl.BlockSpec(memory_space=pltpu.SMEM)
 HB = pl.BlockSpec(memory_space=pltpu.HBM)
 VM = pl.BlockSpec(memory_space=pltpu.VMEM)
 
 
-def call_send(index, count, params_t, row, col):
+def call_send(index, count, params_t, row, col, obs, back):
     return pl.pallas_call(
         send_kernel,
-        out_shape=jax.ShapeDtypeStruct((NSKY, 64, 128), BF16),
-        in_specs=[SM, SM, VM, VM, VM],
-        out_specs=VM,
-        scratch_shapes=[pltpu.VMEM((256, 128), F32)],
+        out_shape=(
+            jax.ShapeDtypeStruct((NSKY, 64, 128), BF16),
+            jax.ShapeDtypeStruct((64, TW), F32),
+            jax.ShapeDtypeStruct((64, TW), F32),
+        ),
+        in_specs=[SM, SM, VM, VM, VM, HB, HB],
+        out_specs=(VM, VM, VM),
+        scratch_shapes=[pltpu.VMEM((256, 128), F32), pltpu.SemaphoreType.DMA((4,))],
         compiler_params=pltpu.CompilerParams(vmem_limit_bytes=60 << 20),
-        cost_estimate=pl.CostEstimate(flops=8 * 10 ** 9, bytes_accessed=16 << 20, transcendentals=0),
-    )(index, count, params_t, row, col)
-
-
-def call_basis(taps, basis):
-    return pl.pallas_call(
-        basis_kernel,
-        out_shape=jax.ShapeDtypeStruct((CHUNKS, 192, 256), BF16),
-        in_specs=[VM, VM],
-        out_specs=HB,
-        scratch_shapes=[
-            pltpu.VMEM((8, 128), F32),
-            pltpu.VMEM((33 * 64, 128), F32),
-            pltpu.VMEM((33 * 64, 128), F32),
-            pltpu.VMEM((CHUNKS, 192, 256), BF16),
-            pltpu.SemaphoreType.DMA((4,)),
-        ],
-        compiler_params=pltpu.CompilerParams(vmem_limit_bytes=ROOMY),
-        cost_estimate=pl.CostEstimate(flops=10 ** 5, bytes_accessed=1 << 10, transcendentals=0),
-    )(taps, basis)
-
-
-def call_sky(row, col, count, shaped, got, obs, back, halo_up, halo_down):
+    )(index, count, params_t, row, col, obs, back)
+
+
+def call_sky(row, col, count, taps, basis, got, obs, back, first, second):
     return pl.pallas_call(
         sky_kernel,
         out_shape=(
@@ -376,14 +374,17 @@
             jax.ShapeDtypeStruct((NSKY, 4, 128), F32),
             jax.ShapeDtypeStruct((NSKY, 4, 128), F32),
         ),
-        in_specs=[SM, SM, SM, HB, VM, HB, HB, VM, VM],
+        in_specs=[SM, SM, SM, VM, VM, VM, HB, HB, VM, VM],
         out_specs=(HB, VM, VM),
         scratch_shapes=[
+            pltpu.VMEM((8, 128), F32),
+            pltpu.VMEM((33 * STEP, 128), F32),
+            pltpu.VMEM((33 * STEP, 128), F32),
             pltpu.VMEM((CHUNKS, 192, 256), BF16),
             pltpu.VMEM((TR, TW), F32),
             pltpu.VMEM((TR, TW), F32),
             pltpu.VMEM((TR, TW), F32),
-            pltpu.SemaphoreType.DMA((4,)),
+            pltpu.SemaphoreType.DMA((3,)),
             pltpu.VMEM((33 * SROWS, 128), F32),
             pltpu.VMEM((PLANES * XROWS, 128), F32),
             pltpu.VMEM((PLANES * XROWS, 128), F32),
@@ -397,7 +398,7 @@
         ] + [pltpu.VMEM((PLANES * CROWS, 128), F32)] * (2 * PAIRS),
         compiler_params=pltpu.CompilerParams(vmem_limit_bytes=54_000_000),
         cost_estimate=pl.CostEstimate(flops=4 * 10 ** 9, bytes_accessed=4 << 20, transcendentals=0),
-    )(row, col, count, shaped, got, obs, back, halo_up, halo_down)
+    )(row, col, count, taps, basis, got, obs, back, first, second)
 
 
 def call_owner(index, got):
@@ -416,16 +417,11 @@
     index = send_index[0]
     row, col = stamp_row[0], stamp_col[0]
     obs, back = observed[0], background[0]
-    low = jnp.concatenate([obs[TR - 32:], back[TR - 32:]], axis=0)
-    high = jnp.concatenate([obs[:32], back[:32]], axis=0)
-    sent = call_send(index, tile_count, params.T, row, col)
+    sent, first, second = call_send(index, tile_count, params.T, row, col, obs, back)
     got = lax.all_to_all(sent, "sky", split_axis=0, concat_axis=0, tiled=True)
-    to_next = [(i, i + 1) for i in range(n - 1)]
-    to_prev = [(i + 1, i) for i in range(n - 1)]
-    halo_up = lax.ppermute(low, "sky", to_next)
-    halo_down = lax.ppermute(high, "sky", to_prev)
-    shaped = call_basis(psf_taps[0], basis)
-    residual, keep, give = call_sky(row, col, tile_count, shaped, got, obs, back, halo_up, halo_down)
+    first = lax.ppermute(first, "sky", [(i, i ^ 1) for i in range(n)])
+    second = lax.ppermute(second, "sky", [(i, ((i + 1) ^ 1) - 1) for i in range(1, n - 1)])
+    residual, keep, give = call_sky(row, col, tile_count, psf_taps[0], basis, got, obs, back, first, second)
     swap = [(i, i ^ 1) for i in range(16)]
     mine = keep + lax.ppermute(give, "epoch", swap)
     spread = jnp.broadcast_to(mine[:, None], (n, 8, 4, 128)).reshape(128, 4, 128)

time: 68.5 us -> 69.3 us (1.012)
  waiting for transfers between devices: 1.73 us -> 7.05 us
  starting transfers between devices: 16.4 us -> 13.9 us
  Pallas kernels: 17.5 us -> 15.1 us
  blocking collectives: 30.8 us -> 31.5 us
    pallas_call x2 -> x1, Pallas kernels: 6.82 us -> 2.83 us  [call_send(): pl.pallas_call(send_kernel, out_shape=(jax.ShapeDtypeStruct((NSKY, 64, 12...]
    ppermute x2, waiting for transfers between devices: 0.01 us -> 3.4 us  [the longest x1 3.39 us: on_device(): first = lax.ppermute(first, 'sky', [(i, i ^ 1) for i in range(n)])]
    ppermute x2, starting transfers between devices: 4.56 us -> 2.15 us  [the longest x1 1.37 us: on_device(): first = lax.ppermute(first, 'sky', [(i, i ^ 1) for i in range(n)])]
    all_to_all x1, waiting for transfers between devices: 0.01 us -> 1.94 us  [on_device(): got = lax.all_to_all(sent, 'sky', split_axis=0, concat_axis=0, tiled=True)]
    pallas_call x1, Pallas kernels: 9.56 us -> 11.2 us  [call_sky(): pl.pallas_call(sky_kernel, out_shape=(jax.ShapeDtypeStruct((TR, TW), F32)...]
  transfers between devices with their start and end apart: 5 -> 5, of which waited for: 2 -> 4; matrix products, arithmetic and copies ran while one was open for 0% -> 0% of each run, Pallas kernels for 7% -> 0%
where the time goes in v4:
time: 69.3 us; the launch traced here: 69 us
  blocking collectives  31.5 us (45%)
  Pallas kernels  15.1 us (22%)
  starting transfers between devices  13.9 us (20%)
  waiting for transfers between devices  7.05 us (10%)
  between operations  0.77 us (1%)
    all_to_all x1, blocking collectives, on_device(): lax.all_to_all(spread, ('sky', 'epoch'), split_axis=0, concat_axis=0, til...  31.5 us
    pallas_call x1, Pallas kernels, call_sky(): pl.pallas_call(sky_kernel, out_shape=(jax.ShapeDtypeStruct((TR, TW), F32)...  11.2 us
    all_to_all x1, starting transfers between devices, on_device(): got = lax.all_to_all(sent, 'sky', split_axis=0, concat_axis=0, tiled=True)  7.73 us
    ppermute x1, waiting for transfers between devices, on_device(): first = lax.ppermute(first, 'sky', [(i, i ^ 1) for i in range(n)])  3.39 us
    pallas_call x1, Pallas kernels, call_send(): pl.pallas_call(send_kernel, out_shape=(jax.ShapeDtypeStruct((NSKY, 64, 12...  2.83 us
    ppermute x1, starting transfers between devices, on_device(): mine = keep + lax.ppermute(give, 'epoch', swap)  2.06 us
    ppermute x1, starting transfers between devices, on_device(): grad = part + lax.ppermute(part, 'epoch', swap)  1.98 us
    all_to_all x1, waiting for transfers between devices, on_device(): got = lax.all_to_all(sent, 'sky', split_axis=0, concat_axis=0, tiled=True)  1.94 us
  transfers between devices with their start and end apart: 5, of which 4 were waited for; matrix products, arithmetic and copies ran while one was open for 0% of the time, Pallas kernels for 0%

profile of v4, /device:TPU:1, one launch (start us, length us, event | category | flops | bytes accessed | tf_op | source)
XLA Modules:
  0.0 69.0 jit_solution(13566638388312853838)
XLA Ops:
  0.6 0.0 copy-start.1
  0.6 0.0 copy-start.3
  0.7 0.0 copy-start.4
  0.7 0.0 copy-start.6
  0.7 2.8 %shard_map.104 = (bf16[16,64,128]{2,1,0:T(8,128)(2,1)}, f32[64,512]{1,0:T(8,128)}, f32[64,512]{1,0:T(8,128)}) custom-call(s32[16,16]{1,0:T(8,128)} %bitcast.15, s32[1,16]{1,0:T(1,128)} %count_s.3, bf16[64,128]{1,0:T(8,128)(2,1)} %bitcast.23, s32[16,16]{1,0:T(8,128)} %bitcast.17, s32[16,16]{1,0:T(8,128)} %bitcast.19, f32[256,512]{1,0:T(8,128)} %bitcast.11, ...), custom_call_target="tpu_custom_call" | custom-call | tf_op jit(solution)/shard_map/pallas_call | solution.py:355
  3.5 0.0 copy-start
  3.5 7.7 %all-to-all-start = ((bf16[16,64,128]{2,1,0:T(8,128)(2,1)}), bf16[16,64,128]{2,1,0:T(8,128)(2,1)S(1)}, u32[]{:S(2)}, u32[]{:S(2)}) async-start(bf16[16,64,128]{2,1,0:T(8,128)(2,1)} %get-tuple-element.8), calls=%async_computation | async-start | bytes 524288 | tf_op jit(solution)/shard_map/all_to_all | solution.py:421
  11.3 1.4 %collective-permute-start = (f32[64,512]{1,0:T(8,128)}, f32[64,512]{1,0:T(8,128)S(1)}, u32[]{:S(2)}, u32[]{:S(2)}) collective-permute-start(f32[64,512]{1,0:T(8,128)} %get-tuple-element.9), channel_id=1, source_target_pairs={{0,16},{16,0},{32,48},{48,32},{64,80},{80,64},{96,112},{112,96},{1... | collective-permute-start | bytes 393224 | tf_op jit(solution)/shard_map/ppermute | solution.py:422
  12.6 0.0 copy-start.5
  12.6 0.0 copy-start.7
  12.6 0.8 %collective-permute-start.1 = (f32[64,512]{1,0:T(8,128)}, f32[64,512]{1,0:T(8,128)S(1)}, u32[]{:S(2)}, u32[]{:S(2)}) collective-permute-start(f32[64,512]{1,0:T(8,128)} %get-tuple-element.10), channel_id=1, source_target_pairs={{16,32},{32,16},{48,64},{64,48},{80,96},{96,80},{112,128},{128,112... | collective-permute-start | bytes 393224 | tf_op jit(solution)/shard_map/ppermute | solution.py:423
  13.4 3.4 %collective-permute-done.first_ref = f32[64,512]{1,0:T(8,128)S(1)} collective-permute-done((f32[64,512]{1,0:T(8,128)}, f32[64,512]{1,0:T(8,128)S(1)}, u32[]{:S(2)}, u32[]{:S(2)}) %collective-permute-start) | collective-permute-done | bytes 131104 | tf_op jit(solution)/shard_map/ppermute | solution.py:422
  16.8 0.0 collective-permute-done.1.second_ref
  16.8 1.9 %all-to-all-done.got_ref = bf16[16,64,128]{2,1,0:T(8,128)(2,1)S(1)} async-done(((bf16[16,64,128]{2,1,0:T(8,128)(2,1)}), bf16[16,64,128]{2,1,0:T(8,128)(2,1)S(1)}, u32[]{:S(2)}, u32[]{:S(2)}) %all-to-all-start) | async-done | bytes 262176 | tf_op jit(solution)/shard_map/all_to_all | solution.py:421
  18.8 0.0 copy-done.1
  18.8 0.0 copy-done.3
  18.8 0.0 copy-done.4
  18.8 0.0 copy-done.6
  18.8 0.0 copy-done
  18.8 0.0 copy-done.5
  18.8 0.0 copy-done.7
  18.8 11.2 %shard_map.105 = (f32[256,512]{1,0:T(8,128)}, f32[16,4,128]{2,1,0:T(4,128)S(1)}, f32[16,4,128]{2,1,0:T(4,128)S(1)}) custom-call(s32[16,16]{1,0:T(8,128)S(1)} %bitcast.18, s32[16,16]{1,0:T(8,128)S(1)} %bitcast.20, s32[1,16]{1,0:T(1,128)S(1)} %copy-done.5, f32[2,51]{1,0:T(2,128)S(1)} %bitcast.21, bf16[64,4096]{1,0:T(8,128)(2,1)S(1)} %copy-done.6, ...), custom_call_target="tpu_custom_call" | custom-call | flops 4000000000 | bytes 4194304 | tf_op jit(solution)/shard_map/pallas_call | solution.py:370
  30.0 2.1 %collective-permute-start.2 = (f32[16,4,128]{2,1,0:T(4,128)S(1)}, f32[16,4,128]{2,1,0:T(4,128)S(1)}, u32[]{:S(2)}, u32[]{:S(2)}) collective-permute-start(f32[16,4,128]{2,1,0:T(4,128)S(1)} %get-tuple-element.12), channel_id=1, source_target_pairs={{0,1},{1,0},{2,3},{3,2},{4,5},{5,4},{6,7},{7,6},{8,9},{9,8},{10,11... | collective-permute-start | bytes 98312 | tf_op jit(solution)/shard_map/ppermute | solution.py:426
  32.1 0.9 %collective-permute-done.2 = f32[16,4,128]{2,1,0:T(4,128)S(1)} collective-permute-done((f32[16,4,128]{2,1,0:T(4,128)S(1)}, f32[16,4,128]{2,1,0:T(4,128)S(1)}, u32[]{:S(2)}, u32[]{:S(2)}) %collective-permute-start.2) | collective-permute-done | bytes 32800 | tf_op jit(solution)/shard_map/ppermute | solution.py:426
  33.0 0.0 copy-start.2
  33.0 31.5 %all_to_all.10.got_ref = f32[128,4,128]{2,1,0:T(4,128)S(1)} all-to-all(f32[128,4,128]{2,1,0:T(4,128)S(1)} %bitcast.22), channel_id=1, replica_groups={{0,2,4,6,8,10,12,14,16,18,20,22,24,26,28,30,32,34,36,38,40,42,44,46,48,..., dimensions={0} | all-to-all | bytes 524288 | tf_op jit(solution)/shard_map/all_to_all | solution.py:429
  64.5 0.0 copy-done.2
  64.5 1.1 %shard_map.106 = f32[64,128]{1,0:T(8,128)S(1)} custom-call(s32[16,16]{1,0:T(8,128)S(1)} %bitcast.16, f32[128,4,128]{2,1,0:T(4,128)S(1)} %all_to_all.10.got_ref), custom_call_target="tpu_custom_call" | custom-call | tf_op jit(solution)/shard_map/pallas_call | solution.py:405
  65.5 2.0 %collective-permute-start.3 = (f32[64,128]{1,0:T(8,128)S(1)}, f32[64,128]{1,0:T(8,128)S(1)}, u32[]{:S(2)}, u32[]{:S(2)}) collective-permute-start(f32[64,128]{1,0:T(8,128)S(1)} %shard_map.106), channel_id=1, source_target_pairs={{0,1},{1,0},{2,3},{3,2},{4,5},{5,4},{6,7},{7,6},{8,9},{9,8},{10,11... | collective-permute-start | bytes 98312 | tf_op jit(solution)/shard_map/ppermute | solution.py:433
  67.5 0.9 %collective-permute-done.3 = f32[64,128]{1,0:T(8,128)S(1)} collective-permute-done((f32[64,128]{1,0:T(8,128)S(1)}, f32[64,128]{1,0:T(8,128)S(1)}, u32[]{:S(2)}, u32[]{:S(2)}) %collective-permute-start.3) | collective-permute-done | bytes 32800 | tf_op jit(solution)/shard_map/ppermute | solution.py:433
  68.4 0.6 add_bitcast_fusion
  (2 shorter events, 0.0 us)
Async XLA Ops:
  0.6 18.1 %copy-start.1 = (f32[1,256,512]{2,1,0:T(8,128)S(1)}, f32[1,256,512]{2,1,0:T(8,128)}, u32[]{:S(2)}) copy-start(f32[1,256,512]{2,1,0:T(8,128)} %param.17) | copy-start | bytes 1572868
  0.6 18.1 %copy-start.3 = (s32[1,16,16]{2,1,0:T(8,128)S(1)}, s32[1,16,16]{2,1,0:T(8,128)}, u32[]{:S(2)}) copy-start(s32[1,16,16]{2,1,0:T(8,128)} %param.14) | copy-start | bytes 3076
  0.7 18.1 %copy-start.4 = (s32[1,16,16]{2,1,0:T(8,128)S(1)}, s32[1,16,16]{2,1,0:T(8,128)}, u32[]{:S(2)}) copy-start(s32[1,16,16]{2,1,0:T(8,128)} %param.15) | copy-start | bytes 3076
  0.7 18.1 %copy-start.6 = (bf16[64,4096]{1,0:T(8,128)(2,1)S(1)}, bf16[64,4096]{1,0:T(8,128)(2,1)}, u32[]{:S(2)}) copy-start(bf16[64,4096]{1,0:T(8,128)(2,1)} %basis_ref.1) | copy-start | bytes 1572868
  3.5 15.3 %copy-start = (f32[1,256,512]{2,1,0:T(8,128)S(1)}, f32[1,256,512]{2,1,0:T(8,128)}, u32[]{:S(2)}) copy-start(f32[1,256,512]{2,1,0:T(8,128)} %param.16) | copy-start | bytes 1572868
  3.5 15.2 %all-to-all-start = ((bf16[16,64,128]{2,1,0:T(8,128)(2,1)}), bf16[16,64,128]{2,1,0:T(8,128)(2,1)S(1)}, u32[]{:S(2)}, u32[]{:S(2)}) async-start(bf16[16,64,128]{2,1,0:T(8,128)(2,1)} %get-tuple-element.8), calls=%async_computation | async-start | bytes 524288 | tf_op jit(solution)/shard_map/all_to_all | solution.py:421
  11.3 5.6 %collective-permute-start = (f32[64,512]{1,0:T(8,128)}, f32[64,512]{1,0:T(8,128)S(1)}, u32[]{:S(2)}, u32[]{:S(2)}) collective-permute-start(f32[64,512]{1,0:T(8,128)} %get-tuple-element.9), channel_id=1, source_target_pairs={{0,16},{16,0},{32,48},{48,32},{64,80},{80,64},{96,112},{112,96},{1... | collective-permute-start | bytes 393224 | tf_op jit(solution)/shard_map/ppermute | solution.py:422
  12.6 6.2 %copy-start.5 = (s32[1,16]{1,0:T(1,128)S(1)}, s32[1,16]{1,0:T(1,128)}, u32[]{:S(2)}) copy-start(s32[1,16]{1,0:T(1,128)} %count_s.3) | copy-start | bytes 196
  12.6 6.2 %copy-start.7 = (f32[1,2,51]{2,1,0:T(2,128)S(1)}, f32[1,2,51]{2,1,0:T(2,128)}, u32[]{:S(2)}) copy-start(f32[1,2,51]{2,1,0:T(2,128)} %param.11) | copy-start | bytes 1228
  12.6 4.2 %collective-permute-start.1 = (f32[64,512]{1,0:T(8,128)}, f32[64,512]{1,0:T(8,128)S(1)}, u32[]{:S(2)}, u32[]{:S(2)}) collective-permute-start(f32[64,512]{1,0:T(8,128)} %get-tuple-element.10), channel_id=1, source_target_pairs={{16,32},{32,16},{48,64},{64,48},{80,96},{96,80},{112,128},{128,112... | collective-permute-start | bytes 393224 | tf_op jit(solution)/shard_map/ppermute | solution.py:423
  30.0 2.9 %collective-permute-start.2 = (f32[16,4,128]{2,1,0:T(4,128)S(1)}, f32[16,4,128]{2,1,0:T(4,128)S(1)}, u32[]{:S(2)}, u32[]{:S(2)}) collective-permute-start(f32[16,4,128]{2,1,0:T(4,128)S(1)} %get-tuple-element.12), channel_id=1, source_target_pairs={{0,1},{1,0},{2,3},{3,2},{4,5},{5,4},{6,7},{7,6},{8,9},{9,8},{10,11... | collective-permute-start | bytes 98312 | tf_op jit(solution)/shard_map/ppermute | solution.py:426
  33.0 31.5 %copy-start.2 = (s32[1,16,16]{2,1,0:T(8,128)S(1)}, s32[1,16,16]{2,1,0:T(8,128)}, u32[]{:S(2)}) copy-start(s32[1,16,16]{2,1,0:T(8,128)} %param.12) | copy-start | bytes 3076
  65.5 2.8 %collective-permute-start.3 = (f32[64,128]{1,0:T(8,128)S(1)}, f32[64,128]{1,0:T(8,128)S(1)}, u32[]{:S(2)}, u32[]{:S(2)}) collective-permute-start(f32[64,128]{1,0:T(8,128)S(1)} %shard_map.106), channel_id=1, source_target_pairs={{0,1},{1,0},{2,3},{3,2},{4,5},{5,4},{6,7},{7,6},{8,9},{9,8},{10,11... | collective-permute-start | bytes 98312 | tf_op jit(solution)/shard_map/ppermute | solution.py:433

commit v5 on v3

--- a/solution.py
+++ b/solution.py
@@ -23,6 +23,7 @@
 GROUP = 16
 CHUNKS = 16
 BLOCK = 128
+STEP = 72
 DEAD = 128
 HIGHEST = lax.Precision.HIGHEST
 F32 = jnp.float32
@@ -83,67 +84,69 @@
     even = pltpu.roll(pltpu.roll(row_taps, 128 - HALF, 1), 0, 1, stride=2, stride_axis=0)
     odd = pltpu.roll(even, 1, 1)
     row_k = jnp.where(lane[:32] < 64, even, pltpu.roll(odd, 64, 1))
-    parts = [x.astype(F32) for x in split3(row_k)] + [jnp.zeros((32, 128), F32)]
-    row_parts = jnp.concatenate(parts, axis=0).T.astype(BF16)
+    rh, rm, rl = [x.astype(F32) for x in split3(row_k)]
+    none = jnp.zeros((64, 128), F32)
+    row_parts = jnp.concatenate([rl, rm, rh, rm, rh, rh, none], axis=0).T.astype(BF16)[:, :192]
 
     col_taps = jnp.broadcast_to(taps_pad[1:2, :], (64, 128))
     col_k = pltpu.roll(pltpu.roll(col_taps, 128 - HALF, 1), 0, 1, stride=1, stride_axis=0)
-    left = jnp.where(lane < 64, col_k, 0.0)
-    right = jnp.where(lane < 64, 0.0, pltpu.roll(col_k, 64, 1))
-    none = jnp.zeros((64, 128), F32)
-    col_k = jnp.concatenate([
-        jnp.concatenate([left, none], axis=1), jnp.concatenate([right, none], axis=1),
-        jnp.concatenate([none, left], axis=1), jnp.concatenate([none, right], axis=1)], axis=0)
+    col_k = jnp.concatenate([jnp.where(lane < 64, col_k, 0.0), jnp.where(lane < 64, 0.0, pltpu.roll(col_k, 64, 1))], axis=0)
     ch, cm, cl = split3(col_k)
-    col_parts = jnp.concatenate([ch, cl, cm, ch, cm, ch], axis=0)
-
-    for j in range(32):
-        xs[j * 64:(j + 1) * 64, :] = basis_ref[:, j * 128:(j + 1) * 128].astype(F32)
+    col_parts = jnp.concatenate([
+        jnp.concatenate([ch, cm], axis=1), jnp.concatenate([cl, jnp.zeros((128, 128), BF16)], axis=1)], axis=0)
+
+    for m in range(4):
+        x = jnp.concatenate([basis_ref[:, j * 128:(j + 1) * 128] for j in range(m * 8, m * 8 + 8)], axis=0)
+        made = dot(jnp.concatenate([x, x], axis=1), col_parts, ((1,), (0,)))
+        made = made[:, :128] + made[:, 128:]
+        for i in range(8):
+            xs[(m * 8 + i) * STEP:(m * 8 + i) * STEP + 64, :] = made[i * 64:(i + 1) * 64]
+
     for g in range(8):
-        images = [xs[pl.ds(g * 8 + i, 32, stride=64), :].astype(BF16) for i in range(8)]
-        wide = jnp.concatenate(images, axis=1)
-        made = dot(row_parts, jnp.concatenate([wide, wide, wide, wide], axis=0), ((1,), (0,)))
+        wide = jnp.concatenate([xs[pl.ds(g * 8 + i, 32, stride=STEP), :] for i in range(8)], axis=1)
+        wh, wm, wl = split3(wide)
+        made = dot(row_parts, jnp.concatenate([wh, wm, wl, wh, wm, wh], axis=0), ((1,), (0,)))
         for i in range(8):
             both = jnp.where(lane < 64, made[:64, i * 128:(i + 1) * 128], made[64:, i * 128:(i + 1) * 128])
             both = both + pltpu.roll(both, 64, 1)
-            ts[pl.ds(g * 8 + i, 32, stride=64), :] = jnp.where(lane[:32] < 64, both[:32], both[32:])
+            ts[pl.ds(g * 8 + i, 32, stride=STEP), :] = jnp.where(lane[:32] < 64, both[:32], both[32:])
+
     copies = []
-    for m in range(4):
-        x = jnp.concatenate([
-            jnp.concatenate([ts[c * 128:c * 128 + 64, :], ts[c * 128 + 64:c * 128 + 128, :]], axis=1)
-            for c in range(m * 4, m * 4 + 4)], axis=0)
-        xh, xm, xl = split3(x)
-        y = dot(jnp.concatenate([xl, xh, xm, xm, xh, xh], axis=1), col_parts, ((1,), (0,)))
+    for c in range(CHUNKS):
+        y = jnp.concatenate([ts[pl.ds(2 * c * STEP, 64), :], ts[pl.ds((2 * c + 1) * STEP, 64), :]], axis=1)
         for part, v in enumerate(split3(y)):
-            for i in range(4):
-                out_ref[m * 4 + i, part * 64:(part + 1) * 64, :] = v[i * 64:(i + 1) * 64]
-        copies.append(pltpu.make_async_copy(out_ref.at[pl.ds(m * 4, 4)], out_hbm.at[pl.ds(m * 4, 4)], sems.at[m]))
-        copies[-1].start()
+            out_ref[c, part * 64:(part + 1) * 64, :] = v
+        if c % 4 == 3:
+            some = pl.ds(c - 3, 4)
+            copies.append(pltpu.make_async_copy(out_ref.at[some], out_hbm.at[some], sems.at[c // 4]))
+            copies[-1].start()
     for copy in copies:
         copy.wait()
 
 
-def sky_kernel(row_s, col_s, count_s, b_hbm, got_ref, obs_hbm, back_hbm, halo_up_ref, halo_down_ref,
+def sky_kernel(row_s, col_s, count_s, b_hbm, got_ref, obs_hbm, back_hbm, first_ref, second_ref,
                res_hbm, keep_ref, give_ref, b_ref, obs_ref, back_ref, res_ref, sems, ss, xs, xt, acc, near, packed, spots_v, spots_s, listed, sem, *canvases):
     tile = lax.axis_index("sky")
     core = lax.axis_index("epoch") % 2
     lane32 = iota((32, 128), 1)
-    b_copy = pltpu.make_async_copy(b_hbm, b_ref, sems.at[0])
+    b_copy = pltpu.make_async_copy(b_hbm, b_ref, sems.at[3])
     b_copy.start()
-    late = [pltpu.make_async_copy(obs_hbm, obs_ref, sems.at[1]), pltpu.make_async_copy(back_hbm, back_ref, sems.at[2])]
+    late = [pltpu.make_async_copy(obs_hbm, obs_ref, sems.at[0]), pltpu.make_async_copy(back_hbm, back_ref, sems.at[1])]
     for each in late:
         each.start()
 
-    def spots_of(which, there):
-        spots = got_ref[which, 48:64, :].astype(F32)
+    slot_at = iota((NSKY, 128), 0) * 32 + iota((NSKY, 128), 1)
+
+    def spots_of(peer, slot, shift, inside):
+        spots = got_ref[peer, 48:64, :].astype(F32)
         row = spots.astype(jnp.int32)
         col = 2 * pltpu.roll(spots, 112, 1).astype(jnp.int32) + pltpu.roll(spots, 96, 1).astype(jnp.int32)
-        return row, col
-
-    row, col = spots_of(jnp.maximum(tile - 1, 0), None)
-    spots_v[0:16, :] = jnp.where((row > 192) & (tile > 0), (row - TR + OFF) * 512 + col, -1)
-    row, col = spots_of(jnp.minimum(tile + 1, NSKY - 1), None)
-    spots_v[16:32, :] = jnp.where((row < 64) & (tile < NSKY - 1), (row + TR + OFF) * 512 + col, -1)
+        return jnp.where(inside(row), (slot * 512 + row + shift) * 512 + col, -1)
+
+    spots_v[0:16, :] = spots_of(
+        jnp.maximum(tile - 1, 0), slot_at, OFF - TR, lambda row: (row > 192) & (tile > 0))
+    spots_v[16:32, :] = spots_of(
+        jnp.minimum(tile + 1, NSKY - 1), slot_at + 16, OFF + TR, lambda row: (row < 64) & (tile < NSKY - 1))
     copy = pltpu.make_async_copy(spots_v, spots_s, sem)
     copy.start()
 
@@ -177,11 +180,19 @@
             for k in range(CAP):
                 entry = spots_s[which * 16 + c, k]
                 listed[count] = entry
-                packed[pl.ds(count, 1), :] = near[pl.ds(c * 32 + which * 16 + k, 1), :]
                 count = count + jnp.where(entry >= 0, 1, 0)
         return count
 
     count = lax.fori_loop(0, CHUNKS, render, jnp.int32(0), unroll=4)
+
+    def pack(g, unused):
+        for i in range(GROUP):
+            at = g * GROUP + i
+            entry = jnp.where(at < count, listed[at], 0)
+            packed[pl.ds(at, 1), :] = near[pl.ds(entry >> 18, 1), :]
+        return unused
+
+    lax.fori_loop(0, (count + GROUP - 1) // GROUP, pack, 0)
 
     def render_near(b, unused):
         base = pl.multiple_of(b * BLOCK, BLOCK)
@@ -214,7 +225,7 @@
             at = g * GROUP + i
             real = at < count
             entry = jnp.where(real, listed[at], OFF * 512)
-            put(i % PAIRS, jnp.where(real, OWN + at, SLOTS), entry >> 9, entry & 511)
+            put(i % PAIRS, jnp.where(real, OWN + at, SLOTS), (entry >> 9) & 511, entry & 511)
         return unused
 
     lax.fori_loop(0, (count + GROUP - 1) // GROUP, place_near, 0)
@@ -262,15 +273,18 @@
             xt[even, :] = turned[q]
             xt[odd, :] = jnp.where(left, turned[q], turned[after])
 
-    def edge(halo, row, real):
+    def edge(from_first, row, real):
         values = []
         for q, image in enumerate(images(row, 32)):
             lanes = slice(q * 128, (q + 1) * 128)
-            values.append(jnp.where(real, pixels(halo[:32, lanes], halo[32:, lanes], image), 0.0))
+            observed = jnp.where(from_first, first_ref[:32, lanes], second_ref[:32, lanes])
+            background = jnp.where(from_first, first_ref[32:, lanes], second_ref[32:, lanes])
+            values.append(jnp.where(real, pixels(observed, background, image), 0.0))
         reach(row, 32, values)
 
-    edge(halo_up_ref, 0, tile > 0)
-    edge(halo_down_ref, 288, tile < NSKY - 1)
+    even = (tile & 1) == 0
+    edge(jnp.logical_not(even), 0, tile > 0)
+    edge(even, 288, tile < NSKY - 1)
 
     def block(i, unused):
         base = pl.multiple_of(i * 32, 32)
@@ -284,7 +298,7 @@
         return unused
 
     lax.fori_loop(0, 8, block, 0, unroll=8)
-    res_copy = pltpu.make_async_copy(res_ref, res_hbm, sems.at[3])
+    res_copy = pltpu.make_async_copy(res_ref, res_hbm, sems.at[2])
     res_copy.start()
 
     def window(g, unused):
@@ -332,7 +346,6 @@
     out_ref[...] = out
 
 
-ROOMY = 62_100_000
 SM = pl.BlockSpec(memory_space=pltpu.SMEM)
 HB = pl.BlockSpec(memory_space=pltpu.HBM)
 VM = pl.BlockSpec(memory_space=pltpu.VMEM)
@@ -358,17 +371,17 @@
         out_specs=HB,
         scratch_shapes=[
             pltpu.VMEM((8, 128), F32),
-            pltpu.VMEM((33 * 64, 128), F32),
-            pltpu.VMEM((33 * 64, 128), F32),
+            pltpu.VMEM((33 * STEP, 128), F32),
+            pltpu.VMEM((33 * STEP, 128), F32),
             pltpu.VMEM((CHUNKS, 192, 256), BF16),
             pltpu.SemaphoreType.DMA((4,)),
         ],
-        compiler_params=pltpu.CompilerParams(vmem_limit_bytes=ROOMY),
+        compiler_params=pltpu.CompilerParams(vmem_limit_bytes=56_000_000),
         cost_estimate=pl.CostEstimate(flops=10 ** 5, bytes_accessed=1 << 10, transcendentals=0),
     )(taps, basis)
 
 
-def call_sky(row, col, count, shaped, got, obs, back, halo_up, halo_down):
+def call_sky(row, col, count, shaped, got, obs, back, first, second):
     return pl.pallas_call(
         sky_kernel,
         out_shape=(
@@ -397,7 +410,7 @@
         ] + [pltpu.VMEM((PLANES * CROWS, 128), F32)] * (2 * PAIRS),
         compiler_params=pltpu.CompilerParams(vmem_limit_bytes=54_000_000),
         cost_estimate=pl.CostEstimate(flops=4 * 10 ** 9, bytes_accessed=4 << 20, transcendentals=0),
-    )(row, col, count, shaped, got, obs, back, halo_up, halo_down)
+    )(row, col, count, shaped, got, obs, back, first, second)
 
 
 def call_owner(index, got):
@@ -416,16 +429,15 @@
     index = send_index[0]
     row, col = stamp_row[0], stamp_col[0]
     obs, back = observed[0], background[0]
+    sent = call_send(index, tile_count, params.T, row, col)
+    even = (lax.axis_index("sky") & 1) == 0
     low = jnp.concatenate([obs[TR - 32:], back[TR - 32:]], axis=0)
     high = jnp.concatenate([obs[:32], back[:32]], axis=0)
-    sent = call_send(index, tile_count, params.T, row, col)
+    first, second = jnp.where(even, low, high), jnp.where(even, high, low)
     got = lax.all_to_all(sent, "sky", split_axis=0, concat_axis=0, tiled=True)
-    to_next = [(i, i + 1) for i in range(n - 1)]
-    to_prev = [(i + 1, i) for i in range(n - 1)]
-    halo_up = lax.ppermute(low, "sky", to_next)
-    halo_down = lax.ppermute(high, "sky", to_prev)
-    shaped = call_basis(psf_taps[0], basis)
-    residual, keep, give = call_sky(row, col, tile_count, shaped, got, obs, back, halo_up, halo_down)
+    first = lax.ppermute(first, "sky", [(i, i ^ 1) for i in range(n)])
+    second = lax.ppermute(second, "sky", [(i, ((i + 1) ^ 1) - 1) for i in range(1, n - 1)])
+    residual, keep, give = call_sky(row, col, tile_count, call_basis(psf_taps[0], basis), got, obs, back, first, second)
     swap = [(i, i ^ 1) for i in range(16)]
     mine = keep + lax.ppermute(give, "epoch", swap)
     spread = jnp.broadcast_to(mine[:, None], (n, 8, 4, 128)).reshape(128, 4, 128)

time: 68.5 us -> 65.4 us (0.955)
  Pallas kernels: 17.5 us -> 15.5 us
  waiting for transfers between devices: 1.73 us -> 3.07 us
  blocking collectives: 30.8 us -> 29.5 us
  starting transfers between devices: 16.4 us -> 15.5 us
    pallas_call x1, Pallas kernels: 4.86 us -> 3.04 us  [call_basis(): pl.pallas_call(basis_kernel, out_shape=jax.ShapeDtypeStruct((CHUNKS, 192,...]
    all_to_all x1, blocking collectives: 30.8 us -> 29.5 us  [on_device(): lax.all_to_all(spread, ('sky', 'epoch'), split_axis=0, concat_axis=0, til...]
    ppermute x2, waiting for transfers between devices: 0.01 us -> 1.35 us  [the longest x1 1.35 us: on_device(): first = lax.ppermute(first, 'sky', [(i, i ^ 1) for i in range(n)])]
    ppermute x1, starting transfers between devices: 2.26 us -> 1.27 us  [on_device(): mine = keep + lax.ppermute(give, 'epoch', swap)]
  transfers between devices with their start and end apart: 5 -> 5, of which waited for: 2 -> 3; matrix products, arithmetic and copies ran while one was open for 0% -> 0% of each run, Pallas kernels for 7% -> 5%
where the time goes in v5:
time: 65.4 us; the launch traced here: 65.1 us
  blocking collectives  29.5 us (45%)
  Pallas kernels  15.5 us (24%)
  starting transfers between devices  15.5 us (24%)
  waiting for transfers between devices  3.07 us (5%)
  between operations  0.79 us (1%)
    all_to_all x1, blocking collectives, on_device(): lax.all_to_all(spread, ('sky', 'epoch'), split_axis=0, concat_axis=0, til...  29.5 us
    pallas_call x1, Pallas kernels, call_sky(): pl.pallas_call(sky_kernel, out_shape=(jax.ShapeDtypeStruct((TR, TW), F32)...  9.46 us
    all_to_all x1, starting transfers between devices, on_device(): got = lax.all_to_all(sent, 'sky', split_axis=0, concat_axis=0, tiled=True)  7.72 us
    ppermute x1, starting transfers between devices, on_device(): first = lax.ppermute(first, 'sky', [(i, i ^ 1) for i in range(n)])  3.86 us
    pallas_call x1, Pallas kernels, call_basis(): pl.pallas_call(basis_kernel, out_shape=jax.ShapeDtypeStruct((CHUNKS, 192,...  3.04 us
    ppermute x1, starting transfers between devices, on_device(): grad = part + lax.ppermute(part, 'epoch', swap)  1.98 us
    pallas_call x1, Pallas kernels, call_send(): pl.pallas_call(send_kernel, out_shape=jax.ShapeDtypeStruct((NSKY, 64, 128...  1.97 us
    ppermute x1, waiting for transfers between devices, on_device(): first = lax.ppermute(first, 'sky', [(i, i ^ 1) for i in range(n)])  1.35 us
  transfers between devices with their start and end apart: 5, of which 3 were waited for; matrix products, arithmetic and copies ran while one was open for 0% of the time, Pallas kernels for 5%

profile of v5, /device:TPU:1, one launch (start us, length us, event | category | flops | bytes accessed | tf_op | source)
XLA Modules:
  0.0 65.1 jit_solution(411800115263443310)
XLA Ops:
  0.6 0.0 copy-start.1
  0.6 0.0 copy-start.2
  0.7 2.0 %shard_map.105 = bf16[16,64,128]{2,1,0:T(8,128)(2,1)} custom-call(s32[16,16]{1,0:T(8,128)} %bitcast.21, s32[1,16]{1,0:T(1,128)} %count_s.3, bf16[64,128]{1,0:T(8,128)(2,1)} %bitcast.29, s32[16,16]{1,0:T(8,128)} %bitcast.24, s32[16,16]{1,0:T(8,128)} %bitcast.26), custom_call_target="tpu_custom_call" | custom-call | flops 8000000000 | bytes 16777216 | tf_op jit(solution)/shard_map/pallas_call | solution.py:355
  2.6 0.0 copy-start
  2.6 0.0 copy-start.4
  2.6 7.7 %all-to-all-start = ((bf16[16,64,128]{2,1,0:T(8,128)(2,1)}), bf16[16,64,128]{2,1,0:T(8,128)(2,1)S(1)}, u32[]{:S(2)}, u32[]{:S(2)}) async-start(bf16[16,64,128]{2,1,0:T(8,128)(2,1)} %shard_map.105), calls=%async_computation | async-start | bytes 524288 | tf_op jit(solution)/shard_map/all_to_all | solution.py:437
  10.4 0.0 copy-done.1
  10.4 0.0 copy-done.2
  10.4 0.0 copy-start.5
  10.4 0.0 copy-start.6
  10.4 0.0 copy-start.7
  10.5 0.7 %collective-permute-start.1 = (f32[64,512]{1,0:T(8,128)S(1)}, f32[64,512]{1,0:T(8,128)S(1)}, u32[]{:S(2)}, u32[]{:S(2)}) collective-permute-start(f32[64,512]{1,0:T(8,128)S(1)} %get-tuple-element.12), channel_id=1, source_target_pairs={{16,32},{32,16},{48,64},{64,48},{80,96},{96,80},{112,128},{128,112... | collective-permute-start | bytes 393224 | tf_op jit(solution)/shard_map/ppermute | solution.py:439
  11.1 3.9 %collective-permute-start = (f32[64,512]{1,0:T(8,128)S(1)}, f32[64,512]{1,0:T(8,128)S(1)}, u32[]{:S(2)}, u32[]{:S(2)}) collective-permute-start(f32[64,512]{1,0:T(8,128)S(1)} %get-tuple-element.13), channel_id=1, source_target_pairs={{0,16},{16,0},{32,48},{48,32},{64,80},{80,64},{96,112},{112,96},{1... | collective-permute-start | bytes 393224 | tf_op jit(solution)/shard_map/ppermute | solution.py:438
  15.0 0.0 copy-done
  15.0 0.0 copy-done.4
  15.0 3.0 %shard_map.104.b_hbm = bf16[16,192,256]{2,1,0:T(8,128)(2,1)} custom-call(f32[2,51]{1,0:T(2,128)S(1)} %bitcast.23, bf16[64,4096]{1,0:T(8,128)(2,1)S(1)} %copy-done), custom_call_target="tpu_custom_call" | custom-call | flops 100000 | bytes 1024 | tf_op jit(solution)/shard_map/pallas_call | solution.py:367
  18.1 0.0 collective-permute-done.1.second_ref
  18.1 1.3 %collective-permute-done.first_ref = f32[64,512]{1,0:T(8,128)S(1)} collective-permute-done((f32[64,512]{1,0:T(8,128)S(1)}, f32[64,512]{1,0:T(8,128)S(1)}, u32[]{:S(2)}, u32[]{:S(2)}) %collective-permute-start) | collective-permute-done | bytes 131104 | tf_op jit(solution)/shard_map/ppermute | solution.py:438
  19.4 0.0 all-to-all-done.got_ref
  19.4 0.0 copy-done.5
  19.4 0.0 copy-done.6
  19.4 0.0 copy-done.7
  19.4 0.0 copy-start.3
  19.5 9.5 %shard_map.106 = (f32[256,512]{1,0:T(8,128)}, f32[16,4,128]{2,1,0:T(4,128)S(1)}, f32[16,4,128]{2,1,0:T(4,128)S(1)}) custom-call(s32[16,16]{1,0:T(8,128)S(1)} %bitcast.25, s32[16,16]{1,0:T(8,128)S(1)} %bitcast.27, s32[1,16]{1,0:T(1,128)S(1)} %copy-done.7, bf16[16,192,256]{2,1,0:T(8,128)(2,1)} %shard_map.104.b_hbm, ...), custom_call_target="tpu_custom_call" | custom-call | flops 4000000000 | bytes 4194304 | tf_op jit(solution)/shard_map/pallas_call | solution.py:385
  28.9 1.3 %collective-permute-start.2 = (f32[16,4,128]{2,1,0:T(4,128)S(1)}, f32[16,4,128]{2,1,0:T(4,128)S(1)}, u32[]{:S(2)}, u32[]{:S(2)}) collective-permute-start(f32[16,4,128]{2,1,0:T(4,128)S(1)} %get-tuple-element.6), channel_id=1, source_target_pairs={{0,1},{1,0},{2,3},{3,2},{4,5},{5,4},{6,7},{7,6},{8,9},{9,8},{10,11... | collective-permute-start | bytes 98312 | tf_op jit(solution)/shard_map/ppermute | solution.py:442
  30.2 0.9 %collective-permute-done.2 = f32[16,4,128]{2,1,0:T(4,128)S(1)} collective-permute-done((f32[16,4,128]{2,1,0:T(4,128)S(1)}, f32[16,4,128]{2,1,0:T(4,128)S(1)}, u32[]{:S(2)}, u32[]{:S(2)}) %collective-permute-start.2) | collective-permute-done | bytes 32800 | tf_op jit(solution)/shard_map/ppermute | solution.py:442
  31.1 29.5 %all_to_all.10.got_ref = f32[128,4,128]{2,1,0:T(4,128)S(1)} all-to-all(f32[128,4,128]{2,1,0:T(4,128)S(1)} %bitcast.28), channel_id=1, replica_groups={{0,2,4,6,8,10,12,14,16,18,20,22,24,26,28,30,32,34,36,38,40,42,44,46,48,..., dimensions={0} | all-to-all | bytes 524288 | tf_op jit(solution)/shard_map/all_to_all | solution.py:445
  60.6 0.0 copy-done.3
  60.6 1.1 %shard_map.107 = f32[64,128]{1,0:T(8,128)S(1)} custom-call(s32[16,16]{1,0:T(8,128)S(1)} %bitcast.22, f32[128,4,128]{2,1,0:T(4,128)S(1)} %all_to_all.10.got_ref), custom_call_target="tpu_custom_call" | custom-call | tf_op jit(solution)/shard_map/pallas_call | solution.py:417
  61.7 2.0 %collective-permute-start.3 = (f32[64,128]{1,0:T(8,128)S(1)}, f32[64,128]{1,0:T(8,128)S(1)}, u32[]{:S(2)}, u32[]{:S(2)}) collective-permute-start(f32[64,128]{1,0:T(8,128)S(1)} %shard_map.107), channel_id=1, source_target_pairs={{0,1},{1,0},{2,3},{3,2},{4,5},{5,4},{6,7},{7,6},{8,9},{9,8},{10,11... | collective-permute-start | bytes 98312 | tf_op jit(solution)/shard_map/ppermute | solution.py:449
  63.7 0.9 %collective-permute-done.3 = f32[64,128]{1,0:T(8,128)S(1)} collective-permute-done((f32[64,128]{1,0:T(8,128)S(1)}, f32[64,128]{1,0:T(8,128)S(1)}, u32[]{:S(2)}, u32[]{:S(2)}) %collective-permute-start.3) | collective-permute-done | bytes 32800 | tf_op jit(solution)/shard_map/ppermute | solution.py:449
  64.5 0.6 add_bitcast_fusion
  (4 shorter events, 0.1 us)
Async XLA Ops:
  0.6 9.7 %copy-start.1 = (f32[1,256,512]{2,1,0:T(8,128)S(1)}, f32[1,256,512]{2,1,0:T(8,128)}, u32[]{:S(2)}) copy-start(f32[1,256,512]{2,1,0:T(8,128)} %param.16) | copy-start | bytes 1572868
  0.6 9.7 %copy-start.2 = (f32[1,256,512]{2,1,0:T(8,128)S(1)}, f32[1,256,512]{2,1,0:T(8,128)}, u32[]{:S(2)}) copy-start(f32[1,256,512]{2,1,0:T(8,128)} %param.17) | copy-start | bytes 1572868
  2.6 12.4 %copy-start = (bf16[64,4096]{1,0:T(8,128)(2,1)S(1)}, bf16[64,4096]{1,0:T(8,128)(2,1)}, u32[]{:S(2)}) copy-start(bf16[64,4096]{1,0:T(8,128)(2,1)} %basis_ref.1) | copy-start | bytes 1572868
  2.6 12.4 %copy-start.4 = (f32[1,2,51]{2,1,0:T(2,128)S(1)}, f32[1,2,51]{2,1,0:T(2,128)}, u32[]{:S(2)}) copy-start(f32[1,2,51]{2,1,0:T(2,128)} %param.11) | copy-start | bytes 1228
  2.6 16.8 %all-to-all-start = ((bf16[16,64,128]{2,1,0:T(8,128)(2,1)}), bf16[16,64,128]{2,1,0:T(8,128)(2,1)S(1)}, u32[]{:S(2)}, u32[]{:S(2)}) async-start(bf16[16,64,128]{2,1,0:T(8,128)(2,1)} %shard_map.105), calls=%async_computation | async-start | bytes 524288 | tf_op jit(solution)/shard_map/all_to_all | solution.py:437
  10.4 9.1 %copy-start.5 = (s32[1,16,16]{2,1,0:T(8,128)S(1)}, s32[1,16,16]{2,1,0:T(8,128)}, u32[]{:S(2)}) copy-start(s32[1,16,16]{2,1,0:T(8,128)} %param.14) | copy-start | bytes 3076
  10.4 9.0 %copy-start.6 = (s32[1,16,16]{2,1,0:T(8,128)S(1)}, s32[1,16,16]{2,1,0:T(8,128)}, u32[]{:S(2)}) copy-start(s32[1,16,16]{2,1,0:T(8,128)} %param.15) | copy-start | bytes 3076
  10.4 9.0 %copy-start.7 = (s32[1,16]{1,0:T(1,128)S(1)}, s32[1,16]{1,0:T(1,128)}, u32[]{:S(2)}) copy-start(s32[1,16]{1,0:T(1,128)} %count_s.3) | copy-start | bytes 196
  10.5 7.6 %collective-permute-start.1 = (f32[64,512]{1,0:T(8,128)S(1)}, f32[64,512]{1,0:T(8,128)S(1)}, u32[]{:S(2)}, u32[]{:S(2)}) collective-permute-start(f32[64,512]{1,0:T(8,128)S(1)} %get-tuple-element.12), channel_id=1, source_target_pairs={{16,32},{32,16},{48,64},{64,48},{80,96},{96,80},{112,128},{128,112... | collective-permute-start | bytes 393224 | tf_op jit(solution)/shard_map/ppermute | solution.py:439
  11.1 8.3 %collective-permute-start = (f32[64,512]{1,0:T(8,128)S(1)}, f32[64,512]{1,0:T(8,128)S(1)}, u32[]{:S(2)}, u32[]{:S(2)}) collective-permute-start(f32[64,512]{1,0:T(8,128)S(1)} %get-tuple-element.13), channel_id=1, source_target_pairs={{0,16},{16,0},{32,48},{48,32},{64,80},{80,64},{96,112},{112,96},{1... | collective-permute-start | bytes 393224 | tf_op jit(solution)/shard_map/ppermute | solution.py:438
  19.4 41.2 %copy-start.3 = (s32[1,16,16]{2,1,0:T(8,128)S(1)}, s32[1,16,16]{2,1,0:T(8,128)}, u32[]{:S(2)}) copy-start(s32[1,16,16]{2,1,0:T(8,128)} %param.12) | copy-start | bytes 3076
  28.9 2.1 %collective-permute-start.2 = (f32[16,4,128]{2,1,0:T(4,128)S(1)}, f32[16,4,128]{2,1,0:T(4,128)S(1)}, u32[]{:S(2)}, u32[]{:S(2)}) collective-permute-start(f32[16,4,128]{2,1,0:T(4,128)S(1)} %get-tuple-element.6), channel_id=1, source_target_pairs={{0,1},{1,0},{2,3},{3,2},{4,5},{5,4},{6,7},{7,6},{8,9},{9,8},{10,11... | collective-permute-start | bytes 98312 | tf_op jit(solution)/shard_map/ppermute | solution.py:442
  61.7 2.8 %collective-permute-start.3 = (f32[64,128]{1,0:T(8,128)S(1)}, f32[64,128]{1,0:T(8,128)S(1)}, u32[]{:S(2)}, u32[]{:S(2)}) collective-permute-start(f32[64,128]{1,0:T(8,128)S(1)} %shard_map.107), channel_id=1, source_target_pairs={{0,1},{1,0},{2,3},{3,2},{4,5},{5,4},{6,7},{7,6},{8,9},{9,8},{10,11... | collective-permute-start | bytes 98312 | tf_op jit(solution)/shard_map/ppermute | solution.py:449

commit v6 on v5

--- a/solution.py
+++ b/solution.py
@@ -74,7 +74,13 @@
     out_ref[NSKY - 1, 32:48, :] = none
 
 
-def basis_kernel(taps_ref, basis_ref, out_hbm, taps_pad, xs, ts, out_ref, sems):
+def basis_kernel(index_s, taps_ref, basis_ref, out_hbm, first, second, taps_pad, xs, ts, out_ref, sems):
+    core = lax.axis_index("epoch") & 1
+    source = iota((1, 128), 1)
+    for t in range(NSKY):
+        for r in range(4):
+            for hot, k in ((first, r), (second, r + 4)):
+                hot[t * 4 + r:t * 4 + r + 1, :] = jnp.where(source == index_s[t, core * 8 + k], 1.0, 0.0).astype(F32)
     taps_pad[...] = jnp.zeros((8, 128), F32)
     taps = taps_ref[...]
     taps_pad[0:2, 0:TAPS] = taps / jnp.sum(taps, axis=1, keepdims=True)
@@ -129,8 +135,13 @@
     tile = lax.axis_index("sky")
     core = lax.axis_index("epoch") % 2
     lane32 = iota((32, 128), 1)
-    b_copy = pltpu.make_async_copy(b_hbm, b_ref, sems.at[3])
-    b_copy.start()
+
+    def b_copy(i):
+        some = pl.ds(4 * i, 4)
+        return pltpu.make_async_copy(b_hbm.at[some], b_ref.at[some], sems.at[3 + i])
+
+    for i in range(4):
+        b_copy(i).start()
     late = [pltpu.make_async_copy(obs_hbm, obs_ref, sems.at[0]), pltpu.make_async_copy(back_hbm, back_ref, sems.at[1])]
     for each in late:
         each.start()
@@ -164,7 +175,6 @@
     for j in range(32):
         ss[j * SROWS + SLOTS:(j + 1) * SROWS, :] = jnp.zeros((SROWS - SLOTS, 128), F32)
     copy.wait()
-    b_copy.wait()
 
     span = PLANES * CROWS // CHUNKS
 
@@ -183,7 +193,10 @@
                 count = count + jnp.where(entry >= 0, 1, 0)
         return count
 
-    count = lax.fori_loop(0, CHUNKS, render, jnp.int32(0), unroll=4)
+    count = tile * 0
+    for i in range(4):
+        b_copy(i).wait()
+        count = lax.fori_loop(4 * i, 4 * i + 4, render, count, unroll=4)
 
     def pack(g, unused):
         for i in range(GROUP):
@@ -329,13 +342,7 @@
     res_copy.wait()
 
 
-def owner_kernel(index_s, got_ref, out_ref, first, second, sums):
-    core = lax.axis_index("epoch") % 2
-    lane = iota((1, 128), 1)
-    for t in range(NSKY):
-        for r in range(4):
-            for hot, k in ((first, r), (second, r + 4)):
-                hot[t * 4 + r:t * 4 + r + 1, :] = jnp.where(lane == index_s[t, core * 8 + k], 1.0, 0.0).astype(F32)
+def owner_kernel(first, second, got_ref, out_ref, sums):
     for t in range(NSKY):
         s = got_ref[t * 8]
         for z in range(1, 8):
@@ -363,12 +370,16 @@
     )(index, count, params_t, row, col)
 
 
-def call_basis(taps, basis):
+def call_basis(index, taps, basis):
     return pl.pallas_call(
         basis_kernel,
-        out_shape=jax.ShapeDtypeStruct((CHUNKS, 192, 256), BF16),
-        in_specs=[VM, VM],
-        out_specs=HB,
+        out_shape=(
+            jax.ShapeDtypeStruct((CHUNKS, 192, 256), BF16),
+            jax.ShapeDtypeStruct((64, 128), F32),
+            jax.ShapeDtypeStruct((64, 128), F32),
+        ),
+        in_specs=[SM, VM, VM],
+        out_specs=(HB, VM, VM),
         scratch_shapes=[
             pltpu.VMEM((8, 128), F32),
             pltpu.VMEM((33 * STEP, 128), F32),
@@ -376,9 +387,9 @@
             pltpu.VMEM((CHUNKS, 192, 256), BF16),
             pltpu.SemaphoreType.DMA((4,)),
         ],
-        compiler_params=pltpu.CompilerParams(vmem_limit_bytes=56_000_000),
+        compiler_params=pltpu.CompilerParams(vmem_limit_bytes=55_000_000),
         cost_estimate=pl.CostEstimate(flops=10 ** 5, bytes_accessed=1 << 10, transcendentals=0),
-    )(taps, basis)
+    )(index, taps, basis)
 
 
 def call_sky(row, col, count, shaped, got, obs, back, first, second):
@@ -396,7 +407,7 @@
             pltpu.VMEM((TR, TW), F32),
             pltpu.VMEM((TR, TW), F32),
             pltpu.VMEM((TR, TW), F32),
-            pltpu.SemaphoreType.DMA((4,)),
+            pltpu.SemaphoreType.DMA((7,)),
             pltpu.VMEM((33 * SROWS, 128), F32),
             pltpu.VMEM((PLANES * XROWS, 128), F32),
             pltpu.VMEM((PLANES * XROWS, 128), F32),
@@ -413,15 +424,15 @@
     )(row, col, count, shaped, got, obs, back, first, second)
 
 
-def call_owner(index, got):
+def call_owner(first, second, got):
     return pl.pallas_call(
         owner_kernel,
         out_shape=jax.ShapeDtypeStruct((PS, 128), F32),
-        in_specs=[SM, VM],
+        in_specs=[VM, VM, VM],
         out_specs=VM,
-        scratch_shapes=[pltpu.VMEM((64, 128), F32)] * 3,
+        scratch_shapes=[pltpu.VMEM((64, 128), F32)],
         compiler_params=pltpu.CompilerParams(vmem_limit_bytes=8 << 20),
-    )(index, got)
+    )(first, second, got)
 
 
 def on_device(params, basis, psf_taps, send_index, tile_count, stamp_row, stamp_col, observed, background):
@@ -437,7 +448,8 @@
     got = lax.all_to_all(sent, "sky", split_axis=0, concat_axis=0, tiled=True)
     first = lax.ppermute(first, "sky", [(i, i ^ 1) for i in range(n)])
     second = lax.ppermute(second, "sky", [(i, ((i + 1) ^ 1) - 1) for i in range(1, n - 1)])
-    residual, keep, give = call_sky(row, col, tile_count, call_basis(psf_taps[0], basis), got, obs, back, first, second)
+    shaped, hot_first, hot_second = call_basis(index, psf_taps[0], basis)
+    residual, keep, give = call_sky(row, col, tile_count, shaped, got, obs, back, first, second)
     swap = [(i, i ^ 1) for i in range(16)]
     mine = keep + lax.ppermute(give, "epoch", swap)
     spread = jnp.broadcast_to(mine[:, None], (n, 8, 4, 128)).reshape(128, 4, 128)
@@ -445,7 +457,7 @@
     back_home = lax.all_to_all(
         spread, ("sky", "epoch"), split_axis=0, concat_axis=0, tiled=True, axis_index_groups=groups
     )
-    part = call_owner(index, back_home)
+    part = call_owner(hot_first, hot_second, back_home)
     grad = part + lax.ppermute(part, "epoch", swap)
     return grad.T, residual[None]
 

time: 65.4 us -> 64.3 us (0.983)
    pallas_call x1, Pallas kernels: 1.07 us -> 0.34 us  [call_owner(): pl.pallas_call(owner_kernel, out_shape=jax.ShapeDtypeStruct((PS, 128), F3...]
    pallas_call x1, Pallas kernels: 3.04 us -> 3.73 us  [call_basis(): pl.pallas_call(basis_kernel, out_shape=(jax.ShapeDtypeStruct((CHUNKS, 192...]
  transfers between devices with their start and end apart: 5 -> 5, of which waited for: 3 -> 3; matrix products, arithmetic and copies ran while one was open for 0% -> 0% of each run, Pallas kernels for 5% -> 6%
where the time goes in v6:
time: 64.3 us
  blocking collectives  29.6 us (46%)
  starting transfers between devices  15.5 us (24%)
  Pallas kernels  15.2 us (24%)
  waiting for transfers between devices  2.46 us (4%)
  between operations  0.79 us (1%)
  other arithmetic  0.65 us (1%)
    all_to_all x1, blocking collectives, on_device(): lax.all_to_all(spread, ('sky', 'epoch'), split_axis=0, concat_axis=0, til...  29.6 us
    pallas_call x1, Pallas kernels, call_sky(): pl.pallas_call(sky_kernel, out_shape=(jax.ShapeDtypeStruct((TR, TW), F32)...  9.21 us
    all_to_all x1, starting transfers between devices, on_device(): got = lax.all_to_all(sent, 'sky', split_axis=0, concat_axis=0, tiled=True)  7.73 us
    ppermute x1, starting transfers between devices, on_device(): first = lax.ppermute(first, 'sky', [(i, i ^ 1) for i in range(n)])  3.86 us
    pallas_call x1, Pallas kernels, call_basis(): pl.pallas_call(basis_kernel, out_shape=(jax.ShapeDtypeStruct((CHUNKS, 192...  3.73 us
    ppermute x1, starting transfers between devices, on_device(): grad = part + lax.ppermute(part, 'epoch', swap)  1.98 us
    pallas_call x1, Pallas kernels, call_send(): pl.pallas_call(send_kernel, out_shape=jax.ShapeDtypeStruct((NSKY, 64, 128...  1.97 us
  transfers between devices with their start and end apart: 5, of which 3 were waited for; matrix products, arithmetic and copies ran while one was open for 0% of the time, Pallas kernels for 6%

profile of v6, /device:TPU:1, one launch (start us, length us, event | category | flops | bytes accessed | tf_op | source)
XLA Modules:
  0.0 64.3 jit_solution(15404694481259098503)
XLA Ops:
  0.6 0.0 copy-start.1
  0.6 0.0 copy-start.2
  0.7 2.0 %shard_map.105 = bf16[16,64,128]{2,1,0:T(8,128)(2,1)} custom-call(s32[16,16]{1,0:T(8,128)} %bitcast.21, s32[1,16]{1,0:T(1,128)} %count_s.3, bf16[64,128]{1,0:T(8,128)(2,1)} %bitcast.29, s32[16,16]{1,0:T(8,128)} %bitcast.24, s32[16,16]{1,0:T(8,128)} %bitcast.26), custom_call_target="tpu_custom_call" | custom-call | flops 8000000000 | bytes 16777216 | tf_op jit(solution)/shard_map/pallas_call | solution.py:362
  2.6 0.0 copy-start
  2.6 0.0 copy-start.3
  2.6 0.0 copy-start.4
  2.6 0.0 copy-start.5
  2.6 0.0 copy-start.6
  2.7 0.0 copy-start.7
  2.7 7.7 %all-to-all-start = ((bf16[16,64,128]{2,1,0:T(8,128)(2,1)}), bf16[16,64,128]{2,1,0:T(8,128)(2,1)S(1)}, u32[]{:S(2)}, u32[]{:S(2)}) async-start(bf16[16,64,128]{2,1,0:T(8,128)(2,1)} %shard_map.105), calls=%async_computation | async-start | bytes 524288 | tf_op jit(solution)/shard_map/all_to_all | solution.py:448
  10.4 0.0 copy-done.1
  10.4 0.0 copy-done.2
  10.5 0.7 %collective-permute-start.1 = (f32[64,512]{1,0:T(8,128)S(1)}, f32[64,512]{1,0:T(8,128)S(1)}, u32[]{:S(2)}, u32[]{:S(2)}) collective-permute-start(f32[64,512]{1,0:T(8,128)S(1)} %get-tuple-element.18), channel_id=1, source_target_pairs={{16,32},{32,16},{48,64},{64,48},{80,96},{96,80},{112,128},{128,112... | collective-permute-start | bytes 393224 | tf_op jit(solution)/shard_map/ppermute | solution.py:450
  11.2 3.9 %collective-permute-start = (f32[64,512]{1,0:T(8,128)S(1)}, f32[64,512]{1,0:T(8,128)S(1)}, u32[]{:S(2)}, u32[]{:S(2)}) collective-permute-start(f32[64,512]{1,0:T(8,128)S(1)} %get-tuple-element.19), channel_id=1, source_target_pairs={{0,16},{16,0},{32,48},{48,32},{64,80},{80,64},{96,112},{112,96},{1... | collective-permute-start | bytes 393224 | tf_op jit(solution)/shard_map/ppermute | solution.py:449
  15.0 0.0 copy-done
  15.0 0.0 copy-done.3
  15.0 0.0 copy-done.4
  15.0 3.7 %shard_map.104 = (bf16[16,192,256]{2,1,0:T(8,128)(2,1)}, f32[64,128]{1,0:T(8,128)S(1)}, f32[64,128]{1,0:T(8,128)S(1)}) custom-call(s32[16,16]{1,0:T(8,128)S(1)} %bitcast.22, f32[2,51]{1,0:T(2,128)S(1)} %bitcast.23, bf16[64,4096]{1,0:T(8,128)(2,1)S(1)} %copy-done), custom_call_target="tpu_custom_call" | custom-call | flops 100000 | bytes 1024 | tf_op jit(solution)/shard_map/pallas_call | solution.py:374
  18.8 0.0 collective-permute-done.1.second_ref
  18.8 0.7 %collective-permute-done.first_ref = f32[64,512]{1,0:T(8,128)S(1)} collective-permute-done((f32[64,512]{1,0:T(8,128)S(1)}, f32[64,512]{1,0:T(8,128)S(1)}, u32[]{:S(2)}, u32[]{:S(2)}) %collective-permute-start) | collective-permute-done | bytes 131104 | tf_op jit(solution)/shard_map/ppermute | solution.py:449
  19.5 0.0 all-to-all-done.got_ref
  19.5 0.0 copy-done.5
  19.5 0.0 copy-done.6
  19.5 0.0 copy-done.7
  19.5 9.2 %shard_map.106 = (f32[256,512]{1,0:T(8,128)}, f32[16,4,128]{2,1,0:T(4,128)S(1)}, f32[16,4,128]{2,1,0:T(4,128)S(1)}) custom-call(s32[16,16]{1,0:T(8,128)S(1)} %bitcast.25, s32[16,16]{1,0:T(8,128)S(1)} %bitcast.27, s32[1,16]{1,0:T(1,128)S(1)} %copy-done.7, bf16[16,192,256]{2,1,0:T(8,128)(2,1)} %get-tuple-element.10.b_hbm, ...), custom_call_target="tpu_custom_call" | custom-call | flops 4000000000 | bytes 4194304 | tf_op jit(solution)/shard_map/pallas_call | solution.py:396
  28.8 1.2 %collective-permute-start.2 = (f32[16,4,128]{2,1,0:T(4,128)S(1)}, f32[16,4,128]{2,1,0:T(4,128)S(1)}, u32[]{:S(2)}, u32[]{:S(2)}) collective-permute-start(f32[16,4,128]{2,1,0:T(4,128)S(1)} %get-tuple-element.12), channel_id=1, source_target_pairs={{0,1},{1,0},{2,3},{3,2},{4,5},{5,4},{6,7},{7,6},{8,9},{9,8},{10,11... | collective-permute-start | bytes 98312 | tf_op jit(solution)/shard_map/ppermute | solution.py:454
  30.0 0.9 %collective-permute-done.2 = f32[16,4,128]{2,1,0:T(4,128)S(1)} collective-permute-done((f32[16,4,128]{2,1,0:T(4,128)S(1)}, f32[16,4,128]{2,1,0:T(4,128)S(1)}, u32[]{:S(2)}, u32[]{:S(2)}) %collective-permute-start.2) | collective-permute-done | bytes 32800 | tf_op jit(solution)/shard_map/ppermute | solution.py:454
  30.9 29.6 %all_to_all.10.got_ref = f32[128,4,128]{2,1,0:T(4,128)S(1)} all-to-all(f32[128,4,128]{2,1,0:T(4,128)S(1)} %bitcast.28), channel_id=1, replica_groups={{0,2,4,6,8,10,12,14,16,18,20,22,24,26,28,30,32,34,36,38,40,42,44,46,48,..., dimensions={0} | all-to-all | bytes 524288 | tf_op jit(solution)/shard_map/all_to_all | solution.py:457
  60.5 0.3 shard_map.107
  60.9 2.0 %collective-permute-start.3 = (f32[64,128]{1,0:T(8,128)S(1)}, f32[64,128]{1,0:T(8,128)S(1)}, u32[]{:S(2)}, u32[]{:S(2)}) collective-permute-start(f32[64,128]{1,0:T(8,128)S(1)} %shard_map.107), channel_id=1, source_target_pairs={{0,1},{1,0},{2,3},{3,2},{4,5},{5,4},{6,7},{7,6},{8,9},{9,8},{10,11... | collective-permute-start | bytes 98312 | tf_op jit(solution)/shard_map/ppermute | solution.py:461
  62.8 0.9 %collective-permute-done.3 = f32[64,128]{1,0:T(8,128)S(1)} collective-permute-done((f32[64,128]{1,0:T(8,128)S(1)}, f32[64,128]{1,0:T(8,128)S(1)}, u32[]{:S(2)}, u32[]{:S(2)}) %collective-permute-start.3) | collective-permute-done | bytes 32800 | tf_op jit(solution)/shard_map/ppermute | solution.py:461
  63.7 0.6 add_bitcast_fusion
  (4 shorter events, 0.1 us)
Async XLA Ops:
  0.6 9.8 %copy-start.1 = (f32[1,256,512]{2,1,0:T(8,128)S(1)}, f32[1,256,512]{2,1,0:T(8,128)}, u32[]{:S(2)}) copy-start(f32[1,256,512]{2,1,0:T(8,128)} %param.16) | copy-start | bytes 1572868
  0.6 9.8 %copy-start.2 = (f32[1,256,512]{2,1,0:T(8,128)S(1)}, f32[1,256,512]{2,1,0:T(8,128)}, u32[]{:S(2)}) copy-start(f32[1,256,512]{2,1,0:T(8,128)} %param.17) | copy-start | bytes 1572868
  2.6 12.4 %copy-start = (bf16[64,4096]{1,0:T(8,128)(2,1)S(1)}, bf16[64,4096]{1,0:T(8,128)(2,1)}, u32[]{:S(2)}) copy-start(bf16[64,4096]{1,0:T(8,128)(2,1)} %basis_ref.1) | copy-start | bytes 1572868
  2.6 12.4 %copy-start.3 = (s32[1,16,16]{2,1,0:T(8,128)S(1)}, s32[1,16,16]{2,1,0:T(8,128)}, u32[]{:S(2)}) copy-start(s32[1,16,16]{2,1,0:T(8,128)} %param.12) | copy-start | bytes 3076
  2.6 12.4 %copy-start.4 = (f32[1,2,51]{2,1,0:T(2,128)S(1)}, f32[1,2,51]{2,1,0:T(2,128)}, u32[]{:S(2)}) copy-start(f32[1,2,51]{2,1,0:T(2,128)} %param.11) | copy-start | bytes 1228
  2.6 16.9 %copy-start.5 = (s32[1,16,16]{2,1,0:T(8,128)S(1)}, s32[1,16,16]{2,1,0:T(8,128)}, u32[]{:S(2)}) copy-start(s32[1,16,16]{2,1,0:T(8,128)} %param.14) | copy-start | bytes 3076
  2.6 16.9 %copy-start.6 = (s32[1,16,16]{2,1,0:T(8,128)S(1)}, s32[1,16,16]{2,1,0:T(8,128)}, u32[]{:S(2)}) copy-start(s32[1,16,16]{2,1,0:T(8,128)} %param.15) | copy-start | bytes 3076
  2.7 16.9 %copy-start.7 = (s32[1,16]{1,0:T(1,128)S(1)}, s32[1,16]{1,0:T(1,128)}, u32[]{:S(2)}) copy-start(s32[1,16]{1,0:T(1,128)} %count_s.3) | copy-start | bytes 196
  2.7 16.9 %all-to-all-start = ((bf16[16,64,128]{2,1,0:T(8,128)(2,1)}), bf16[16,64,128]{2,1,0:T(8,128)(2,1)S(1)}, u32[]{:S(2)}, u32[]{:S(2)}) async-start(bf16[16,64,128]{2,1,0:T(8,128)(2,1)} %shard_map.105), calls=%async_computation | async-start | bytes 524288 | tf_op jit(solution)/shard_map/all_to_all | solution.py:448
  10.5 8.3 %collective-permute-start.1 = (f32[64,512]{1,0:T(8,128)S(1)}, f32[64,512]{1,0:T(8,128)S(1)}, u32[]{:S(2)}, u32[]{:S(2)}) collective-permute-start(f32[64,512]{1,0:T(8,128)S(1)} %get-tuple-element.18), channel_id=1, source_target_pairs={{16,32},{32,16},{48,64},{64,48},{80,96},{96,80},{112,128},{128,112... | collective-permute-start | bytes 393224 | tf_op jit(solution)/shard_map/ppermute | solution.py:450
  11.2 8.4 %collective-permute-start = (f32[64,512]{1,0:T(8,128)S(1)}, f32[64,512]{1,0:T(8,128)S(1)}, u32[]{:S(2)}, u32[]{:S(2)}) collective-permute-start(f32[64,512]{1,0:T(8,128)S(1)} %get-tuple-element.19), channel_id=1, source_target_pairs={{0,16},{16,0},{32,48},{48,32},{64,80},{80,64},{96,112},{112,96},{1... | collective-permute-start | bytes 393224 | tf_op jit(solution)/shard_map/ppermute | solution.py:449
  28.8 2.1 %collective-permute-start.2 = (f32[16,4,128]{2,1,0:T(4,128)S(1)}, f32[16,4,128]{2,1,0:T(4,128)S(1)}, u32[]{:S(2)}, u32[]{:S(2)}) collective-permute-start(f32[16,4,128]{2,1,0:T(4,128)S(1)} %get-tuple-element.12), channel_id=1, source_target_pairs={{0,1},{1,0},{2,3},{3,2},{4,5},{5,4},{6,7},{7,6},{8,9},{9,8},{10,11... | collective-permute-start | bytes 98312 | tf_op jit(solution)/shard_map/ppermute | solution.py:454
  60.9 2.8 %collective-permute-start.3 = (f32[64,128]{1,0:T(8,128)S(1)}, f32[64,128]{1,0:T(8,128)S(1)}, u32[]{:S(2)}, u32[]{:S(2)}) collective-permute-start(f32[64,128]{1,0:T(8,128)S(1)} %shard_map.107), channel_id=1, source_target_pairs={{0,1},{1,0},{2,3},{3,2},{4,5},{5,4},{6,7},{7,6},{8,9},{9,8},{10,11... | collective-permute-start | bytes 98312 | tf_op jit(solution)/shard_map/ppermute | solution.py:461

commit v7 on v6

--- a/solution.py
+++ b/solution.py
@@ -231,7 +231,7 @@
             put(i % PAIRS, g * CAP + i, row_s[g, i] + OFF, col_s[g, i])
         return unused
 
-    lax.fori_loop(0, NSKY, place, 0, unroll=4)
+    lax.fori_loop(0, NSKY, place, 0, unroll=16)
 
     def place_near(g, unused):
         for i in range(GROUP):
@@ -324,7 +324,7 @@
             ss[pl.ds(g * CAP + i, 32, stride=SROWS), :] = pltpu.roll(seen, (128 - turn) & 127, 1)
         return unused
 
-    lax.fori_loop(0, NSKY, window, 0, unroll=4)
+    lax.fori_loop(0, NSKY, window, 0, unroll=8)
 
     total = jnp.zeros((OWN, 192), F32)
     for c in range(CHUNKS):

time: 64.3 us -> 64.2 us (level)
  no operation moved by 1% of the time
where the time goes in v7:
time: 64.2 us; the launch traced here: 63.7 us
  blocking collectives  29.4 us (46%)
  starting transfers between devices  15.5 us (24%)
  Pallas kernels  14.8 us (23%)
  waiting for transfers between devices  2.46 us (4%)
  between operations  0.79 us (1%)
  other arithmetic  0.65 us (1%)
    all_to_all x1, blocking collectives, on_device(): lax.all_to_all(spread, ('sky', 'epoch'), split_axis=0, concat_axis=0, til...  29.4 us
    pallas_call x1, Pallas kernels, call_sky(): pl.pallas_call(sky_kernel, out_shape=(jax.ShapeDtypeStruct((TR, TW), F32)...  8.74 us
    all_to_all x1, starting transfers between devices, on_device(): got = lax.all_to_all(sent, 'sky', split_axis=0, concat_axis=0, tiled=True)  7.73 us
    ppermute x1, starting transfers between devices, on_device(): first = lax.ppermute(first, 'sky', [(i, i ^ 1) for i in range(n)])  3.86 us
    pallas_call x1, Pallas kernels, call_basis(): pl.pallas_call(basis_kernel, out_shape=(jax.ShapeDtypeStruct((CHUNKS, 192...  3.73 us
    ppermute x1, starting transfers between devices, on_device(): grad = part + lax.ppermute(part, 'epoch', swap)  1.98 us
    pallas_call x1, Pallas kernels, call_send(): pl.pallas_call(send_kernel, out_shape=jax.ShapeDtypeStruct((NSKY, 64, 128...  1.97 us
  transfers between devices with their start and end apart: 5, of which 3 were waited for; matrix products, arithmetic and copies ran while one was open for 0% of the time, Pallas kernels for 6%

profile of v7, /device:TPU:1, one launch (start us, length us, event | category | flops | bytes accessed | tf_op | source)
XLA Modules:
  0.0 63.7 jit_solution(14747917843070001269)
XLA Ops:
  0.6 0.0 copy-start.1
  0.6 0.0 copy-start.2
  0.7 2.0 %shard_map.105 = bf16[16,64,128]{2,1,0:T(8,128)(2,1)} custom-call(s32[16,16]{1,0:T(8,128)} %bitcast.21, s32[1,16]{1,0:T(1,128)} %count_s.3, bf16[64,128]{1,0:T(8,128)(2,1)} %bitcast.29, s32[16,16]{1,0:T(8,128)} %bitcast.24, s32[16,16]{1,0:T(8,128)} %bitcast.26), custom_call_target="tpu_custom_call" | custom-call | flops 8000000000 | bytes 16777216 | tf_op jit(solution)/shard_map/pallas_call | solution.py:362
  2.6 0.0 copy-start
  2.6 0.0 copy-start.3
  2.6 0.0 copy-start.4
  2.6 0.0 copy-start.5
  2.6 0.0 copy-start.6
  2.7 0.0 copy-start.7
  2.7 7.7 %all-to-all-start = ((bf16[16,64,128]{2,1,0:T(8,128)(2,1)}), bf16[16,64,128]{2,1,0:T(8,128)(2,1)S(1)}, u32[]{:S(2)}, u32[]{:S(2)}) async-start(bf16[16,64,128]{2,1,0:T(8,128)(2,1)} %shard_map.105), calls=%async_computation | async-start | bytes 524288 | tf_op jit(solution)/shard_map/all_to_all | solution.py:448
  10.4 0.0 copy-done.1
  10.4 0.0 copy-done.2
  10.5 0.7 %collective-permute-start.1 = (f32[64,512]{1,0:T(8,128)S(1)}, f32[64,512]{1,0:T(8,128)S(1)}, u32[]{:S(2)}, u32[]{:S(2)}) collective-permute-start(f32[64,512]{1,0:T(8,128)S(1)} %get-tuple-element.18), channel_id=1, source_target_pairs={{16,32},{32,16},{48,64},{64,48},{80,96},{96,80},{112,128},{128,112... | collective-permute-start | bytes 393224 | tf_op jit(solution)/shard_map/ppermute | solution.py:450
  11.2 3.9 %collective-permute-start = (f32[64,512]{1,0:T(8,128)S(1)}, f32[64,512]{1,0:T(8,128)S(1)}, u32[]{:S(2)}, u32[]{:S(2)}) collective-permute-start(f32[64,512]{1,0:T(8,128)S(1)} %get-tuple-element.19), channel_id=1, source_target_pairs={{0,16},{16,0},{32,48},{48,32},{64,80},{80,64},{96,112},{112,96},{1... | collective-permute-start | bytes 393224 | tf_op jit(solution)/shard_map/ppermute | solution.py:449
  15.0 0.0 copy-done
  15.0 0.0 copy-done.3
  15.0 0.0 copy-done.4
  15.0 3.7 %shard_map.104 = (bf16[16,192,256]{2,1,0:T(8,128)(2,1)}, f32[64,128]{1,0:T(8,128)S(1)}, f32[64,128]{1,0:T(8,128)S(1)}) custom-call(s32[16,16]{1,0:T(8,128)S(1)} %bitcast.22, f32[2,51]{1,0:T(2,128)S(1)} %bitcast.23, bf16[64,4096]{1,0:T(8,128)(2,1)S(1)} %copy-done), custom_call_target="tpu_custom_call" | custom-call | flops 100000 | bytes 1024 | tf_op jit(solution)/shard_map/pallas_call | solution.py:374
  18.8 0.0 collective-permute-done.1.second_ref
  18.8 0.7 %collective-permute-done.first_ref = f32[64,512]{1,0:T(8,128)S(1)} collective-permute-done((f32[64,512]{1,0:T(8,128)S(1)}, f32[64,512]{1,0:T(8,128)S(1)}, u32[]{:S(2)}, u32[]{:S(2)}) %collective-permute-start) | collective-permute-done | bytes 131104 | tf_op jit(solution)/shard_map/ppermute | solution.py:449
  19.5 0.0 all-to-all-done.got_ref
  19.5 0.0 copy-done.5
  19.5 0.0 copy-done.6
  19.5 0.0 copy-done.7
  19.5 8.7 %shard_map.106 = (f32[256,512]{1,0:T(8,128)}, f32[16,4,128]{2,1,0:T(4,128)S(1)}, f32[16,4,128]{2,1,0:T(4,128)S(1)}) custom-call(s32[16,16]{1,0:T(8,128)S(1)} %bitcast.25, s32[16,16]{1,0:T(8,128)S(1)} %bitcast.27, s32[1,16]{1,0:T(1,128)S(1)} %copy-done.7, bf16[16,192,256]{2,1,0:T(8,128)(2,1)} %get-tuple-element.10.b_hbm, ...), custom_call_target="tpu_custom_call" | custom-call | flops 4000000000 | bytes 4194304 | tf_op jit(solution)/shard_map/pallas_call | solution.py:396
  28.3 1.2 %collective-permute-start.2 = (f32[16,4,128]{2,1,0:T(4,128)S(1)}, f32[16,4,128]{2,1,0:T(4,128)S(1)}, u32[]{:S(2)}, u32[]{:S(2)}) collective-permute-start(f32[16,4,128]{2,1,0:T(4,128)S(1)} %get-tuple-element.12), channel_id=1, source_target_pairs={{0,1},{1,0},{2,3},{3,2},{4,5},{5,4},{6,7},{7,6},{8,9},{9,8},{10,11... | collective-permute-start | bytes 98312 | tf_op jit(solution)/shard_map/ppermute | solution.py:454
  29.5 0.9 %collective-permute-done.2 = f32[16,4,128]{2,1,0:T(4,128)S(1)} collective-permute-done((f32[16,4,128]{2,1,0:T(4,128)S(1)}, f32[16,4,128]{2,1,0:T(4,128)S(1)}, u32[]{:S(2)}, u32[]{:S(2)}) %collective-permute-start.2) | collective-permute-done | bytes 32800 | tf_op jit(solution)/shard_map/ppermute | solution.py:454
  30.4 29.4 %all_to_all.10.got_ref = f32[128,4,128]{2,1,0:T(4,128)S(1)} all-to-all(f32[128,4,128]{2,1,0:T(4,128)S(1)} %bitcast.28), channel_id=1, replica_groups={{0,2,4,6,8,10,12,14,16,18,20,22,24,26,28,30,32,34,36,38,40,42,44,46,48,..., dimensions={0} | all-to-all | bytes 524288 | tf_op jit(solution)/shard_map/all_to_all | solution.py:457
  59.9 0.3 shard_map.107
  60.2 2.0 %collective-permute-start.3 = (f32[64,128]{1,0:T(8,128)S(1)}, f32[64,128]{1,0:T(8,128)S(1)}, u32[]{:S(2)}, u32[]{:S(2)}) collective-permute-start(f32[64,128]{1,0:T(8,128)S(1)} %shard_map.107), channel_id=1, source_target_pairs={{0,1},{1,0},{2,3},{3,2},{4,5},{5,4},{6,7},{7,6},{8,9},{9,8},{10,11... | collective-permute-start | bytes 98312 | tf_op jit(solution)/shard_map/ppermute | solution.py:461
  62.2 0.9 %collective-permute-done.3 = f32[64,128]{1,0:T(8,128)S(1)} collective-permute-done((f32[64,128]{1,0:T(8,128)S(1)}, f32[64,128]{1,0:T(8,128)S(1)}, u32[]{:S(2)}, u32[]{:S(2)}) %collective-permute-start.3) | collective-permute-done | bytes 32800 | tf_op jit(solution)/shard_map/ppermute | solution.py:461
  63.1 0.6 add_bitcast_fusion
  (4 shorter events, 0.1 us)
Async XLA Ops:
  0.6 9.8 %copy-start.1 = (f32[1,256,512]{2,1,0:T(8,128)S(1)}, f32[1,256,512]{2,1,0:T(8,128)}, u32[]{:S(2)}) copy-start(f32[1,256,512]{2,1,0:T(8,128)} %param.16) | copy-start | bytes 1572868
  0.6 9.8 %copy-start.2 = (f32[1,256,512]{2,1,0:T(8,128)S(1)}, f32[1,256,512]{2,1,0:T(8,128)}, u32[]{:S(2)}) copy-start(f32[1,256,512]{2,1,0:T(8,128)} %param.17) | copy-start | bytes 1572868
  2.6 12.4 %copy-start = (bf16[64,4096]{1,0:T(8,128)(2,1)S(1)}, bf16[64,4096]{1,0:T(8,128)(2,1)}, u32[]{:S(2)}) copy-start(bf16[64,4096]{1,0:T(8,128)(2,1)} %basis_ref.1) | copy-start | bytes 1572868
  2.6 12.4 %copy-start.3 = (s32[1,16,16]{2,1,0:T(8,128)S(1)}, s32[1,16,16]{2,1,0:T(8,128)}, u32[]{:S(2)}) copy-start(s32[1,16,16]{2,1,0:T(8,128)} %param.12) | copy-start | bytes 3076
  2.6 12.4 %copy-start.4 = (f32[1,2,51]{2,1,0:T(2,128)S(1)}, f32[1,2,51]{2,1,0:T(2,128)}, u32[]{:S(2)}) copy-start(f32[1,2,51]{2,1,0:T(2,128)} %param.11) | copy-start | bytes 1228
  2.6 16.9 %copy-start.5 = (s32[1,16,16]{2,1,0:T(8,128)S(1)}, s32[1,16,16]{2,1,0:T(8,128)}, u32[]{:S(2)}) copy-start(s32[1,16,16]{2,1,0:T(8,128)} %param.14) | copy-start | bytes 3076
  2.6 16.9 %copy-start.6 = (s32[1,16,16]{2,1,0:T(8,128)S(1)}, s32[1,16,16]{2,1,0:T(8,128)}, u32[]{:S(2)}) copy-start(s32[1,16,16]{2,1,0:T(8,128)} %param.15) | copy-start | bytes 3076
  2.7 16.9 %copy-start.7 = (s32[1,16]{1,0:T(1,128)S(1)}, s32[1,16]{1,0:T(1,128)}, u32[]{:S(2)}) copy-start(s32[1,16]{1,0:T(1,128)} %count_s.3) | copy-start | bytes 196
  2.7 16.9 %all-to-all-start = ((bf16[16,64,128]{2,1,0:T(8,128)(2,1)}), bf16[16,64,128]{2,1,0:T(8,128)(2,1)S(1)}, u32[]{:S(2)}, u32[]{:S(2)}) async-start(bf16[16,64,128]{2,1,0:T(8,128)(2,1)} %shard_map.105), calls=%async_computation | async-start | bytes 524288 | tf_op jit(solution)/shard_map/all_to_all | solution.py:448
  10.5 8.3 %collective-permute-start.1 = (f32[64,512]{1,0:T(8,128)S(1)}, f32[64,512]{1,0:T(8,128)S(1)}, u32[]{:S(2)}, u32[]{:S(2)}) collective-permute-start(f32[64,512]{1,0:T(8,128)S(1)} %get-tuple-element.18), channel_id=1, source_target_pairs={{16,32},{32,16},{48,64},{64,48},{80,96},{96,80},{112,128},{128,112... | collective-permute-start | bytes 393224 | tf_op jit(solution)/shard_map/ppermute | solution.py:450
  11.2 8.4 %collective-permute-start = (f32[64,512]{1,0:T(8,128)S(1)}, f32[64,512]{1,0:T(8,128)S(1)}, u32[]{:S(2)}, u32[]{:S(2)}) collective-permute-start(f32[64,512]{1,0:T(8,128)S(1)} %get-tuple-element.19), channel_id=1, source_target_pairs={{0,16},{16,0},{32,48},{48,32},{64,80},{80,64},{96,112},{112,96},{1... | collective-permute-start | bytes 393224 | tf_op jit(solution)/shard_map/ppermute | solution.py:449
  28.3 2.1 %collective-permute-start.2 = (f32[16,4,128]{2,1,0:T(4,128)S(1)}, f32[16,4,128]{2,1,0:T(4,128)S(1)}, u32[]{:S(2)}, u32[]{:S(2)}) collective-permute-start(f32[16,4,128]{2,1,0:T(4,128)S(1)} %get-tuple-element.12), channel_id=1, source_target_pairs={{0,1},{1,0},{2,3},{3,2},{4,5},{5,4},{6,7},{7,6},{8,9},{9,8},{10,11... | collective-permute-start | bytes 98312 | tf_op jit(solution)/shard_map/ppermute | solution.py:454
  60.2 2.8 %collective-permute-start.3 = (f32[64,128]{1,0:T(8,128)S(1)}, f32[64,128]{1,0:T(8,128)S(1)}, u32[]{:S(2)}, u32[]{:S(2)}) collective-permute-start(f32[64,128]{1,0:T(8,128)S(1)} %shard_map.107), channel_id=1, source_target_pairs={{0,1},{1,0},{2,3},{3,2},{4,5},{5,4},{6,7},{7,6},{8,9},{9,8},{10,11... | collective-permute-start | bytes 98312 | tf_op jit(solution)/shard_map/ppermute | solution.py:461

commit v8 on v7

--- a/solution.py
+++ b/solution.py
@@ -20,7 +20,7 @@
 XROWS = 320
 PLANES = 8
 PAIRS = 2
-GROUP = 16
+GROUP = 32
 CHUNKS = 16
 BLOCK = 128
 STEP = 72

time: 64.2 us -> 64.2 us (level)
  no operation moved by 1% of the time
where the time goes in v8:
time: 64.2 us; the launch traced here: 63.8 us
  blocking collectives  29.1 us (45%)
  starting transfers between devices  15.4 us (24%)
  Pallas kernels  15.2 us (24%)
  waiting for transfers between devices  2.46 us (4%)
  between operations  0.79 us (1%)
  other arithmetic  0.65 us (1%)
    all_to_all x1, blocking collectives, on_device(): lax.all_to_all(spread, ('sky', 'epoch'), split_axis=0, concat_axis=0, til...  29.1 us
    pallas_call x1, Pallas kernels, call_sky(): pl.pallas_call(sky_kernel, out_shape=(jax.ShapeDtypeStruct((TR, TW), F32)...  9.21 us
    all_to_all x1, starting transfers between devices, on_device(): got = lax.all_to_all(sent, 'sky', split_axis=0, concat_axis=0, tiled=True)  7.73 us
    ppermute x1, starting transfers between devices, on_device(): first = lax.ppermute(first, 'sky', [(i, i ^ 1) for i in range(n)])  3.86 us
    pallas_call x1, Pallas kernels, call_basis(): pl.pallas_call(basis_kernel, out_shape=(jax.ShapeDtypeStruct((CHUNKS, 192...  3.73 us
    ppermute x1, starting transfers between devices, on_device(): grad = part + lax.ppermute(part, 'epoch', swap)  1.98 us
    pallas_call x1, Pallas kernels, call_send(): pl.pallas_call(send_kernel, out_shape=jax.ShapeDtypeStruct((NSKY, 64, 128...  1.97 us
  transfers between devices with their start and end apart: 5, of which 3 were waited for; matrix products, arithmetic and copies ran while one was open for 0% of the time, Pallas kernels for 6%

profile of v8, /device:TPU:1, one launch (start us, length us, event | category | flops | bytes accessed | tf_op | source)
XLA Modules:
  0.0 63.8 jit_solution(3401243922883614318)
XLA Ops:
  0.6 0.0 copy-start.1
  0.6 0.0 copy-start.2
  0.7 2.0 %shard_map.105 = bf16[16,64,128]{2,1,0:T(8,128)(2,1)} custom-call(s32[16,16]{1,0:T(8,128)} %bitcast.21, s32[1,16]{1,0:T(1,128)} %count_s.3, bf16[64,128]{1,0:T(8,128)(2,1)} %bitcast.29, s32[16,16]{1,0:T(8,128)} %bitcast.24, s32[16,16]{1,0:T(8,128)} %bitcast.26), custom_call_target="tpu_custom_call" | custom-call | flops 8000000000 | bytes 16777216 | tf_op jit(solution)/shard_map/pallas_call | solution.py:362
  2.6 0.0 copy-start
  2.6 0.0 copy-start.3
  2.6 0.0 copy-start.4
  2.6 0.0 copy-start.5
  2.6 0.0 copy-start.6
  2.7 0.0 copy-start.7
  2.7 7.7 %all-to-all-start = ((bf16[16,64,128]{2,1,0:T(8,128)(2,1)}), bf16[16,64,128]{2,1,0:T(8,128)(2,1)S(1)}, u32[]{:S(2)}, u32[]{:S(2)}) async-start(bf16[16,64,128]{2,1,0:T(8,128)(2,1)} %shard_map.105), calls=%async_computation | async-start | bytes 524288 | tf_op jit(solution)/shard_map/all_to_all | solution.py:448
  10.4 0.0 copy-done.1
  10.4 0.0 copy-done.2
  10.5 0.7 %collective-permute-start.1 = (f32[64,512]{1,0:T(8,128)S(1)}, f32[64,512]{1,0:T(8,128)S(1)}, u32[]{:S(2)}, u32[]{:S(2)}) collective-permute-start(f32[64,512]{1,0:T(8,128)S(1)} %get-tuple-element.18), channel_id=1, source_target_pairs={{16,32},{32,16},{48,64},{64,48},{80,96},{96,80},{112,128},{128,112... | collective-permute-start | bytes 393224 | tf_op jit(solution)/shard_map/ppermute | solution.py:450
  11.2 3.9 %collective-permute-start = (f32[64,512]{1,0:T(8,128)S(1)}, f32[64,512]{1,0:T(8,128)S(1)}, u32[]{:S(2)}, u32[]{:S(2)}) collective-permute-start(f32[64,512]{1,0:T(8,128)S(1)} %get-tuple-element.19), channel_id=1, source_target_pairs={{0,16},{16,0},{32,48},{48,32},{64,80},{80,64},{96,112},{112,96},{1... | collective-permute-start | bytes 393224 | tf_op jit(solution)/shard_map/ppermute | solution.py:449
  15.0 0.0 copy-done
  15.0 0.0 copy-done.3
  15.0 0.0 copy-done.4
  15.0 3.7 %shard_map.104 = (bf16[16,192,256]{2,1,0:T(8,128)(2,1)}, f32[64,128]{1,0:T(8,128)S(1)}, f32[64,128]{1,0:T(8,128)S(1)}) custom-call(s32[16,16]{1,0:T(8,128)S(1)} %bitcast.22, f32[2,51]{1,0:T(2,128)S(1)} %bitcast.23, bf16[64,4096]{1,0:T(8,128)(2,1)S(1)} %copy-done), custom_call_target="tpu_custom_call" | custom-call | flops 100000 | bytes 1024 | tf_op jit(solution)/shard_map/pallas_call | solution.py:374
  18.8 0.0 collective-permute-done.1.second_ref
  18.8 0.7 %collective-permute-done.first_ref = f32[64,512]{1,0:T(8,128)S(1)} collective-permute-done((f32[64,512]{1,0:T(8,128)S(1)}, f32[64,512]{1,0:T(8,128)S(1)}, u32[]{:S(2)}, u32[]{:S(2)}) %collective-permute-start) | collective-permute-done | bytes 131104 | tf_op jit(solution)/shard_map/ppermute | solution.py:449
  19.5 0.0 all-to-all-done.got_ref
  19.5 0.0 copy-done.5
  19.5 0.0 copy-done.6
  19.5 0.0 copy-done.7
  19.5 9.2 %shard_map.106 = (f32[256,512]{1,0:T(8,128)}, f32[16,4,128]{2,1,0:T(4,128)S(1)}, f32[16,4,128]{2,1,0:T(4,128)S(1)}) custom-call(s32[16,16]{1,0:T(8,128)S(1)} %bitcast.25, s32[16,16]{1,0:T(8,128)S(1)} %bitcast.27, s32[1,16]{1,0:T(1,128)S(1)} %copy-done.7, bf16[16,192,256]{2,1,0:T(8,128)(2,1)} %get-tuple-element.10.b_hbm, ...), custom_call_target="tpu_custom_call" | custom-call | flops 4000000000 | bytes 4194304 | tf_op jit(solution)/shard_map/pallas_call | solution.py:396
  28.8 1.2 %collective-permute-start.2 = (f32[16,4,128]{2,1,0:T(4,128)S(1)}, f32[16,4,128]{2,1,0:T(4,128)S(1)}, u32[]{:S(2)}, u32[]{:S(2)}) collective-permute-start(f32[16,4,128]{2,1,0:T(4,128)S(1)} %get-tuple-element.12), channel_id=1, source_target_pairs={{0,1},{1,0},{2,3},{3,2},{4,5},{5,4},{6,7},{7,6},{8,9},{9,8},{10,11... | collective-permute-start | bytes 98312 | tf_op jit(solution)/shard_map/ppermute | solution.py:454
  30.0 0.9 %collective-permute-done.2 = f32[16,4,128]{2,1,0:T(4,128)S(1)} collective-permute-done((f32[16,4,128]{2,1,0:T(4,128)S(1)}, f32[16,4,128]{2,1,0:T(4,128)S(1)}, u32[]{:S(2)}, u32[]{:S(2)}) %collective-permute-start.2) | collective-permute-done | bytes 32800 | tf_op jit(solution)/shard_map/ppermute | solution.py:454
  30.9 29.1 %all_to_all.10.got_ref = f32[128,4,128]{2,1,0:T(4,128)S(1)} all-to-all(f32[128,4,128]{2,1,0:T(4,128)S(1)} %bitcast.28), channel_id=1, replica_groups={{0,2,4,6,8,10,12,14,16,18,20,22,24,26,28,30,32,34,36,38,40,42,44,46,48,..., dimensions={0} | all-to-all | bytes 524288 | tf_op jit(solution)/shard_map/all_to_all | solution.py:457
  60.0 0.3 shard_map.107
  60.4 2.0 %collective-permute-start.3 = (f32[64,128]{1,0:T(8,128)S(1)}, f32[64,128]{1,0:T(8,128)S(1)}, u32[]{:S(2)}, u32[]{:S(2)}) collective-permute-start(f32[64,128]{1,0:T(8,128)S(1)} %shard_map.107), channel_id=1, source_target_pairs={{0,1},{1,0},{2,3},{3,2},{4,5},{5,4},{6,7},{7,6},{8,9},{9,8},{10,11... | collective-permute-start | bytes 98312 | tf_op jit(solution)/shard_map/ppermute | solution.py:461
  62.3 0.9 %collective-permute-done.3 = f32[64,128]{1,0:T(8,128)S(1)} collective-permute-done((f32[64,128]{1,0:T(8,128)S(1)}, f32[64,128]{1,0:T(8,128)S(1)}, u32[]{:S(2)}, u32[]{:S(2)}) %collective-permute-start.3) | collective-permute-done | bytes 32800 | tf_op jit(solution)/shard_map/ppermute | solution.py:461
  63.2 0.6 add_bitcast_fusion
  (4 shorter events, 0.1 us)
Async XLA Ops:
  0.6 9.8 %copy-start.1 = (f32[1,256,512]{2,1,0:T(8,128)S(1)}, f32[1,256,512]{2,1,0:T(8,128)}, u32[]{:S(2)}) copy-start(f32[1,256,512]{2,1,0:T(8,128)} %param.16) | copy-start | bytes 1572868
  0.6 9.8 %copy-start.2 = (f32[1,256,512]{2,1,0:T(8,128)S(1)}, f32[1,256,512]{2,1,0:T(8,128)}, u32[]{:S(2)}) copy-start(f32[1,256,512]{2,1,0:T(8,128)} %param.17) | copy-start | bytes 1572868
  2.6 12.4 %copy-start = (bf16[64,4096]{1,0:T(8,128)(2,1)S(1)}, bf16[64,4096]{1,0:T(8,128)(2,1)}, u32[]{:S(2)}) copy-start(bf16[64,4096]{1,0:T(8,128)(2,1)} %basis_ref.1) | copy-start | bytes 1572868
  2.6 12.4 %copy-start.3 = (s32[1,16,16]{2,1,0:T(8,128)S(1)}, s32[1,16,16]{2,1,0:T(8,128)}, u32[]{:S(2)}) copy-start(s32[1,16,16]{2,1,0:T(8,128)} %param.12) | copy-start | bytes 3076
  2.6 12.4 %copy-start.4 = (f32[1,2,51]{2,1,0:T(2,128)S(1)}, f32[1,2,51]{2,1,0:T(2,128)}, u32[]{:S(2)}) copy-start(f32[1,2,51]{2,1,0:T(2,128)} %param.11) | copy-start | bytes 1228
  2.6 16.9 %copy-start.5 = (s32[1,16,16]{2,1,0:T(8,128)S(1)}, s32[1,16,16]{2,1,0:T(8,128)}, u32[]{:S(2)}) copy-start(s32[1,16,16]{2,1,0:T(8,128)} %param.14) | copy-start | bytes 3076
  2.6 16.9 %copy-start.6 = (s32[1,16,16]{2,1,0:T(8,128)S(1)}, s32[1,16,16]{2,1,0:T(8,128)}, u32[]{:S(2)}) copy-start(s32[1,16,16]{2,1,0:T(8,128)} %param.15) | copy-start | bytes 3076
  2.7 16.9 %copy-start.7 = (s32[1,16]{1,0:T(1,128)S(1)}, s32[1,16]{1,0:T(1,128)}, u32[]{:S(2)}) copy-start(s32[1,16]{1,0:T(1,128)} %count_s.3) | copy-start | bytes 196
  2.7 16.9 %all-to-all-start = ((bf16[16,64,128]{2,1,0:T(8,128)(2,1)}), bf16[16,64,128]{2,1,0:T(8,128)(2,1)S(1)}, u32[]{:S(2)}, u32[]{:S(2)}) async-start(bf16[16,64,128]{2,1,0:T(8,128)(2,1)} %shard_map.105), calls=%async_computation | async-start | bytes 524288 | tf_op jit(solution)/shard_map/all_to_all | solution.py:448
  10.5 8.3 %collective-permute-start.1 = (f32[64,512]{1,0:T(8,128)S(1)}, f32[64,512]{1,0:T(8,128)S(1)}, u32[]{:S(2)}, u32[]{:S(2)}) collective-permute-start(f32[64,512]{1,0:T(8,128)S(1)} %get-tuple-element.18), channel_id=1, source_target_pairs={{16,32},{32,16},{48,64},{64,48},{80,96},{96,80},{112,128},{128,112... | collective-permute-start | bytes 393224 | tf_op jit(solution)/shard_map/ppermute | solution.py:450
  11.2 8.4 %collective-permute-start = (f32[64,512]{1,0:T(8,128)S(1)}, f32[64,512]{1,0:T(8,128)S(1)}, u32[]{:S(2)}, u32[]{:S(2)}) collective-permute-start(f32[64,512]{1,0:T(8,128)S(1)} %get-tuple-element.19), channel_id=1, source_target_pairs={{0,16},{16,0},{32,48},{48,32},{64,80},{80,64},{96,112},{112,96},{1... | collective-permute-start | bytes 393224 | tf_op jit(solution)/shard_map/ppermute | solution.py:449
  28.8 2.1 %collective-permute-start.2 = (f32[16,4,128]{2,1,0:T(4,128)S(1)}, f32[16,4,128]{2,1,0:T(4,128)S(1)}, u32[]{:S(2)}, u32[]{:S(2)}) collective-permute-start(f32[16,4,128]{2,1,0:T(4,128)S(1)} %get-tuple-element.12), channel_id=1, source_target_pairs={{0,1},{1,0},{2,3},{3,2},{4,5},{5,4},{6,7},{7,6},{8,9},{9,8},{10,11... | collective-permute-start | bytes 98312 | tf_op jit(solution)/shard_map/ppermute | solution.py:454
  60.4 2.8 %collective-permute-start.3 = (f32[64,128]{1,0:T(8,128)S(1)}, f32[64,128]{1,0:T(8,128)S(1)}, u32[]{:S(2)}, u32[]{:S(2)}) collective-permute-start(f32[64,128]{1,0:T(8,128)S(1)} %shard_map.107), channel_id=1, source_target_pairs={{0,1},{1,0},{2,3},{3,2},{4,5},{5,4},{6,7},{7,6},{8,9},{9,8},{10,11... | collective-permute-start | bytes 98312 | tf_op jit(solution)/shard_map/ppermute | solution.py:461
